TPU v7x, 512 devices: a whole 4x4x16 slice. The times are simulated.
512 devices in a mesh: dp: 8 (over x, core), fsdp: 64 (over z, y).
Axes of the slice: x: 4, y: 4, z: 16, core: 2. Of those that a mesh axis runs over, the one named last changes fastest.
Arguments:
- grad_parts: bfloat16 [8, 4096, 16384], P('dp', 'fsdp'), may hold values from -6 to 6
- slot_table: int32 [8, 32], P('dp'), may hold values from 0 to 31, each once within a row
- left_stat: bfloat16 [8, 32, 512, 512], P('dp', None, 'fsdp'), may hold values from -6 to 6
- right_stat: bfloat16 [8, 32, 512, 512], P('dp', None, 'fsdp'), may hold values from -6 to 6
- left_root: bfloat16 [8, 32, 512, 512], P('dp', None, 'fsdp'), may hold values from -0.25 to 0.25
- right_root: bfloat16 [8, 32, 512, 512], P('dp', None, 'fsdp'), may hold values from -0.25 to 0.25
Outputs:
- left_new: bfloat16 [8, 32, 512, 512], P('dp', None, 'fsdp')
- right_new: bfloat16 [8, 32, 512, 512], P('dp', None, 'fsdp')
- update: bfloat16 [4096, 16384], P('fsdp', 'dp')
Inputs may be any that keep to these rules, and one draw needn't show every extreme that they name: Each row of slot_table is a permutation: slot_table[d, k] is where block k of band d keeps its factors.
All inputs are finite; a program needn't handle non-finite values.
Results may differ from a plain program's by a relative error of at most 0.022.
Values may be sent and summed in bfloat16 or wider, within the bound.
No kernel may reach another device: no remote copies, remote signals or barrier semaphores. Data moves between devices by JAX's collectives and lax.ppermute only.
A program may use at most 64 MiB of HBM per device.

v0:
```python
import jax
import jax.numpy as jnp
from jax import lax
from jax.sharding import PartitionSpec as P

decay = 0.9


def spread_rows(stacked, senders, piece):
    count, width, block, last = (
        stacked.shape[0],
        stacked.shape[1],
        stacked.shape[2],
        stacked.shape[3],
    )
    return stacked.reshape(count, width, senders, piece, last).transpose(2, 0, 1, 3, 4)


def send_all(stacked, senders, piece):
    return lax.all_to_all(
        spread_rows(stacked, senders, piece), "fsdp", split_axis=0, concat_axis=0, tiled=True
    )


def settle(new_left, new_right, make_update, senders, piece):
    result = make_update()
    return send_all(jnp.stack([new_left, new_right, result], 1), senders, piece)


def local(grad_parts, slot_table, left_stat, right_stat, left_root, right_root):
    senders = lax.axis_size("fsdp")
    groups = lax.axis_size("dp")
    nblocks, piece, block = (left_stat.shape[1], left_stat.shape[2], left_stat.shape[3])
    rows_dev = grad_parts.shape[1]
    band_cols = grad_parts.shape[2] // groups
    nrows_blk = rows_dev // piece
    ncols_blk = band_cols // block
    summed = lax.psum_scatter(grad_parts, "dp", scatter_dimension=2, tiled=True).astype(jnp.float32)
    total = summed[0].astype(jnp.bfloat16).reshape(nrows_blk, piece, ncols_blk, block)
    total = total.transpose(0, 2, 1, 3).reshape(nblocks, piece, block)
    table = slot_table[0]
    spread = (nblocks + senders - 1) // senders
    slots = senders * spread
    placed = jnp.zeros((slots, piece, block), jnp.bfloat16).at[table].set(total)
    padding = ((0, slots - nblocks), (0, 0), (0, 0))
    payload = jnp.stack(
        [
            placed,
            jnp.pad(left_stat[0], padding),
            jnp.pad(right_stat[0], padding),
            jnp.pad(left_root[0], padding),
            jnp.pad(right_root[0], padding),
        ],
        1,
    )
    payload = payload.reshape(senders, spread, 5, piece, block)
    arrived = lax.all_to_all(payload, "fsdp", split_axis=0, concat_axis=0, tiled=True)
    count = arrived.shape[1]
    full = arrived.transpose(1, 2, 0, 3, 4).reshape(count, 5, senders * piece, block)
    grads = full[:, 0]
    left_gram = jnp.einsum("mij,mkj->mik", grads, grads, preferred_element_type=jnp.float32)
    right_gram = jnp.einsum("mji,mjk->mik", grads, grads, preferred_element_type=jnp.float32)
    new_left = (decay * full[:, 1].astype(jnp.float32) + (1.0 - decay) / block * left_gram).astype(
        jnp.bfloat16
    )
    new_right = (
        decay * full[:, 2].astype(jnp.float32) + (1.0 - decay) / block * right_gram
    ).astype(jnp.bfloat16)

    def make_update():
        half = jnp.einsum(
            "mij,mjk->mik", full[:, 3], grads, preferred_element_type=jnp.float32
        ).astype(jnp.bfloat16)
        return jnp.einsum(
            "mij,mjk->mik", half, full[:, 4], preferred_element_type=jnp.float32
        ).astype(jnp.bfloat16)

    back = settle(new_left, new_right, make_update, senders, piece)
    flat = back.reshape(slots, 3, piece, block)[:nblocks]
    left_new = flat[:, 0][None]
    right_new = flat[:, 1][None]
    blocks_home = jnp.take(flat[:, 2], table, axis=0)
    blocks_home = blocks_home.reshape(nrows_blk, ncols_blk, piece, block).transpose(0, 2, 1, 3)
    return (left_new, right_new, blocks_home.reshape(rows_dev, band_cols))


def solution(mesh):
    return jax.shard_map(
        local,
        mesh=mesh,
        in_specs=(
            P("dp", "fsdp", None),
            P("dp", None),
            P("dp", None, "fsdp", None),
            P("dp", None, "fsdp", None),
            P("dp", None, "fsdp", None),
            P("dp", None, "fsdp", None),
        ),
        out_specs=(P("dp", None, "fsdp", None), P("dp", None, "fsdp", None), P("fsdp", "dp")),
        check_vma=False,
    )
```

profile of v0, /device:TPU:6, one launch (start us, length us, event | category | flops | bytes accessed | tf_op | source)
XLA Modules:
  0.0 292.0 jit_solution(17418563814347391124)
XLA Ops:
  7.2 0.0 copy-start
  7.2 0.0 copy-start.1
  7.2 0.0 reduce-scatter.2.cloned.1.call-start
  7.2 0.7 reduce-scatter.2.cloned.1.call-update
  7.9 0.7 fusion.8
  8.6 44.7 %reduce-scatter.2.cloned.1.call-done = bf16[1,64,2048]{2,1,0:T(8,128)(2,1)} async-done(((bf16[1,64,16384]{2,1,0:T(8,128)(2,1)}), bf16[1,64,2048]{2,1,0:T(8,128)(2,1)}) %reduce-scatter.2.cloned.1.call-update) | async-done | bytes 262160 | tf_op jit(solution)/shard_map/reduce_scatter | solution.py:38
  53.4 2.8 scatter_fusion
  56.4 0.0 copy-done.3
  56.5 138.8 %all_to_all.10 = bf16[64,1,5,8,512]{4,3,2,1,0:T(8,128)(2,1)S(1)} all-to-all(bf16[64,1,5,8,512]{4,3,2,1,0:T(8,128)(2,1)S(1)} %bitcast.75), channel_id=1, replica_groups=mesh['dp'=8,'fsdp'=64] {'fsdp'}, dimensions={0} | all-to-all | bytes 5242880 | tf_op jit(solution)/shard_map/all_to_all | solution.py:57
  195.3 0.2 copy_bitcast_fusion
  195.5 0.7 fusion.4
  196.2 0.5 fusion.5
  196.7 0.5 fusion.6
  197.2 0.0 copy-start.4
  197.2 1.4 maximum_bitcast_fusion
  198.6 6.1 %all-to-all-start.1 = ((bf16[64,1,3,8,512]{4,3,2,1,0:T(8,128)(2,1)}), bf16[64,1,3,8,512]{4,3,2,1,0:T(8,128)(2,1)S(1)}, u32[]{:S(2)}, u32[]{:S(2)}) async-start(bf16[64,1,3,8,512]{4,3,2,1,0:T(8,128)(2,1)} %maximum_bitcast_fusion), calls=%async_computation.2 | async-start | bytes 3145728 | tf_op jit(solution)/shard_map/all_to_all | solution.py:20
  204.7 0.5 broadcast.75
  205.2 0.7 reduce.3
  205.9 0.1 squeeze.31
  206.0 76.9 %all-to-all-done.1 = bf16[64,1,3,8,512]{4,3,2,1,0:T(8,128)(2,1)S(1)} async-done(((bf16[64,1,3,8,512]{4,3,2,1,0:T(8,128)(2,1)}), bf16[64,1,3,8,512]{4,3,2,1,0:T(8,128)(2,1)S(1)}, u32[]{:S(2)}, u32[]{:S(2)}) %all-to-all-start.1) | async-done | bytes 1572896 | tf_op jit(solution)/shard_map/all_to_all | solution.py:20
  282.9 0.1 slice_bitcast_fusion
  282.9 0.9 slice_bitcast_fusion.11
  283.8 0.6 gather_fusion
  284.4 0.8 broadcast_select_fusion
  (14 shorter events, 0.2 us)
Async XLA Ops:
  7.2 49.1 %copy-start = (bf16[1,32,8,512]{3,2,1,0:T(8,128)(2,1)S(1)}, bf16[1,32,8,512]{3,2,1,0:T(8,128)(2,1)}, u32[]{:S(2)}) copy-start(bf16[1,32,8,512]{3,2,1,0:T(8,128)(2,1)} %param.8) | copy-start | bytes 786436
  7.2 49.1 %copy-start.1 = (bf16[1,32,8,512]{3,2,1,0:T(8,128)(2,1)S(1)}, bf16[1,32,8,512]{3,2,1,0:T(8,128)(2,1)}, u32[]{:S(2)}) copy-start(bf16[1,32,8,512]{3,2,1,0:T(8,128)(2,1)} %param.9) | copy-start | bytes 786436
  7.2 49.2 %copy-start.2 = (bf16[1,32,8,512]{3,2,1,0:T(8,128)(2,1)S(1)}, bf16[1,32,8,512]{3,2,1,0:T(8,128)(2,1)}, u32[]{:S(2)}) copy-start(bf16[1,32,8,512]{3,2,1,0:T(8,128)(2,1)} %param.10) | copy-start | bytes 786436
  7.2 46.1 %reduce-scatter.2.cloned.1.call-start = ((), (), s32[]{:S(2)}) async-start(), calls=%async_computation.3 | async-start | bytes 2359296 | tf_op jit(solution)/shard_map/reduce_scatter | solution.py:38
  7.9 48.5 %copy-start.3 = (bf16[1,32,8,512]{3,2,1,0:T(8,128)(2,1)S(1)}, bf16[1,32,8,512]{3,2,1,0:T(8,128)(2,1)}, u32[]{:S(2)}) copy-start(bf16[1,32,8,512]{3,2,1,0:T(8,128)(2,1)} %param.11) | copy-start | bytes 786436
  197.2 8.0 %copy-start.4 = (s32[1,32]{1,0:T(1,128)S(1)}, s32[1,32]{1,0:T(1,128)}, u32[]{:S(2)}) copy-start(s32[1,32]{1,0:T(1,128)} %param.7) | copy-start | bytes 388
  198.6 84.3 %all-to-all-start.1 = ((bf16[64,1,3,8,512]{4,3,2,1,0:T(8,128)(2,1)}), bf16[64,1,3,8,512]{4,3,2,1,0:T(8,128)(2,1)S(1)}, u32[]{:S(2)}, u32[]{:S(2)}) async-start(bf16[64,1,3,8,512]{4,3,2,1,0:T(8,128)(2,1)} %maximum_bitcast_fusion), calls=%async_computation.2 | async-start | bytes 3145728 | tf_op jit(solution)/shard_map/all_to_all | solution.py:20
Sparse Core Ops, SparseCore 0:
  10.9 42.3 reduce-scatter.1
where the time goes:
time: 292 us
  blocking collectives  139 us (48%)
  waiting for transfers between devices  122 us (42%)
  between operations  14.2 us (5%)
  starting transfers between devices  6.16 us (2%)
  local copies, waits for them, and re-layouts  5.36 us (2%)
  other arithmetic  3.56 us (1%)
    all_to_all x1, blocking collectives, local(): lax.all_to_all(payload, 'fsdp', split_axis=0, concat_axis=0, tiled=True)  139 us
    all_to_all x1, waiting for transfers between devices, send_all(): lax.all_to_all(spread_rows(stacked, senders, piece), 'fsdp', split_axis=0...  76.9 us
    reduce_scatter x1, waiting for transfers between devices, local(): lax.psum_scatter(grad_parts, 'dp', scatter_dimension=2, tiled=True)  44.7 us
    all_to_all x1, starting transfers between devices, send_all(): lax.all_to_all(spread_rows(stacked, senders, piece), 'fsdp', split_axis=0...  6.13 us
  transfers between devices with their start and end apart: 2, of which 2 were waited for; matrix products, arithmetic and copies ran while one was open for 1% of the time, Pallas kernels for 0%

commit v1 on v0

v1 whole, which is shorter than its diff:
```python
import jax
import jax.numpy as jnp
from jax import lax
from jax.sharding import Mesh, PartitionSpec as P

decay = 0.9
bf16 = jnp.bfloat16
f32 = jnp.float32


def shift(value, axis, by):
    n = lax.axis_size(axis)
    return lax.ppermute(value, axis, [(i, (i + by) % n) for i in range(n)])


def gather_y(value):
    n = lax.axis_size("y")
    me = lax.axis_index("y")
    parts = [value] + [shift(value, "y", by) for by in range(1, n)]
    return jnp.stack([
        lax.select_n((me - owner) % n, *parts) for owner in range(n)
    ])


def sum_dp(grad):
    nx = lax.axis_size("x")
    core = lax.axis_index("core")
    x = lax.axis_index("x")
    rows = grad.shape[0]
    parts = grad.reshape(rows, nx, 2, -1)
    mine = lax.dynamic_index_in_dim(parts, core, 2, keepdims=False)
    other = lax.dynamic_index_in_dim(parts, 1 - core, 2, keepdims=False)
    got = lax.ppermute(other, "core", [(0, 1), (1, 0)])
    pair = (mine.astype(f32) + got.astype(f32)).astype(bf16)
    total = lax.dynamic_index_in_dim(pair, x, 1, keepdims=False).astype(f32)
    for by in range(1, nx):
        piece = lax.dynamic_index_in_dim(pair, (x + by) % nx, 1, keepdims=False)
        total = total + shift(piece, "x", by).astype(f32)
    return total.astype(bf16)


def local(grad_parts, slot_table, left_stat, right_stat, left_root, right_root):
    nz, ny = lax.axis_size("z"), lax.axis_size("y")
    y = lax.axis_index("y")
    nblocks, piece, block = left_stat.shape[1:]
    rows_dev = grad_parts.shape[1]
    nrb = rows_dev // piece
    ncb = nblocks // nrb
    per = nblocks // nz
    table = slot_table[0]

    roots = jnp.stack(
        [left_root[0].reshape(nz, per, piece, block), right_root[0].reshape(nz, per, piece, block)], 1
    )
    roots = lax.all_to_all(roots, "z", 0, 0, tiled=True)

    total = sum_dp(grad_parts[0])
    total = total.reshape(nrb, piece, ncb, block).transpose(0, 2, 1, 3).reshape(nblocks, piece, block)
    placed = jnp.zeros_like(total).at[table].set(total)
    grads = lax.all_to_all(placed.reshape(nz, per, piece, block), "z", 0, 0, tiled=True)

    def whole(parts):
        return gather_y(parts).transpose(2, 1, 0, 3, 4).reshape(per, block, block)

    def rows_of_y(value):
        picked = lax.dynamic_index_in_dim(value.reshape(per, nz, ny, piece, block), y, 2, keepdims=False)
        return picked.transpose(1, 0, 2, 3)

    right_full = whole(roots[:, 1])
    left_rows = roots[:, 0].transpose(1, 0, 2, 3).reshape(per, nz * piece, block)
    full = whole(grads)
    scale = (1.0 - decay) / block
    left_gram = (scale * jnp.einsum("mij,mkj->mik", full, full, preferred_element_type=f32)).astype(bf16)
    right_gram = (scale * jnp.einsum("mji,mjk->mik", full, full, preferred_element_type=f32)).astype(bf16)
    half = jnp.einsum("mij,mjk->mik", left_rows, full, preferred_element_type=f32).astype(bf16)
    result = jnp.einsum("mij,mjk->mik", half, right_full, preferred_element_type=f32).astype(bf16)
    result = result.reshape(per, nz, piece, block).transpose(1, 0, 2, 3)
    back = jnp.stack([rows_of_y(left_gram), rows_of_y(right_gram), result], 1)
    back = lax.all_to_all(back, "z", 0, 0, tiled=True)

    def settle(stat, gram):
        return (decay * stat.astype(f32) + gram.reshape(stat.shape).astype(f32)).astype(bf16)

    left_new = settle(left_stat, back[:, 0])
    right_new = settle(right_stat, back[:, 1])
    home = jnp.take(back[:, 2].reshape(nblocks, piece, block), table, axis=0)
    home = home.reshape(nrb, ncb, piece, block).transpose(0, 2, 1, 3)
    return left_new, right_new, home.reshape(rows_dev, ncb * block)


def solution(mesh):
    ny = 4
    devices = mesh.devices
    split = Mesh(
        devices.reshape(devices.shape[0] // 2, 2, devices.shape[1] // ny, ny), ("x", "core", "z", "y")
    )
    dp, fsdp = ("x", "core"), ("z", "y")
    factor = P(dp, None, fsdp, None)
    return jax.shard_map(
        local,
        mesh=split,
        in_specs=(P(dp, fsdp, None), P(dp, None), factor, factor, factor, factor),
        out_specs=(factor, factor, P(fsdp, dp)),
        check_vma=False,
    )
```

time: 292 us -> 164 us (0.56)
  the two profiles are of different devices: /device:TPU:6 before, /device:TPU:42 now
where the time goes in v1:
time: 164 us; the launch traced here: 163 us
  starting transfers between devices  67.9 us (41%)
  waiting for transfers between devices  63.8 us (39%)
  other arithmetic  15.8 us (10%)
  local copies, waits for them, and re-layouts  12.9 us (8%)
  matrix products  1.98 us (1%)
    all_to_all x1, waiting for transfers between devices, local(): back = lax.all_to_all(back, 'z', 0, 0, tiled=True)  38.4 us
    ppermute x9, starting transfers between devices, shift(): return lax.ppermute(value, axis, [(i, (i + by) % n) for i in range(n)])  32 us
    ppermute x9, waiting for transfers between devices, shift(): return lax.ppermute(value, axis, [(i, (i + by) % n) for i in range(n)])  17.9 us
    all_to_all x1, starting transfers between devices, local(): roots = lax.all_to_all(roots, 'z', 0, 0, tiled=True)  15.2 us
    all_to_all x1, starting transfers between devices, local(): lax.all_to_all(placed.reshape(nz, per, piece, block), 'z', 0, 0, tiled=True)  12 us
    all_to_all x1, waiting for transfers between devices, local(): lax.all_to_all(placed.reshape(nz, per, piece, block), 'z', 0, 0, tiled=True)  7.47 us
    all_to_all x1, starting transfers between devices, local(): back = lax.all_to_all(back, 'z', 0, 0, tiled=True)  6.8 us
    dynamic_slice x1, other arithmetic, sum_dp(): other = lax.dynamic_index_in_dim(parts, 1 - core, 2, keepdims=False)  5.6 us
  transfers between devices with their start and end apart: 13, of which 6 were waited for; matrix products, arithmetic and copies ran while one was open for 8% of the time, Pallas kernels for 0%

profile of v1, /device:TPU:42, one launch (start us, length us, event | category | flops | bytes accessed | tf_op | source)
XLA Modules:
  0.0 163.4 jit_solution(3516978514238300291)
XLA Ops:
  0.6 3.3 %reshape_squeeze.8 = bf16[64,4,2,2048]{3,2,1,0:T(2,128)(2,1)S(1)} reshape(bf16[1,64,16384]{2,1,0:T(8,128)(2,1)} %param.6) | data formatting | bytes 4194304 | tf_op jit(solution)/shard_map/reshape;squeeze | solution.py:30
  3.9 5.6 %constant_dynamic-slice_fusion.5 = (bf16[64,4,1,2048]{3,2,1,0:T(2,128)(2,1)S(1)}, f32[64,4,1,2048]{3,2,1,0:T(1,128)}) fusion(bf16[64,4,2,2048]{3,2,1,0:T(2,128)(2,1)S(1)} %reshape_squeeze.8, s32[]{:T(128)S(6)} %select_n.262, s32[]{:T(128)S(6)} %select_n.261), kind=kLoop, calls=%fused_computation.50 | loop fusion | flops 524288 | bytes 5242888 | tf_op jit(solution)/shard_map/jit(dynamic_index_in_dim)/dynamic_slice | solution.py:32
  12.5 1.9 %collective-permute-start = (bf16[64,4,2048]{2,1,0:T(4,128)(2,1)}, bf16[64,4,2048]{2,1,0:T(4,128)(2,1)}, u32[]{:S(2)}, u32[]{:S(2)}) collective-permute-start(bf16[64,4,2048]{2,1,0:T(4,128)(2,1)} %copy.34), channel_id=1, source_target_pairs={{0,64},{64,0},{1,65},{65,1},{2,66},{66,2},{3,67},{67,3},{4,68},{68... | collective-permute-start | bytes 3145736 | tf_op jit(solution)/shard_map/ppermute | solution.py:33
  15.2 15.2 %all-to-all-start.1 = ((bf16[16,2,2,8,512]{4,3,2,1,0:T(8,128)(2,1)}), bf16[16,2,2,8,512]{4,3,2,1,0:T(8,128)(2,1)S(1)}, u32[]{:S(2)}, u32[]{:S(2)}) async-start(bf16[16,2,2,8,512]{4,3,2,1,0:T(8,128)(2,1)} %pad_maximum_fusion.1), calls=%async_computation.1 | async-start | bytes 1048576 | tf_op jit(solution)/shard_map/all_to_all | solution.py:55
  30.5 2.4 %fusion = bf16[64,4,2048]{2,1,0:T(4,128)(2,1)S(1)} fusion(f32[64,4,1,2048]{3,2,1,0:T(1,128)S(1)} %copy-done, bf16[64,4,2048]{2,1,0:T(4,128)(2,1)} %collective-permute-done), kind=kLoop, calls=%fused_computation.3 | loop fusion | flops 1572864 | bytes 4194304 | tf_op jit(solution)/shard_map/convert_element_type | solution.py:34
  32.8 2.2 %constant_dynamic-slice_fusion.4 = (bf16[64,1,2048]{2,1,0:T(2,128)(2,1)S(1)}, bf16[64,1,2048]{2,1,0:T(2,128)(2,1)S(1)}, bf16[64,1,2048]{2,1,0:T(2,128)(2,1)S(1)}, f32[64,1,2048]{2,1,0:T(1,128)S(1)}) fusion(bf16[64,4,2048]{2,1,0:T(4,128)(2,1)S(1)} %fusion, s32[]{:T(128)S(6)} %select_n.265, s32[]{:T(128)S(6)} %select_n.269, s32[]{:T(128)S(6)} %select_n.267, ...), kind=kLoop, calls=%fused_computation.49 | loop fusion | flops 131072 | bytes 2359312 | tf_op jit(solution)/shard_map/jit(dynamic_index_in_dim)/dynamic_slice | solution.py:37
  35.2 3.4 %collective-permute-start.1 = (bf16[64,2048]{1,0:T(8,128)(2,1)S(1)}, bf16[64,2048]{1,0:T(8,128)(2,1)S(1)}, u32[]{:S(2)}, u32[]{:S(2)}) collective-permute-start(bf16[64,2048]{1,0:T(8,128)(2,1)S(1)} %bitcast.131), channel_id=1, source_target_pairs={{0,128},{128,256},{256,384},{384,0},{1,129},{129,257},{257,385},{3... | collective-permute-start | bytes 786440 | tf_op jit(solution)/shard_map/ppermute | solution.py:13
  38.7 3.0 %collective-permute-start.2 = (bf16[64,2048]{1,0:T(8,128)(2,1)S(1)}, bf16[64,2048]{1,0:T(8,128)(2,1)S(1)}, u32[]{:S(2)}, u32[]{:S(2)}) collective-permute-start(bf16[64,2048]{1,0:T(8,128)(2,1)S(1)} %bitcast.132), channel_id=1, source_target_pairs={{0,256},{128,384},{256,0},{384,128},{1,257},{129,385},{257,1},{385... | collective-permute-start | bytes 786440 | tf_op jit(solution)/shard_map/ppermute | solution.py:13
  41.9 4.2 %collective-permute-start.3 = (bf16[64,2048]{1,0:T(8,128)(2,1)S(1)}, bf16[64,2048]{1,0:T(8,128)(2,1)S(1)}, u32[]{:S(2)}, u32[]{:S(2)}) collective-permute-start(bf16[64,2048]{1,0:T(8,128)(2,1)S(1)} %bitcast.133), channel_id=1, source_target_pairs={{0,384},{128,0},{256,128},{384,256},{1,385},{129,1},{257,129},{385... | collective-permute-start | bytes 786440 | tf_op jit(solution)/shard_map/ppermute | solution.py:13
  46.3 5.2 %collective-permute-done.2 = bf16[64,2048]{1,0:T(8,128)(2,1)S(1)} collective-permute-done((bf16[64,2048]{1,0:T(8,128)(2,1)S(1)}, bf16[64,2048]{1,0:T(8,128)(2,1)S(1)}, u32[]{:S(2)}, u32[]{:S(2)}) %collective-permute-start.2) | collective-permute-done | bytes 262176 | tf_op jit(solution)/shard_map/ppermute | solution.py:13
  51.4 4.2 %collective-permute-done.3 = bf16[64,2048]{1,0:T(8,128)(2,1)S(1)} collective-permute-done((bf16[64,2048]{1,0:T(8,128)(2,1)S(1)}, bf16[64,2048]{1,0:T(8,128)(2,1)S(1)}, u32[]{:S(2)}, u32[]{:S(2)}) %collective-permute-start.3) | collective-permute-done | bytes 262176 | tf_op jit(solution)/shard_map/ppermute | solution.py:13
  56.6 3.9 %scatter_fusion = bf16[32,8,512]{2,1,0:T(8,128)(2,1)} fusion(bf16[32,8,512]{2,1,0:T(8,128)(2,1)} %broadcast_in_dim.14, s32[32]{0:T(128)S(1)} %fusion.7, bf16[32,8,512]{2,1,0:T(8,128)(2,1)S(1)} %bitcast.130), kind=kCustom, calls=%fused_computation.1 | custom fusion | bytes 786560 | tf_op jit(solution)/shard_map/scatter | solution.py:59
  60.5 12.0 %all-to-all-start = ((bf16[16,2,8,512]{3,2,1,0:T(8,128)(2,1)}), bf16[16,2,8,512]{3,2,1,0:T(8,128)(2,1)S(1)}, u32[]{:S(2)}, u32[]{:S(2)}) async-start(bf16[16,2,8,512]{3,2,1,0:T(8,128)(2,1)} %bitcast.6), calls=%async_computation | async-start | bytes 524288 | tf_op jit(solution)/shard_map/all_to_all | solution.py:60
  72.5 3.5 %collective-permute-start.7 = (bf16[16,2,8,512]{3,2,1,0:T(8,128)(2,1)S(1)}, bf16[16,2,8,512]{3,2,1,0:T(8,128)(2,1)S(1)}, u32[]{:S(2)}, u32[]{:S(2)}) collective-permute-start(bf16[16,2,8,512]{3,2,1,0:T(8,128)(2,1)S(1)} %get-tuple-element.21), channel_id=1, source_target_pairs={{0,1},{1,2},{2,3},{3,0},{4,5},{5,6},{6,7},{7,4},{8,9},{9,10},{10,1... | collective-permute-start | bytes 786440 | tf_op jit(solution)/shard_map/ppermute | solution.py:13
  76.0 2.8 %collective-permute-start.8 = (bf16[16,2,8,512]{3,2,1,0:T(8,128)(2,1)S(1)}, bf16[16,2,8,512]{3,2,1,0:T(8,128)(2,1)S(1)}, u32[]{:S(2)}, u32[]{:S(2)}) collective-permute-start(bf16[16,2,8,512]{3,2,1,0:T(8,128)(2,1)S(1)} %get-tuple-element.21), channel_id=1, source_target_pairs={{0,2},{1,3},{2,0},{3,1},{4,6},{5,7},{6,4},{7,5},{8,10},{9,11},{10,... | collective-permute-start | bytes 786440 | tf_op jit(solution)/shard_map/ppermute | solution.py:13
  78.9 4.3 %collective-permute-start.9 = (bf16[16,2,8,512]{3,2,1,0:T(8,128)(2,1)S(1)}, bf16[16,2,8,512]{3,2,1,0:T(8,128)(2,1)S(1)}, u32[]{:S(2)}, u32[]{:S(2)}) collective-permute-start(bf16[16,2,8,512]{3,2,1,0:T(8,128)(2,1)S(1)} %get-tuple-element.21), channel_id=1, source_target_pairs={{0,3},{1,0},{2,1},{3,2},{4,7},{5,4},{6,5},{7,6},{8,11},{9,8},{10,9... | collective-permute-start | bytes 786440 | tf_op jit(solution)/shard_map/ppermute | solution.py:13
  83.3 7.5 %all-to-all-done = bf16[16,2,8,512]{3,2,1,0:T(8,128)(2,1)S(1)} async-done(((bf16[16,2,8,512]{3,2,1,0:T(8,128)(2,1)}), bf16[16,2,8,512]{3,2,1,0:T(8,128)(2,1)S(1)}, u32[]{:S(2)}, u32[]{:S(2)}) %all-to-all-start) | async-done | bytes 262176 | tf_op jit(solution)/shard_map/all_to_all | solution.py:60
  90.8 3.5 %collective-permute-start.4 = (bf16[16,2,8,512]{3,2,1,0:T(8,128)(2,1)S(1)}, bf16[16,2,8,512]{3,2,1,0:T(8,128)(2,1)S(1)}, u32[]{:S(2)}, u32[]{:S(2)}) collective-permute-start(bf16[16,2,8,512]{3,2,1,0:T(8,128)(2,1)S(1)} %all-to-all-done), channel_id=1, source_target_pairs={{0,1},{1,2},{2,3},{3,0},{4,5},{5,6},{6,7},{7,4},{8,9},{9,10},{10,1... | collective-permute-start | bytes 786440 | tf_op jit(solution)/shard_map/ppermute | solution.py:13
  94.2 2.8 %collective-permute-start.5 = (bf16[16,2,8,512]{3,2,1,0:T(8,128)(2,1)S(1)}, bf16[16,2,8,512]{3,2,1,0:T(8,128)(2,1)S(1)}, u32[]{:S(2)}, u32[]{:S(2)}) collective-permute-start(bf16[16,2,8,512]{3,2,1,0:T(8,128)(2,1)S(1)} %all-to-all-done), channel_id=1, source_target_pairs={{0,2},{1,3},{2,0},{3,1},{4,6},{5,7},{6,4},{7,5},{8,10},{9,11},{10,... | collective-permute-start | bytes 786440 | tf_op jit(solution)/shard_map/ppermute | solution.py:13
  97.1 4.3 %collective-permute-start.6 = (bf16[16,2,8,512]{3,2,1,0:T(8,128)(2,1)S(1)}, bf16[16,2,8,512]{3,2,1,0:T(8,128)(2,1)S(1)}, u32[]{:S(2)}, u32[]{:S(2)}) collective-permute-start(bf16[16,2,8,512]{3,2,1,0:T(8,128)(2,1)S(1)} %all-to-all-done), channel_id=1, source_target_pairs={{0,3},{1,0},{2,1},{3,2},{4,7},{5,4},{6,5},{7,6},{8,11},{9,8},{10,9... | collective-permute-start | bytes 786440 | tf_op jit(solution)/shard_map/ppermute | solution.py:13
  101.9 5.0 %collective-permute-done.5 = bf16[16,2,8,512]{3,2,1,0:T(8,128)(2,1)S(1)} collective-permute-done((bf16[16,2,8,512]{3,2,1,0:T(8,128)(2,1)S(1)}, bf16[16,2,8,512]{3,2,1,0:T(8,128)(2,1)S(1)}, u32[]{:S(2)}, u32[]{:S(2)}) %collective-permute-start.5) | collective-permute-done | bytes 262176 | tf_op jit(solution)/shard_map/ppermute | solution.py:13
  106.9 3.4 %collective-permute-done.6 = bf16[16,2,8,512]{3,2,1,0:T(8,128)(2,1)S(1)} collective-permute-done((bf16[16,2,8,512]{3,2,1,0:T(8,128)(2,1)S(1)}, bf16[16,2,8,512]{3,2,1,0:T(8,128)(2,1)S(1)}, u32[]{:S(2)}, u32[]{:S(2)}) %collective-permute-start.6) | collective-permute-done | bytes 262176 | tf_op jit(solution)/shard_map/ppermute | solution.py:13
  113.9 6.8 %all-to-all-start.2 = ((bf16[16,3,2,8,512]{4,3,2,1,0:T(8,128)(2,1)}), bf16[16,3,2,8,512]{4,3,2,1,0:T(8,128)(2,1)S(1)}, u32[]{:S(2)}, u32[]{:S(2)}) async-start(bf16[16,3,2,8,512]{4,3,2,1,0:T(8,128)(2,1)} %pad_maximum_fusion), calls=%async_computation.2 | async-start | bytes 1572864 | tf_op jit(solution)/shard_map/all_to_all | solution.py:79
  122.0 38.4 %all-to-all-done.2 = bf16[16,3,2,8,512]{4,3,2,1,0:T(8,128)(2,1)S(1)} async-done(((bf16[16,3,2,8,512]{4,3,2,1,0:T(8,128)(2,1)}), bf16[16,3,2,8,512]{4,3,2,1,0:T(8,128)(2,1)S(1)}, u32[]{:S(2)}, u32[]{:S(2)}) %all-to-all-start.2) | async-done | bytes 786464 | tf_op jit(solution)/shard_map/all_to_all | solution.py:79
  (53 shorter events, 13.4 us)
Async XLA Ops:
  9.5 4.8 %copy-start.3 = (bf16[1,32,8,512]{3,2,1,0:T(8,128)(2,1)S(1)}, bf16[1,32,8,512]{3,2,1,0:T(8,128)(2,1)}, u32[]{:S(2)}) copy-start(bf16[1,32,8,512]{3,2,1,0:T(8,128)(2,1)} %param.11) | copy-start | bytes 786436
  9.5 4.9 %copy-start.4 = (bf16[1,32,8,512]{3,2,1,0:T(8,128)(2,1)S(1)}, bf16[1,32,8,512]{3,2,1,0:T(8,128)(2,1)}, u32[]{:S(2)}) copy-start(bf16[1,32,8,512]{3,2,1,0:T(8,128)(2,1)} %param.10) | copy-start | bytes 786436
  10.7 19.8 %copy-start = (f32[64,4,1,2048]{3,2,1,0:T(1,128)S(1)}, f32[64,4,1,2048]{3,2,1,0:T(1,128)}, u32[]{:S(2)}) copy-start(f32[64,4,1,2048]{3,2,1,0:T(1,128)} %get-tuple-element.4) | copy-start | bytes 6291460
  12.5 18.0 %collective-permute-start = (bf16[64,4,2048]{2,1,0:T(4,128)(2,1)}, bf16[64,4,2048]{2,1,0:T(4,128)(2,1)}, u32[]{:S(2)}, u32[]{:S(2)}) collective-permute-start(bf16[64,4,2048]{2,1,0:T(4,128)(2,1)} %copy.34), channel_id=1, source_target_pairs={{0,64},{64,0},{1,65},{65,1},{2,66},{66,2},{3,67},{67,3},{4,68},{68... | collective-permute-start | bytes 3145736 | tf_op jit(solution)/shard_map/ppermute | solution.py:33
  15.2 45.2 %all-to-all-start.1 = ((bf16[16,2,2,8,512]{4,3,2,1,0:T(8,128)(2,1)}), bf16[16,2,2,8,512]{4,3,2,1,0:T(8,128)(2,1)S(1)}, u32[]{:S(2)}, u32[]{:S(2)}) async-start(bf16[16,2,2,8,512]{4,3,2,1,0:T(8,128)(2,1)} %pad_maximum_fusion.1), calls=%async_computation.1 | async-start | bytes 1048576 | tf_op jit(solution)/shard_map/all_to_all | solution.py:55
  35.0 11.2 %copy-start.5 = (s32[1,32]{1,0:T(1,128)S(1)}, s32[1,32]{1,0:T(1,128)}, u32[]{:S(2)}) copy-start(s32[1,32]{1,0:T(1,128)} %param.7) | copy-start | bytes 388
  35.2 11.1 %collective-permute-start.1 = (bf16[64,2048]{1,0:T(8,128)(2,1)S(1)}, bf16[64,2048]{1,0:T(8,128)(2,1)S(1)}, u32[]{:S(2)}, u32[]{:S(2)}) collective-permute-start(bf16[64,2048]{1,0:T(8,128)(2,1)S(1)} %bitcast.131), channel_id=1, source_target_pairs={{0,128},{128,256},{256,384},{384,0},{1,129},{129,257},{257,385},{3... | collective-permute-start | bytes 786440 | tf_op jit(solution)/shard_map/ppermute | solution.py:13
  38.7 12.7 %collective-permute-start.2 = (bf16[64,2048]{1,0:T(8,128)(2,1)S(1)}, bf16[64,2048]{1,0:T(8,128)(2,1)S(1)}, u32[]{:S(2)}, u32[]{:S(2)}) collective-permute-start(bf16[64,2048]{1,0:T(8,128)(2,1)S(1)} %bitcast.132), channel_id=1, source_target_pairs={{0,256},{128,384},{256,0},{384,128},{1,257},{129,385},{257,1},{385... | collective-permute-start | bytes 786440 | tf_op jit(solution)/shard_map/ppermute | solution.py:13
  41.9 13.7 %collective-permute-start.3 = (bf16[64,2048]{1,0:T(8,128)(2,1)S(1)}, bf16[64,2048]{1,0:T(8,128)(2,1)S(1)}, u32[]{:S(2)}, u32[]{:S(2)}) collective-permute-start(bf16[64,2048]{1,0:T(8,128)(2,1)S(1)} %bitcast.133), channel_id=1, source_target_pairs={{0,384},{128,0},{256,128},{384,256},{1,385},{129,1},{257,129},{385... | collective-permute-start | bytes 786440 | tf_op jit(solution)/shard_map/ppermute | solution.py:13
  60.5 30.3 %all-to-all-start = ((bf16[16,2,8,512]{3,2,1,0:T(8,128)(2,1)}), bf16[16,2,8,512]{3,2,1,0:T(8,128)(2,1)S(1)}, u32[]{:S(2)}, u32[]{:S(2)}) async-start(bf16[16,2,8,512]{3,2,1,0:T(8,128)(2,1)} %bitcast.6), calls=%async_computation | async-start | bytes 524288 | tf_op jit(solution)/shard_map/all_to_all | solution.py:60
  72.5 24.6 %collective-permute-start.7 = (bf16[16,2,8,512]{3,2,1,0:T(8,128)(2,1)S(1)}, bf16[16,2,8,512]{3,2,1,0:T(8,128)(2,1)S(1)}, u32[]{:S(2)}, u32[]{:S(2)}) collective-permute-start(bf16[16,2,8,512]{3,2,1,0:T(8,128)(2,1)S(1)} %get-tuple-element.21), channel_id=1, source_target_pairs={{0,1},{1,2},{2,3},{3,0},{4,5},{5,6},{6,7},{7,4},{8,9},{9,10},{10,1... | collective-permute-start | bytes 786440 | tf_op jit(solution)/shard_map/ppermute | solution.py:13
  76.0 25.4 %collective-permute-start.8 = (bf16[16,2,8,512]{3,2,1,0:T(8,128)(2,1)S(1)}, bf16[16,2,8,512]{3,2,1,0:T(8,128)(2,1)S(1)}, u32[]{:S(2)}, u32[]{:S(2)}) collective-permute-start(bf16[16,2,8,512]{3,2,1,0:T(8,128)(2,1)S(1)} %get-tuple-element.21), channel_id=1, source_target_pairs={{0,2},{1,3},{2,0},{3,1},{4,6},{5,7},{6,4},{7,5},{8,10},{9,11},{10,... | collective-permute-start | bytes 786440 | tf_op jit(solution)/shard_map/ppermute | solution.py:13
  78.9 22.6 %collective-permute-start.9 = (bf16[16,2,8,512]{3,2,1,0:T(8,128)(2,1)S(1)}, bf16[16,2,8,512]{3,2,1,0:T(8,128)(2,1)S(1)}, u32[]{:S(2)}, u32[]{:S(2)}) collective-permute-start(bf16[16,2,8,512]{3,2,1,0:T(8,128)(2,1)S(1)} %get-tuple-element.21), channel_id=1, source_target_pairs={{0,3},{1,0},{2,1},{3,2},{4,7},{5,4},{6,5},{7,6},{8,11},{9,8},{10,9... | collective-permute-start | bytes 786440 | tf_op jit(solution)/shard_map/ppermute | solution.py:13
  90.8 11.1 %collective-permute-start.4 = (bf16[16,2,8,512]{3,2,1,0:T(8,128)(2,1)S(1)}, bf16[16,2,8,512]{3,2,1,0:T(8,128)(2,1)S(1)}, u32[]{:S(2)}, u32[]{:S(2)}) collective-permute-start(bf16[16,2,8,512]{3,2,1,0:T(8,128)(2,1)S(1)} %all-to-all-done), channel_id=1, source_target_pairs={{0,1},{1,2},{2,3},{3,0},{4,5},{5,6},{6,7},{7,4},{8,9},{9,10},{10,1... | collective-permute-start | bytes 786440 | tf_op jit(solution)/shard_map/ppermute | solution.py:13
  94.2 12.7 %collective-permute-start.5 = (bf16[16,2,8,512]{3,2,1,0:T(8,128)(2,1)S(1)}, bf16[16,2,8,512]{3,2,1,0:T(8,128)(2,1)S(1)}, u32[]{:S(2)}, u32[]{:S(2)}) collective-permute-start(bf16[16,2,8,512]{3,2,1,0:T(8,128)(2,1)S(1)} %all-to-all-done), channel_id=1, source_target_pairs={{0,2},{1,3},{2,0},{3,1},{4,6},{5,7},{6,4},{7,5},{8,10},{9,11},{10,... | collective-permute-start | bytes 786440 | tf_op jit(solution)/shard_map/ppermute | solution.py:13
  97.1 13.2 %collective-permute-start.6 = (bf16[16,2,8,512]{3,2,1,0:T(8,128)(2,1)S(1)}, bf16[16,2,8,512]{3,2,1,0:T(8,128)(2,1)S(1)}, u32[]{:S(2)}, u32[]{:S(2)}) collective-permute-start(bf16[16,2,8,512]{3,2,1,0:T(8,128)(2,1)S(1)} %all-to-all-done), channel_id=1, source_target_pairs={{0,3},{1,0},{2,1},{3,2},{4,7},{5,4},{6,5},{7,6},{8,11},{9,8},{10,9... | collective-permute-start | bytes 786440 | tf_op jit(solution)/shard_map/ppermute | solution.py:13
  113.9 48.0 %copy-start.1 = (bf16[1,32,8,512]{3,2,1,0:T(8,128)(2,1)S(1)}, bf16[1,32,8,512]{3,2,1,0:T(8,128)(2,1)}, u32[]{:S(2)}) copy-start(bf16[1,32,8,512]{3,2,1,0:T(8,128)(2,1)} %param.9) | copy-start | bytes 786436
  113.9 46.5 %all-to-all-start.2 = ((bf16[16,3,2,8,512]{4,3,2,1,0:T(8,128)(2,1)}), bf16[16,3,2,8,512]{4,3,2,1,0:T(8,128)(2,1)S(1)}, u32[]{:S(2)}, u32[]{:S(2)}) async-start(bf16[16,3,2,8,512]{4,3,2,1,0:T(8,128)(2,1)} %pad_maximum_fusion), calls=%async_computation.2 | async-start | bytes 1572864 | tf_op jit(solution)/shard_map/all_to_all | solution.py:79
  120.7 42.0 %copy-start.2 = (bf16[1,32,8,512]{3,2,1,0:T(8,128)(2,1)S(1)}, bf16[1,32,8,512]{3,2,1,0:T(8,128)(2,1)}, u32[]{:S(2)}) copy-start(bf16[1,32,8,512]{3,2,1,0:T(8,128)(2,1)} %param.8) | copy-start | bytes 786436

commit v2 on v1

v2 whole, which is shorter than its diff:
```python
import jax
import jax.numpy as jnp
from jax import lax
from jax.experimental import pallas as pl
from jax.experimental.pallas import tpu as pltpu
from jax.sharding import Mesh, PartitionSpec as P

decay = 0.9
bf16 = jnp.bfloat16
f32 = jnp.float32
params = pltpu.CompilerParams(vmem_limit_bytes=32 * 1024 * 1024)
wide = pltpu.CompilerParams(vmem_limit_bytes=56 * 1024 * 1024)


def shift(value, axis, by):
    n = lax.axis_size(axis)
    return lax.ppermute(value, axis, [(i, (i + by) % n) for i in range(n)])


def take_kernel(where, grad, out):
    out[0] = grad[...]


def stack_kernel(left, right, out):
    out[:, 0] = left[...]
    out[:, 1] = right[...]


def add_kernel(where, grad, got, own, *outs):
    step = pl.program_id(0)
    total = grad[...].astype(f32) + got[0].astype(f32)
    for i, out in enumerate(outs):

        @pl.when(step == i)
        def _():
            out[...] = total.astype(bf16)

    @pl.when(step == len(outs))
    def _():
        own[...] = total


def total_kernel(table, own, first, second, third, out):
    nblocks, piece, block = out.shape
    ncb = own.shape[1] // block
    total = own[...] + first[...].astype(f32) + second[...].astype(f32) + third[...].astype(f32)
    for k in range(nblocks):
        row, col = k // ncb * piece, k % ncb * block
        out[table[k]] = total[row : row + piece, col : col + block].astype(bf16)


def spec(shape):
    return pl.BlockSpec(shape, lambda *_: (0,) * len(shape))


def stack_roots(left, right):
    nz, per, piece, block = left.shape
    half = nz // 2
    return pl.pallas_call(
        stack_kernel,
        grid=(2,),
        in_specs=[pl.BlockSpec((half, per, piece, block), lambda i: (i, 0, 0, 0))] * 2,
        out_specs=pl.BlockSpec((half, 2, per, piece, block), lambda i: (i, 0, 0, 0, 0)),
        out_shape=jax.ShapeDtypeStruct((nz, 2, per, piece, block), bf16),
        cost_estimate=pl.CostEstimate(flops=0, bytes_accessed=8 * left.size, transcendentals=0),
        compiler_params=params,
        name="stack_roots",
    )(left, right)


def sum_dp(grad, table, nblocks, piece, block):
    nx = lax.axis_size("x")
    core = lax.axis_index("core")
    x = lax.axis_index("x")
    rows, cols = grad.shape
    band = cols // (2 * nx)
    other = pl.pallas_call(
        take_kernel,
        grid_spec=pltpu.PrefetchScalarGridSpec(
            num_scalar_prefetch=1,
            grid=(nx,),
            in_specs=[pl.BlockSpec((rows, band), lambda i, s: (0, 2 * i + s[0]))],
            out_specs=pl.BlockSpec((1, rows, band), lambda i, s: (i, 0, 0)),
        ),
        out_shape=jax.ShapeDtypeStruct((nx, rows, band), bf16),
        cost_estimate=pl.CostEstimate(flops=0, bytes_accessed=2 * rows * cols, transcendentals=0),
        compiler_params=params,
        name="other_core_bands",
    )((1 - core).astype(jnp.int32).reshape(1), grad)
    got = lax.ppermute(other, "core", [(0, 1), (1, 0)])

    order = (2, 1, 3, 0)
    owners = jnp.stack([(x + by) % nx for by in order]).astype(jnp.int32)
    piece_spec = spec((rows, band))
    bf_piece = jax.ShapeDtypeStruct((rows, band), bf16)
    own, *pieces = pl.pallas_call(
        add_kernel,
        grid_spec=pltpu.PrefetchScalarGridSpec(
            num_scalar_prefetch=1,
            grid=(nx,),
            in_specs=[
                pl.BlockSpec((rows, band), lambda i, s: (0, s[nx + i])),
                pl.BlockSpec((1, rows, band), lambda i, s: (s[i], 0, 0)),
            ],
            out_specs=[piece_spec] * nx,
        ),
        out_shape=[jax.ShapeDtypeStruct((rows, band), f32)] + [bf_piece] * (nx - 1),
        cost_estimate=pl.CostEstimate(
            flops=rows * cols // 2, bytes_accessed=4 * rows * cols, transcendentals=0
        ),
        compiler_params=params,
        name="add_cores",
    )(jnp.concatenate([owners, 2 * owners + core]).astype(jnp.int32), grad, got)
    pieces = [shift(value, "x", by) for by, value in zip(order, pieces)]
    return pl.pallas_call(
        total_kernel,
        grid_spec=pltpu.PrefetchScalarGridSpec(
            num_scalar_prefetch=1,
            grid=(1,),
            in_specs=[piece_spec] * nx,
            out_specs=spec((nblocks, piece, block)),
        ),
        out_shape=jax.ShapeDtypeStruct((nblocks, piece, block), bf16),
        cost_estimate=pl.CostEstimate(
            flops=3 * rows * band, bytes_accessed=6 * rows * band * 2, transcendentals=0
        ),
        compiler_params=params,
        name="total_in_slots",
    )(table, own, *pieces)


def settle_kernel(table, back, left, right, left_new, right_new, update):
    nz, _, per, piece, block = back.shape
    ncb = update.shape[1] // block
    for arr, stat, new in ((0, left, left_new), (1, right, right_new)):
        gram = back[:, arr].astype(f32).reshape(nz * per, piece, block)
        new[...] = (decay * stat[...].astype(f32) + gram).astype(bf16)
    for rb in range(0, update.shape[0] // piece, 2):
        for cb in range(ncb):
            pair = []
            for k in (rb * ncb + cb, (rb + 1) * ncb + cb):
                slot = table[k]
                pair.append(back[slot // per, 2, slot % per].astype(f32))
            update[rb * piece : (rb + 2) * piece, cb * block : (cb + 1) * block] = jnp.concatenate(
                pair, 0
            ).astype(bf16)


def settle(table, back, left, right, rows, cols):
    whole = lambda shape: pl.BlockSpec(shape, lambda i, t: (0,) * len(shape))
    return pl.pallas_call(
        settle_kernel,
        grid_spec=pltpu.PrefetchScalarGridSpec(
            num_scalar_prefetch=1,
            grid=(1,),
            in_specs=[whole(back.shape), whole(left.shape), whole(right.shape)],
            out_specs=[whole(left.shape), whole(right.shape), whole((rows, cols))],
        ),
        out_shape=[
            jax.ShapeDtypeStruct(left.shape, bf16),
            jax.ShapeDtypeStruct(right.shape, bf16),
            jax.ShapeDtypeStruct((rows, cols), bf16),
        ],
        cost_estimate=pl.CostEstimate(
            flops=4 * left.size, bytes_accessed=8 * left.size * 2, transcendentals=0
        ),
        compiler_params=params,
        name="settle",
    )(table, back, left, right)


def products_kernel(where, *refs):
    g_parts, (left_root, right_root, back, rows, gram) = refs[:4], refs[4:]
    nz, _, _, piece, block = back.shape
    ny = len(g_parts)
    y = where[0]
    scale = (1.0 - decay) / block

    def flat(value):
        return value.astype(f32).reshape(nz * piece, block).astype(bf16)

    def dot(a, b, over=((1,), (0,))):
        return lax.dot_general(a, b, (over, ((), ())), preferred_element_type=f32)

    for by, part in enumerate(g_parts):
        rows[:, lax.rem(y - by + ny, ny)] = part[:, 0].astype(f32)
    g = rows[...].reshape(block, block).astype(bf16)
    half = dot(flat(left_root[:, 0, 0]), g).astype(bf16)
    back[:, 2, 0] = dot(half, right_root[0]).reshape(nz, piece, block).astype(bf16)
    left = dot(flat(g_parts[0][:, 0]), g, ((1,), (1,)))
    back[:, 0, 0] = (scale * left).reshape(nz, piece, block).astype(bf16)
    gram[...] = dot(g, g, ((0,), (0,))).reshape(gram.shape)
    back[:, 1, 0] = (scale * gram[:, y]).astype(bf16)


def products(g_parts, roots, right_root, y):
    ny = len(g_parts)
    nz, per, piece, block = g_parts[0].shape
    part = pl.BlockSpec((nz, 1, piece, block), lambda s, _: (0, s, 0, 0))
    several = lambda n: pl.BlockSpec((nz, n, 1, piece, block), lambda s, _: (0, 0, s, 0, 0))
    return pl.pallas_call(
        products_kernel,
        grid_spec=pltpu.PrefetchScalarGridSpec(
            num_scalar_prefetch=1,
            grid=(per,),
            in_specs=[part] * ny + [several(1), pl.BlockSpec((1, block, block), lambda s, _: (s, 0, 0))],
            out_specs=several(3),
            scratch_shapes=[pltpu.VMEM((nz, ny, piece, block), f32)] * 2,
        ),
        out_shape=jax.ShapeDtypeStruct((nz, 3, per, piece, block), bf16),
        cost_estimate=pl.CostEstimate(
            flops=4 * per * block**3, bytes_accessed=24 * per * block * block, transcendentals=0
        ),
        compiler_params=wide,
        name="products",
    )(y.astype(jnp.int32).reshape(1), *g_parts, roots, right_root)


def local(grad_parts, slot_table, left_stat, right_stat, left_root, right_root):
    nz, ny = lax.axis_size("z"), lax.axis_size("y")
    y = lax.axis_index("y")
    nblocks, piece, block = left_stat.shape[1:]
    rows_dev = grad_parts.shape[1]
    ncb = nblocks // (rows_dev // piece)
    per = nblocks // nz
    table = slot_table[0]
    by_owner = (nz, per, piece, block)

    def to_owner(value):
        return lax.all_to_all(value, "z", 0, 0, tiled=True)

    def from_y(value):
        far = [shift(value, "y", by) for by in (2, 1, 3)]
        return [value, far[1], far[0], far[2]]

    roots = to_owner(stack_roots(left_root[0].reshape(by_owner), right_root[0].reshape(by_owner)))
    placed = sum_dp(grad_parts[0], table, nblocks, piece, block)
    grads = to_owner(placed.reshape(by_owner))
    right = from_y(roots[:, 1])
    right = jnp.stack([lax.select_n((y - owner) % ny, *right) for owner in range(ny)])
    right = right.transpose(2, 1, 0, 3, 4).reshape(per, block, block)
    back = products(from_y(grads), roots, right, y)
    back = lax.all_to_all(back, "z", 0, 0, tiled=True)
    left_new, right_new, update = settle(
        table, back, left_stat[0], right_stat[0], rows_dev, ncb * block
    )
    return left_new[None], right_new[None], update


def solution(mesh):
    ny = 4
    devices = mesh.devices
    split = Mesh(
        devices.reshape(devices.shape[0] // 2, 2, devices.shape[1] // ny, ny), ("x", "core", "z", "y")
    )
    dp, fsdp = ("x", "core"), ("z", "y")
    factor = P(dp, None, fsdp, None)
    return jax.shard_map(
        local,
        mesh=split,
        in_specs=(P(dp, fsdp, None), P(dp, None), factor, factor, factor, factor),
        out_specs=(factor, factor, P(fsdp, dp)),
        check_vma=False,
    )
```

time: 164 us -> 151 us (0.921)
  the two profiles are of different devices: /device:TPU:42 before, /device:TPU:44 now
where the time goes in v2:
time: 151 us; the launch traced here: 150 us
  starting transfers between devices  56.5 us (37%)
  blocking collectives  48.2 us (32%)
  waiting for transfers between devices  27.1 us (18%)
  Pallas kernels  11.1 us (7%)
  local copies, waits for them, and re-layouts  4.97 us (3%)
    all_to_all x1, blocking collectives, local(): back = lax.all_to_all(back, 'z', 0, 0, tiled=True)  48.2 us
    ppermute x9, starting transfers between devices, shift(): return lax.ppermute(value, axis, [(i, (i + by) % n) for i in range(n)])  29.1 us
    all_to_all x2, starting transfers between devices, to_owner(): return lax.all_to_all(value, 'z', 0, 0, tiled=True)  25.4 us
    ppermute x9, waiting for transfers between devices, shift(): return lax.ppermute(value, axis, [(i, (i + by) % n) for i in range(n)])  15.4 us
    all_to_all x2, waiting for transfers between devices, to_owner(): return lax.all_to_all(value, 'z', 0, 0, tiled=True)  8.99 us
    pallas_call x1, Pallas kernels, products(): pl.pallas_call(products_kernel, grid_spec=pltpu.PrefetchScalarGridSpec(nu...  4.28 us
  transfers between devices with their start and end apart: 12, of which 7 were waited for; matrix products, arithmetic and copies ran while one was open for 2% of the time, Pallas kernels for 3%

profile of v2, /device:TPU:44, one launch (start us, length us, event | category | flops | bytes accessed | tf_op | source)
XLA Modules:
  0.0 150.1 jit_solution(3114259212103345253)
XLA Ops:
  3.5 15.2 %all-to-all-start.1 = ((bf16[16,2,2,8,512]{4,3,2,1,0:T(8,128)(2,1)}), bf16[16,2,2,8,512]{4,3,2,1,0:T(8,128)(2,1)}, u32[]{:S(2)}, u32[]{:S(2)}) async-start(bf16[16,2,2,8,512]{4,3,2,1,0:T(8,128)(2,1)} %stack_roots.1), calls=%async_computation.1 | async-start | bytes 1048576 | tf_op jit(solution)/shard_map/all_to_all | solution.py:230
  18.7 1.6 %other_core_bands.1 = bf16[4,64,2048]{2,1,0:T(8,128)(2,1)} custom-call(s32[1]{0:T(128)} %bitcast.7.where, bf16[64,16384]{1,0:T(8,128)(2,1)S(1)} %bitcast.36), custom_call_target="tpu_custom_call" | custom-call | bytes 2097152 | tf_op jit(solution)/shard_map/other_core_bands/pallas_call | solution.py:77
  20.4 2.0 %collective-permute-start = (bf16[4,64,2048]{2,1,0:T(8,128)(2,1)}, bf16[4,64,2048]{2,1,0:T(8,128)(2,1)S(1)}, u32[]{:S(2)}, u32[]{:S(2)}) collective-permute-start(bf16[4,64,2048]{2,1,0:T(8,128)(2,1)} %other_core_bands.1), channel_id=1, source_target_pairs={{0,64},{64,0},{1,65},{65,1},{2,66},{66,2},{3,67},{67,3},{4,68},{68... | collective-permute-start | bytes 3145736 | tf_op jit(solution)/shard_map/ppermute | solution.py:90
  22.6 2.6 %collective-permute-done.got = bf16[4,64,2048]{2,1,0:T(8,128)(2,1)S(1)} collective-permute-done((bf16[4,64,2048]{2,1,0:T(8,128)(2,1)}, bf16[4,64,2048]{2,1,0:T(8,128)(2,1)S(1)}, u32[]{:S(2)}, u32[]{:S(2)}) %collective-permute-start) | collective-permute-done | bytes 1048608 | tf_op jit(solution)/shard_map/ppermute | solution.py:90
  26.5 2.4 %collective-permute-start.1 = (bf16[64,2048]{1,0:T(8,128)(2,1)S(1)}, bf16[64,2048]{1,0:T(8,128)(2,1)S(1)}, u32[]{:S(2)}, u32[]{:S(2)}) collective-permute-start(bf16[64,2048]{1,0:T(8,128)(2,1)S(1)} %get-tuple-element.11), channel_id=1, source_target_pairs={{0,256},{128,384},{256,0},{384,128},{1,257},{129,385},{257,1},{385... | collective-permute-start | bytes 786440 | tf_op jit(solution)/shard_map/ppermute | solution.py:17
  29.0 4.0 %collective-permute-start.2 = (bf16[64,2048]{1,0:T(8,128)(2,1)S(1)}, bf16[64,2048]{1,0:T(8,128)(2,1)S(1)}, u32[]{:S(2)}, u32[]{:S(2)}) collective-permute-start(bf16[64,2048]{1,0:T(8,128)(2,1)S(1)} %get-tuple-element.12), channel_id=1, source_target_pairs={{0,128},{128,256},{256,384},{384,0},{1,129},{129,257},{257,385},{3... | collective-permute-start | bytes 786440 | tf_op jit(solution)/shard_map/ppermute | solution.py:17
  33.0 2.0 %collective-permute-start.3 = (bf16[64,2048]{1,0:T(8,128)(2,1)S(1)}, bf16[64,2048]{1,0:T(8,128)(2,1)S(1)}, u32[]{:S(2)}, u32[]{:S(2)}) collective-permute-start(bf16[64,2048]{1,0:T(8,128)(2,1)S(1)} %get-tuple-element.13), channel_id=1, source_target_pairs={{0,384},{128,0},{256,128},{384,256},{1,385},{129,1},{257,129},{385... | collective-permute-start | bytes 786440 | tf_op jit(solution)/shard_map/ppermute | solution.py:17
  35.0 4.2 %collective-permute-done.1.first = bf16[64,2048]{1,0:T(8,128)(2,1)S(1)} collective-permute-done((bf16[64,2048]{1,0:T(8,128)(2,1)S(1)}, bf16[64,2048]{1,0:T(8,128)(2,1)S(1)}, u32[]{:S(2)}, u32[]{:S(2)}) %collective-permute-start.1) | collective-permute-done | bytes 262176 | tf_op jit(solution)/shard_map/ppermute | solution.py:17
  39.1 4.8 %collective-permute-done.2.second = bf16[64,2048]{1,0:T(8,128)(2,1)S(1)} collective-permute-done((bf16[64,2048]{1,0:T(8,128)(2,1)S(1)}, bf16[64,2048]{1,0:T(8,128)(2,1)S(1)}, u32[]{:S(2)}, u32[]{:S(2)}) %collective-permute-start.2) | collective-permute-done | bytes 262176 | tf_op jit(solution)/shard_map/ppermute | solution.py:17
  43.9 1.4 total_in_slots.1
  45.3 1.8 %all-to-all-done.1.refs_4_ = bf16[16,2,2,8,512]{4,3,2,1,0:T(8,128)(2,1)} async-done(((bf16[16,2,2,8,512]{4,3,2,1,0:T(8,128)(2,1)}), bf16[16,2,2,8,512]{4,3,2,1,0:T(8,128)(2,1)}, u32[]{:S(2)}, u32[]{:S(2)}) %all-to-all-start.1) | async-done | bytes 524320 | tf_op jit(solution)/shard_map/all_to_all | solution.py:230
  47.1 10.2 %all-to-all-start = ((bf16[16,2,8,512]{3,2,1,0:T(8,128)(2,1)}), bf16[16,2,8,512]{3,2,1,0:T(8,128)(2,1)S(1)}, u32[]{:S(2)}, u32[]{:S(2)}) async-start(bf16[16,2,8,512]{3,2,1,0:T(8,128)(2,1)} %bitcast.8), calls=%async_computation | async-start | bytes 524288 | tf_op jit(solution)/shard_map/all_to_all | solution.py:230
  58.3 4.2 %collective-permute-start.8 = (bf16[16,2,8,512]{3,2,1,0:T(8,128)(2,1)S(1)}, bf16[16,2,8,512]{3,2,1,0:T(8,128)(2,1)S(1)}, u32[]{:S(2)}, u32[]{:S(2)}) collective-permute-start(bf16[16,2,8,512]{3,2,1,0:T(8,128)(2,1)S(1)} %slice_bitcast_fusion), channel_id=1, source_target_pairs={{0,2},{1,3},{2,0},{3,1},{4,6},{5,7},{6,4},{7,5},{8,10},{9,11},{10,... | collective-permute-start | bytes 786440 | tf_op jit(solution)/shard_map/ppermute | solution.py:17
  62.5 3.3 %collective-permute-start.9 = (bf16[16,2,8,512]{3,2,1,0:T(8,128)(2,1)S(1)}, bf16[16,2,8,512]{3,2,1,0:T(8,128)(2,1)S(1)}, u32[]{:S(2)}, u32[]{:S(2)}) collective-permute-start(bf16[16,2,8,512]{3,2,1,0:T(8,128)(2,1)S(1)} %slice_bitcast_fusion), channel_id=1, source_target_pairs={{0,3},{1,0},{2,1},{3,2},{4,7},{5,4},{6,5},{7,6},{8,11},{9,8},{10,9... | collective-permute-start | bytes 786440 | tf_op jit(solution)/shard_map/ppermute | solution.py:17
  65.7 2.6 %collective-permute-start.7 = (bf16[16,2,8,512]{3,2,1,0:T(8,128)(2,1)S(1)}, bf16[16,2,8,512]{3,2,1,0:T(8,128)(2,1)S(1)}, u32[]{:S(2)}, u32[]{:S(2)}) collective-permute-start(bf16[16,2,8,512]{3,2,1,0:T(8,128)(2,1)S(1)} %slice_bitcast_fusion), channel_id=1, source_target_pairs={{0,1},{1,2},{2,3},{3,0},{4,5},{5,6},{6,7},{7,4},{8,9},{9,10},{10,1... | collective-permute-start | bytes 786440 | tf_op jit(solution)/shard_map/ppermute | solution.py:17
  68.4 7.2 %all-to-all-done.refs_0_ = bf16[16,2,8,512]{3,2,1,0:T(8,128)(2,1)S(1)} async-done(((bf16[16,2,8,512]{3,2,1,0:T(8,128)(2,1)}), bf16[16,2,8,512]{3,2,1,0:T(8,128)(2,1)S(1)}, u32[]{:S(2)}, u32[]{:S(2)}) %all-to-all-start) | async-done | bytes 262176 | tf_op jit(solution)/shard_map/all_to_all | solution.py:230
  75.6 3.5 %collective-permute-start.4 = (bf16[16,2,8,512]{3,2,1,0:T(8,128)(2,1)S(1)}, bf16[16,2,8,512]{3,2,1,0:T(8,128)(2,1)S(1)}, u32[]{:S(2)}, u32[]{:S(2)}) collective-permute-start(bf16[16,2,8,512]{3,2,1,0:T(8,128)(2,1)S(1)} %all-to-all-done.refs_0_), channel_id=1, source_target_pairs={{0,1},{1,2},{2,3},{3,0},{4,5},{5,6},{6,7},{7,4},{8,9},{9,10},{10,1... | collective-permute-start | bytes 786440 | tf_op jit(solution)/shard_map/ppermute | solution.py:17
  79.1 2.8 %collective-permute-start.5 = (bf16[16,2,8,512]{3,2,1,0:T(8,128)(2,1)S(1)}, bf16[16,2,8,512]{3,2,1,0:T(8,128)(2,1)S(1)}, u32[]{:S(2)}, u32[]{:S(2)}) collective-permute-start(bf16[16,2,8,512]{3,2,1,0:T(8,128)(2,1)S(1)} %all-to-all-done.refs_0_), channel_id=1, source_target_pairs={{0,2},{1,3},{2,0},{3,1},{4,6},{5,7},{6,4},{7,5},{8,10},{9,11},{10,... | collective-permute-start | bytes 786440 | tf_op jit(solution)/shard_map/ppermute | solution.py:17
  81.9 4.3 %collective-permute-start.6 = (bf16[16,2,8,512]{3,2,1,0:T(8,128)(2,1)S(1)}, bf16[16,2,8,512]{3,2,1,0:T(8,128)(2,1)S(1)}, u32[]{:S(2)}, u32[]{:S(2)}) collective-permute-start(bf16[16,2,8,512]{3,2,1,0:T(8,128)(2,1)S(1)} %all-to-all-done.refs_0_), channel_id=1, source_target_pairs={{0,3},{1,0},{2,1},{3,2},{4,7},{5,4},{6,5},{7,6},{8,11},{9,8},{10,9... | collective-permute-start | bytes 786440 | tf_op jit(solution)/shard_map/ppermute | solution.py:17
  88.7 3.1 %collective-permute-done.5.refs_2_ = bf16[16,2,8,512]{3,2,1,0:T(8,128)(2,1)S(1)} collective-permute-done((bf16[16,2,8,512]{3,2,1,0:T(8,128)(2,1)S(1)}, bf16[16,2,8,512]{3,2,1,0:T(8,128)(2,1)S(1)}, u32[]{:S(2)}, u32[]{:S(2)}) %collective-permute-start.5) | collective-permute-done | bytes 262176 | tf_op jit(solution)/shard_map/ppermute | solution.py:17
  91.8 3.4 %collective-permute-done.6.refs_3_ = bf16[16,2,8,512]{3,2,1,0:T(8,128)(2,1)S(1)} collective-permute-done((bf16[16,2,8,512]{3,2,1,0:T(8,128)(2,1)S(1)}, bf16[16,2,8,512]{3,2,1,0:T(8,128)(2,1)S(1)}, u32[]{:S(2)}, u32[]{:S(2)}) %collective-permute-start.6) | collective-permute-done | bytes 262176 | tf_op jit(solution)/shard_map/ppermute | solution.py:17
  95.9 4.3 %products.1 = bf16[16,3,2,8,512]{4,3,2,1,0:T(8,128)(2,1)} custom-call(s32[1]{0:T(128)} %bitcast.1.where, bf16[16,2,8,512]{3,2,1,0:T(8,128)(2,1)} %copy-done.6, bf16[16,2,8,512]{3,2,1,0:T(8,128)(2,1)} %copy-done.7, bf16[16,2,8,512]{3,2,1,0:T(8,128)(2,1)} %copy-done.8, bf16[16,2,8,512]{3,2,1,0:T(8,128)(2,1)} %copy-done.9, ...), custom_call_target="tpu_custom_call" | custom-call | flops 1073741824 | bytes 12582912 | tf_op jit(solution)/shard_map/products/pallas_call | solution.py:201
  100.2 48.2 %all_to_all.15.back = bf16[16,3,2,8,512]{4,3,2,1,0:T(8,128)(2,1)S(1)} all-to-all(bf16[16,3,2,8,512]{4,3,2,1,0:T(8,128)(2,1)} %products.1), channel_id=1, replica_groups=mesh['x'=4,'core'=2,'z'=16,'y'=4] {'z'}, dimensions={0} | all-to-all | bytes 1572864 | tf_op jit(solution)/shard_map/all_to_all | solution.py:243
  148.4 1.7 %settle.1 = (bf16[32,8,512]{2,1,0:T(8,128)(2,1)}, bf16[32,8,512]{2,1,0:T(8,128)(2,1)}, bf16[64,2048]{1,0:T(8,128)(2,1)}) custom-call(s32[32]{0:T(128)S(1)} %bitcast.43, bf16[16,3,2,8,512]{4,3,2,1,0:T(8,128)(2,1)S(1)} %all_to_all.15.back, bf16[32,8,512]{2,1,0:T(8,128)(2,1)S(1)} %bitcast.38, bf16[32,8,512]{2,1,0:T(8,128)(2,1)S(1)} %bitcast.39), custom_call_target="tpu_custom_call" | custom-call | flops 524288 | bytes 2097152 | tf_op jit(solution)/shard_map/settle/pallas_call | solution.py:151
  (33 shorter events, 8.4 us)
Async XLA Ops:
  0.6 18.1 %copy-start = (bf16[1,64,16384]{2,1,0:T(8,128)(2,1)S(1)}, bf16[1,64,16384]{2,1,0:T(8,128)(2,1)}, u32[]{:S(2)}) copy-start(bf16[1,64,16384]{2,1,0:T(8,128)(2,1)} %param.6) | copy-start | bytes 6291460
  0.6 1.1 copy-start.3
  1.7 0.9 copy-start.4
  3.5 43.6 %all-to-all-start.1 = ((bf16[16,2,2,8,512]{4,3,2,1,0:T(8,128)(2,1)}), bf16[16,2,2,8,512]{4,3,2,1,0:T(8,128)(2,1)}, u32[]{:S(2)}, u32[]{:S(2)}) async-start(bf16[16,2,2,8,512]{4,3,2,1,0:T(8,128)(2,1)} %stack_roots.1), calls=%async_computation.1 | async-start | bytes 1048576 | tf_op jit(solution)/shard_map/all_to_all | solution.py:230
  20.4 23.5 %copy-start.5 = (s32[1,32]{1,0:T(1,128)S(1)}, s32[1,32]{1,0:T(1,128)}, u32[]{:S(2)}) copy-start(s32[1,32]{1,0:T(1,128)} %param.7) | copy-start | bytes 388
  20.4 4.9 %collective-permute-start = (bf16[4,64,2048]{2,1,0:T(8,128)(2,1)}, bf16[4,64,2048]{2,1,0:T(8,128)(2,1)S(1)}, u32[]{:S(2)}, u32[]{:S(2)}) collective-permute-start(bf16[4,64,2048]{2,1,0:T(8,128)(2,1)} %other_core_bands.1), channel_id=1, source_target_pairs={{0,64},{64,0},{1,65},{65,1},{2,66},{66,2},{3,67},{67,3},{4,68},{68... | collective-permute-start | bytes 3145736 | tf_op jit(solution)/shard_map/ppermute | solution.py:90
  26.5 12.6 %collective-permute-start.1 = (bf16[64,2048]{1,0:T(8,128)(2,1)S(1)}, bf16[64,2048]{1,0:T(8,128)(2,1)S(1)}, u32[]{:S(2)}, u32[]{:S(2)}) collective-permute-start(bf16[64,2048]{1,0:T(8,128)(2,1)S(1)} %get-tuple-element.11), channel_id=1, source_target_pairs={{0,256},{128,384},{256,0},{384,128},{1,257},{129,385},{257,1},{385... | collective-permute-start | bytes 786440 | tf_op jit(solution)/shard_map/ppermute | solution.py:17
  29.0 14.9 %collective-permute-start.2 = (bf16[64,2048]{1,0:T(8,128)(2,1)S(1)}, bf16[64,2048]{1,0:T(8,128)(2,1)S(1)}, u32[]{:S(2)}, u32[]{:S(2)}) collective-permute-start(bf16[64,2048]{1,0:T(8,128)(2,1)S(1)} %get-tuple-element.12), channel_id=1, source_target_pairs={{0,128},{128,256},{256,384},{384,0},{1,129},{129,257},{257,385},{3... | collective-permute-start | bytes 786440 | tf_op jit(solution)/shard_map/ppermute | solution.py:17
  33.0 10.9 %collective-permute-start.3 = (bf16[64,2048]{1,0:T(8,128)(2,1)S(1)}, bf16[64,2048]{1,0:T(8,128)(2,1)S(1)}, u32[]{:S(2)}, u32[]{:S(2)}) collective-permute-start(bf16[64,2048]{1,0:T(8,128)(2,1)S(1)} %get-tuple-element.13), channel_id=1, source_target_pairs={{0,384},{128,0},{256,128},{384,256},{1,385},{129,1},{257,129},{385... | collective-permute-start | bytes 786440 | tf_op jit(solution)/shard_map/ppermute | solution.py:17
  47.1 28.5 %all-to-all-start = ((bf16[16,2,8,512]{3,2,1,0:T(8,128)(2,1)}), bf16[16,2,8,512]{3,2,1,0:T(8,128)(2,1)S(1)}, u32[]{:S(2)}, u32[]{:S(2)}) async-start(bf16[16,2,8,512]{3,2,1,0:T(8,128)(2,1)} %bitcast.8), calls=%async_computation | async-start | bytes 524288 | tf_op jit(solution)/shard_map/all_to_all | solution.py:230
  58.3 23.7 %collective-permute-start.8 = (bf16[16,2,8,512]{3,2,1,0:T(8,128)(2,1)S(1)}, bf16[16,2,8,512]{3,2,1,0:T(8,128)(2,1)S(1)}, u32[]{:S(2)}, u32[]{:S(2)}) collective-permute-start(bf16[16,2,8,512]{3,2,1,0:T(8,128)(2,1)S(1)} %slice_bitcast_fusion), channel_id=1, source_target_pairs={{0,2},{1,3},{2,0},{3,1},{4,6},{5,7},{6,4},{7,5},{8,10},{9,11},{10,... | collective-permute-start | bytes 786440 | tf_op jit(solution)/shard_map/ppermute | solution.py:17
  62.5 23.8 %collective-permute-start.9 = (bf16[16,2,8,512]{3,2,1,0:T(8,128)(2,1)S(1)}, bf16[16,2,8,512]{3,2,1,0:T(8,128)(2,1)S(1)}, u32[]{:S(2)}, u32[]{:S(2)}) collective-permute-start(bf16[16,2,8,512]{3,2,1,0:T(8,128)(2,1)S(1)} %slice_bitcast_fusion), channel_id=1, source_target_pairs={{0,3},{1,0},{2,1},{3,2},{4,7},{5,4},{6,5},{7,6},{8,11},{9,8},{10,9... | collective-permute-start | bytes 786440 | tf_op jit(solution)/shard_map/ppermute | solution.py:17
  65.7 20.5 %collective-permute-start.7 = (bf16[16,2,8,512]{3,2,1,0:T(8,128)(2,1)S(1)}, bf16[16,2,8,512]{3,2,1,0:T(8,128)(2,1)S(1)}, u32[]{:S(2)}, u32[]{:S(2)}) collective-permute-start(bf16[16,2,8,512]{3,2,1,0:T(8,128)(2,1)S(1)} %slice_bitcast_fusion), channel_id=1, source_target_pairs={{0,1},{1,2},{2,3},{3,0},{4,5},{5,6},{6,7},{7,4},{8,9},{9,10},{10,1... | collective-permute-start | bytes 786440 | tf_op jit(solution)/shard_map/ppermute | solution.py:17
  75.6 11.9 %copy-start.6 = (bf16[16,2,8,512]{3,2,1,0:T(8,128)(2,1)}, bf16[16,2,8,512]{3,2,1,0:T(8,128)(2,1)S(1)}, u32[]{:S(2)}) copy-start(bf16[16,2,8,512]{3,2,1,0:T(8,128)(2,1)S(1)} %all-to-all-done.refs_0_) | copy-start | bytes 786436
  75.6 13.1 %collective-permute-start.4 = (bf16[16,2,8,512]{3,2,1,0:T(8,128)(2,1)S(1)}, bf16[16,2,8,512]{3,2,1,0:T(8,128)(2,1)S(1)}, u32[]{:S(2)}, u32[]{:S(2)}) collective-permute-start(bf16[16,2,8,512]{3,2,1,0:T(8,128)(2,1)S(1)} %all-to-all-done.refs_0_), channel_id=1, source_target_pairs={{0,1},{1,2},{2,3},{3,0},{4,5},{5,6},{6,7},{7,4},{8,9},{9,10},{10,1... | collective-permute-start | bytes 786440 | tf_op jit(solution)/shard_map/ppermute | solution.py:17
  79.1 12.7 %collective-permute-start.5 = (bf16[16,2,8,512]{3,2,1,0:T(8,128)(2,1)S(1)}, bf16[16,2,8,512]{3,2,1,0:T(8,128)(2,1)S(1)}, u32[]{:S(2)}, u32[]{:S(2)}) collective-permute-start(bf16[16,2,8,512]{3,2,1,0:T(8,128)(2,1)S(1)} %all-to-all-done.refs_0_), channel_id=1, source_target_pairs={{0,2},{1,3},{2,0},{3,1},{4,6},{5,7},{6,4},{7,5},{8,10},{9,11},{10,... | collective-permute-start | bytes 786440 | tf_op jit(solution)/shard_map/ppermute | solution.py:17
  81.9 13.2 %collective-permute-start.6 = (bf16[16,2,8,512]{3,2,1,0:T(8,128)(2,1)S(1)}, bf16[16,2,8,512]{3,2,1,0:T(8,128)(2,1)S(1)}, u32[]{:S(2)}, u32[]{:S(2)}) collective-permute-start(bf16[16,2,8,512]{3,2,1,0:T(8,128)(2,1)S(1)} %all-to-all-done.refs_0_), channel_id=1, source_target_pairs={{0,3},{1,0},{2,1},{3,2},{4,7},{5,4},{6,5},{7,6},{8,11},{9,8},{10,9... | collective-permute-start | bytes 786440 | tf_op jit(solution)/shard_map/ppermute | solution.py:17
  88.7 6.5 %copy-start.7 = (bf16[16,2,8,512]{3,2,1,0:T(8,128)(2,1)}, bf16[16,2,8,512]{3,2,1,0:T(8,128)(2,1)S(1)}, u32[]{:S(2)}) copy-start(bf16[16,2,8,512]{3,2,1,0:T(8,128)(2,1)S(1)} %collective-permute-done.4.refs_1_) | copy-start | bytes 786436
  91.8 3.4 %copy-start.8 = (bf16[16,2,8,512]{3,2,1,0:T(8,128)(2,1)}, bf16[16,2,8,512]{3,2,1,0:T(8,128)(2,1)S(1)}, u32[]{:S(2)}) copy-start(bf16[16,2,8,512]{3,2,1,0:T(8,128)(2,1)S(1)} %collective-permute-done.5.refs_2_) | copy-start | bytes 786436
  95.2 0.7 copy-start.9
  95.9 52.5 %copy-start.1 = (bf16[1,32,8,512]{3,2,1,0:T(8,128)(2,1)S(1)}, bf16[1,32,8,512]{3,2,1,0:T(8,128)(2,1)}, u32[]{:S(2)}) copy-start(bf16[1,32,8,512]{3,2,1,0:T(8,128)(2,1)} %param.8) | copy-start | bytes 786436
  95.9 52.5 %copy-start.2 = (bf16[1,32,8,512]{3,2,1,0:T(8,128)(2,1)S(1)}, bf16[1,32,8,512]{3,2,1,0:T(8,128)(2,1)}, u32[]{:S(2)}) copy-start(bf16[1,32,8,512]{3,2,1,0:T(8,128)(2,1)} %param.9) | copy-start | bytes 786436

commit v3 on v2

--- a/solution.py
+++ b/solution.py
@@ -8,8 +8,7 @@
 decay = 0.9
 bf16 = jnp.bfloat16
 f32 = jnp.float32
-params = pltpu.CompilerParams(vmem_limit_bytes=32 * 1024 * 1024)
-wide = pltpu.CompilerParams(vmem_limit_bytes=56 * 1024 * 1024)
+params = pltpu.CompilerParams(vmem_limit_bytes=12 * 1024 * 1024)
 
 
 def shift(value, axis, by):
@@ -17,18 +16,9 @@
     return lax.ppermute(value, axis, [(i, (i + by) % n) for i in range(n)])
 
 
-def take_kernel(where, grad, out):
-    out[0] = grad[...]
-
-
-def stack_kernel(left, right, out):
-    out[:, 0] = left[...]
-    out[:, 1] = right[...]
-
-
 def add_kernel(where, grad, got, own, *outs):
     step = pl.program_id(0)
-    total = grad[...].astype(f32) + got[0].astype(f32)
+    total = grad[...].astype(f32) + got[...].astype(f32)
     for i, out in enumerate(outs):
 
         @pl.when(step == i)
@@ -53,41 +43,13 @@
     return pl.BlockSpec(shape, lambda *_: (0,) * len(shape))
 
 
-def stack_roots(left, right):
-    nz, per, piece, block = left.shape
-    half = nz // 2
-    return pl.pallas_call(
-        stack_kernel,
-        grid=(2,),
-        in_specs=[pl.BlockSpec((half, per, piece, block), lambda i: (i, 0, 0, 0))] * 2,
-        out_specs=pl.BlockSpec((half, 2, per, piece, block), lambda i: (i, 0, 0, 0, 0)),
-        out_shape=jax.ShapeDtypeStruct((nz, 2, per, piece, block), bf16),
-        cost_estimate=pl.CostEstimate(flops=0, bytes_accessed=8 * left.size, transcendentals=0),
-        compiler_params=params,
-        name="stack_roots",
-    )(left, right)
-
-
 def sum_dp(grad, table, nblocks, piece, block):
     nx = lax.axis_size("x")
     core = lax.axis_index("core")
     x = lax.axis_index("x")
     rows, cols = grad.shape
     band = cols // (2 * nx)
-    other = pl.pallas_call(
-        take_kernel,
-        grid_spec=pltpu.PrefetchScalarGridSpec(
-            num_scalar_prefetch=1,
-            grid=(nx,),
-            in_specs=[pl.BlockSpec((rows, band), lambda i, s: (0, 2 * i + s[0]))],
-            out_specs=pl.BlockSpec((1, rows, band), lambda i, s: (i, 0, 0)),
-        ),
-        out_shape=jax.ShapeDtypeStruct((nx, rows, band), bf16),
-        cost_estimate=pl.CostEstimate(flops=0, bytes_accessed=2 * rows * cols, transcendentals=0),
-        compiler_params=params,
-        name="other_core_bands",
-    )((1 - core).astype(jnp.int32).reshape(1), grad)
-    got = lax.ppermute(other, "core", [(0, 1), (1, 0)])
+    got = lax.ppermute(grad, "core", [(0, 1), (1, 0)])
 
     order = (2, 1, 3, 0)
     owners = jnp.stack([(x + by) % nx for by in order]).astype(jnp.int32)
@@ -100,7 +62,7 @@
             grid=(nx,),
             in_specs=[
                 pl.BlockSpec((rows, band), lambda i, s: (0, s[nx + i])),
-                pl.BlockSpec((1, rows, band), lambda i, s: (s[i], 0, 0)),
+                pl.BlockSpec((rows, band), lambda i, s: (0, s[nx + i])),
             ],
             out_specs=[piece_spec] * nx,
         ),
@@ -211,7 +173,7 @@
         cost_estimate=pl.CostEstimate(
             flops=4 * per * block**3, bytes_accessed=24 * per * block * block, transcendentals=0
         ),
-        compiler_params=wide,
+        compiler_params=params,
         name="products",
     )(y.astype(jnp.int32).reshape(1), *g_parts, roots, right_root)
 
@@ -233,7 +195,7 @@
         far = [shift(value, "y", by) for by in (2, 1, 3)]
         return [value, far[1], far[0], far[2]]
 
-    roots = to_owner(stack_roots(left_root[0].reshape(by_owner), right_root[0].reshape(by_owner)))
+    roots = to_owner(jnp.stack([left_root[0].reshape(by_owner), right_root[0].reshape(by_owner)], 1))
     placed = sum_dp(grad_parts[0], table, nblocks, piece, block)
     grads = to_owner(placed.reshape(by_owner))
     right = from_y(roots[:, 1])

time: 151 us -> 146 us (0.967)
  the two profiles are of different devices: /device:TPU:44 before, /device:TPU:42 now
where the time goes in v3:
time: 146 us
  starting transfers between devices  54 us (37%)
  blocking collectives  48 us (33%)
  waiting for transfers between devices  32 us (22%)
  Pallas kernels  8.35 us (6%)
  other arithmetic  2.22 us (2%)
    all_to_all x1, blocking collectives, local(): back = lax.all_to_all(back, 'z', 0, 0, tiled=True)  48 us
    ppermute x9, starting transfers between devices, shift(): return lax.ppermute(value, axis, [(i, (i + by) % n) for i in range(n)])  30.6 us
    all_to_all x2, starting transfers between devices, to_owner(): return lax.all_to_all(value, 'z', 0, 0, tiled=True)  21.4 us
    all_to_all x2, waiting for transfers between devices, to_owner(): return lax.all_to_all(value, 'z', 0, 0, tiled=True)  16.2 us
    ppermute x9, waiting for transfers between devices, shift(): return lax.ppermute(value, axis, [(i, (i + by) % n) for i in range(n)])  15.8 us
    pallas_call x1, Pallas kernels, sum_dp(): pl.pallas_call(add_kernel, grid_spec=pltpu.PrefetchScalarGridSpec(num_sca...  3.01 us
  transfers between devices with their start and end apart: 12, of which 6 were waited for; matrix products, arithmetic and copies ran while one was open for 2% of the time, Pallas kernels for 3%

profile of v3, /device:TPU:42, one launch (start us, length us, event | category | flops | bytes accessed | tf_op | source)
XLA Modules:
  0.0 145.8 jit_solution(5542318907982620023)
XLA Ops:
  0.6 2.1 %collective-permute-start = (bf16[64,16384]{1,0:T(8,128)(2,1)}, bf16[64,16384]{1,0:T(8,128)(2,1)}, u32[]{:S(2)}, u32[]{:S(2)}) collective-permute-start(bf16[64,16384]{1,0:T(8,128)(2,1)} %bitcast.35), channel_id=1, source_target_pairs={{0,64},{64,0},{1,65},{65,1},{2,66},{66,2},{3,67},{67,3},{4,68},{68... | collective-permute-start | bytes 6291464 | tf_op jit(solution)/shard_map/ppermute | solution.py:52
  2.7 1.9 %pad_maximum_fusion = bf16[16,2,2,8,512]{4,3,2,1,0:T(8,128)(2,1)} fusion(bf16[16,1,2,8,512]{4,3,2,1,0:T(8,128)(2,1)} %bitcast.42, bf16[16,1,2,8,512]{4,3,2,1,0:T(8,128)(2,1)} %bitcast.43), kind=kLoop, calls=%fused_computation.1 | loop fusion | flops 262144 | bytes 1048576 | tf_op jit(solution)/shard_map/stack | solution.py:198
  4.6 15.2 %all-to-all-start.1 = ((bf16[16,2,2,8,512]{4,3,2,1,0:T(8,128)(2,1)}), bf16[16,2,2,8,512]{4,3,2,1,0:T(8,128)(2,1)S(1)}, u32[]{:S(2)}, u32[]{:S(2)}) async-start(bf16[16,2,2,8,512]{4,3,2,1,0:T(8,128)(2,1)} %pad_maximum_fusion), calls=%async_computation.1 | async-start | bytes 1048576 | tf_op jit(solution)/shard_map/all_to_all | solution.py:192
  20.0 3.0 %add_cores.1 = (f32[64,2048]{1,0:T(8,128)S(1)}, bf16[64,2048]{1,0:T(8,128)(2,1)S(1)}, bf16[64,2048]{1,0:T(8,128)(2,1)S(1)}, bf16[64,2048]{1,0:T(8,128)(2,1)S(1)}) custom-call(s32[8]{0:T(128)S(1)} %concatenate.4.where, bf16[64,16384]{1,0:T(8,128)(2,1)S(1)} %bitcast.36, bf16[64,16384]{1,0:T(8,128)(2,1)} %collective-permute-done.got), custom_call_target="tpu_custom_call" | custom-call | flops 524288 | bytes 4194304 | tf_op jit(solution)/shard_map/add_cores/pallas_call | solution.py:58
  23.0 4.0 %collective-permute-start.1 = (bf16[64,2048]{1,0:T(8,128)(2,1)S(1)}, bf16[64,2048]{1,0:T(8,128)(2,1)S(1)}, u32[]{:S(2)}, u32[]{:S(2)}) collective-permute-start(bf16[64,2048]{1,0:T(8,128)(2,1)S(1)} %get-tuple-element.11), channel_id=1, source_target_pairs={{0,256},{128,384},{256,0},{384,128},{1,257},{129,385},{257,1},{385... | collective-permute-start | bytes 786440 | tf_op jit(solution)/shard_map/ppermute | solution.py:16
  27.0 1.9 %collective-permute-start.2 = (bf16[64,2048]{1,0:T(8,128)(2,1)S(1)}, bf16[64,2048]{1,0:T(8,128)(2,1)S(1)}, u32[]{:S(2)}, u32[]{:S(2)}) collective-permute-start(bf16[64,2048]{1,0:T(8,128)(2,1)S(1)} %get-tuple-element.12), channel_id=1, source_target_pairs={{0,128},{128,256},{256,384},{384,0},{1,129},{129,257},{257,385},{3... | collective-permute-start | bytes 786440 | tf_op jit(solution)/shard_map/ppermute | solution.py:16
  28.9 3.9 %collective-permute-start.3 = (bf16[64,2048]{1,0:T(8,128)(2,1)S(1)}, bf16[64,2048]{1,0:T(8,128)(2,1)S(1)}, u32[]{:S(2)}, u32[]{:S(2)}) collective-permute-start(bf16[64,2048]{1,0:T(8,128)(2,1)S(1)} %get-tuple-element.13), channel_id=1, source_target_pairs={{0,384},{128,0},{256,128},{384,256},{1,385},{129,1},{257,129},{385... | collective-permute-start | bytes 786440 | tf_op jit(solution)/shard_map/ppermute | solution.py:16
  32.9 1.8 %collective-permute-done.1.first = bf16[64,2048]{1,0:T(8,128)(2,1)S(1)} collective-permute-done((bf16[64,2048]{1,0:T(8,128)(2,1)S(1)}, bf16[64,2048]{1,0:T(8,128)(2,1)S(1)}, u32[]{:S(2)}, u32[]{:S(2)}) %collective-permute-start.1) | collective-permute-done | bytes 262176 | tf_op jit(solution)/shard_map/ppermute | solution.py:16
  34.6 5.6 %collective-permute-done.2.second = bf16[64,2048]{1,0:T(8,128)(2,1)S(1)} collective-permute-done((bf16[64,2048]{1,0:T(8,128)(2,1)S(1)}, bf16[64,2048]{1,0:T(8,128)(2,1)S(1)}, u32[]{:S(2)}, u32[]{:S(2)}) %collective-permute-start.2) | collective-permute-done | bytes 262176 | tf_op jit(solution)/shard_map/ppermute | solution.py:16
  40.2 1.4 total_in_slots.1
  41.6 8.1 %all-to-all-done.1.refs_4_ = bf16[16,2,2,8,512]{4,3,2,1,0:T(8,128)(2,1)S(1)} async-done(((bf16[16,2,2,8,512]{4,3,2,1,0:T(8,128)(2,1)}), bf16[16,2,2,8,512]{4,3,2,1,0:T(8,128)(2,1)S(1)}, u32[]{:S(2)}, u32[]{:S(2)}) %all-to-all-start.1) | async-done | bytes 524320 | tf_op jit(solution)/shard_map/all_to_all | solution.py:192
  49.7 6.2 %all-to-all-start = ((bf16[16,2,8,512]{3,2,1,0:T(8,128)(2,1)}), bf16[16,2,8,512]{3,2,1,0:T(8,128)(2,1)S(1)}, u32[]{:S(2)}, u32[]{:S(2)}) async-start(bf16[16,2,8,512]{3,2,1,0:T(8,128)(2,1)} %bitcast.7), calls=%async_computation | async-start | bytes 524288 | tf_op jit(solution)/shard_map/all_to_all | solution.py:192
  55.9 4.2 %collective-permute-start.8 = (bf16[16,2,8,512]{3,2,1,0:T(8,128)(2,1)S(1)}, bf16[16,2,8,512]{3,2,1,0:T(8,128)(2,1)S(1)}, u32[]{:S(2)}, u32[]{:S(2)}) collective-permute-start(bf16[16,2,8,512]{3,2,1,0:T(8,128)(2,1)S(1)} %slice_bitcast_fusion), channel_id=1, source_target_pairs={{0,2},{1,3},{2,0},{3,1},{4,6},{5,7},{6,4},{7,5},{8,10},{9,11},{10,... | collective-permute-start | bytes 786440 | tf_op jit(solution)/shard_map/ppermute | solution.py:16
  60.1 3.3 %collective-permute-start.9 = (bf16[16,2,8,512]{3,2,1,0:T(8,128)(2,1)S(1)}, bf16[16,2,8,512]{3,2,1,0:T(8,128)(2,1)S(1)}, u32[]{:S(2)}, u32[]{:S(2)}) collective-permute-start(bf16[16,2,8,512]{3,2,1,0:T(8,128)(2,1)S(1)} %slice_bitcast_fusion), channel_id=1, source_target_pairs={{0,3},{1,0},{2,1},{3,2},{4,7},{5,4},{6,5},{7,6},{8,11},{9,8},{10,9... | collective-permute-start | bytes 786440 | tf_op jit(solution)/shard_map/ppermute | solution.py:16
  63.3 2.6 %collective-permute-start.7 = (bf16[16,2,8,512]{3,2,1,0:T(8,128)(2,1)S(1)}, bf16[16,2,8,512]{3,2,1,0:T(8,128)(2,1)S(1)}, u32[]{:S(2)}, u32[]{:S(2)}) collective-permute-start(bf16[16,2,8,512]{3,2,1,0:T(8,128)(2,1)S(1)} %slice_bitcast_fusion), channel_id=1, source_target_pairs={{0,1},{1,2},{2,3},{3,0},{4,5},{5,6},{6,7},{7,4},{8,9},{9,10},{10,1... | collective-permute-start | bytes 786440 | tf_op jit(solution)/shard_map/ppermute | solution.py:16
  66.0 8.1 %all-to-all-done.refs_0_ = bf16[16,2,8,512]{3,2,1,0:T(8,128)(2,1)S(1)} async-done(((bf16[16,2,8,512]{3,2,1,0:T(8,128)(2,1)}), bf16[16,2,8,512]{3,2,1,0:T(8,128)(2,1)S(1)}, u32[]{:S(2)}, u32[]{:S(2)}) %all-to-all-start) | async-done | bytes 262176 | tf_op jit(solution)/shard_map/all_to_all | solution.py:192
  74.1 3.5 %collective-permute-start.4 = (bf16[16,2,8,512]{3,2,1,0:T(8,128)(2,1)S(1)}, bf16[16,2,8,512]{3,2,1,0:T(8,128)(2,1)S(1)}, u32[]{:S(2)}, u32[]{:S(2)}) collective-permute-start(bf16[16,2,8,512]{3,2,1,0:T(8,128)(2,1)S(1)} %all-to-all-done.refs_0_), channel_id=1, source_target_pairs={{0,1},{1,2},{2,3},{3,0},{4,5},{5,6},{6,7},{7,4},{8,9},{9,10},{10,1... | collective-permute-start | bytes 786440 | tf_op jit(solution)/shard_map/ppermute | solution.py:16
  77.6 2.8 %collective-permute-start.5 = (bf16[16,2,8,512]{3,2,1,0:T(8,128)(2,1)S(1)}, bf16[16,2,8,512]{3,2,1,0:T(8,128)(2,1)S(1)}, u32[]{:S(2)}, u32[]{:S(2)}) collective-permute-start(bf16[16,2,8,512]{3,2,1,0:T(8,128)(2,1)S(1)} %all-to-all-done.refs_0_), channel_id=1, source_target_pairs={{0,2},{1,3},{2,0},{3,1},{4,6},{5,7},{6,4},{7,5},{8,10},{9,11},{10,... | collective-permute-start | bytes 786440 | tf_op jit(solution)/shard_map/ppermute | solution.py:16
  80.5 4.3 %collective-permute-start.6 = (bf16[16,2,8,512]{3,2,1,0:T(8,128)(2,1)S(1)}, bf16[16,2,8,512]{3,2,1,0:T(8,128)(2,1)S(1)}, u32[]{:S(2)}, u32[]{:S(2)}) collective-permute-start(bf16[16,2,8,512]{3,2,1,0:T(8,128)(2,1)S(1)} %all-to-all-done.refs_0_), channel_id=1, source_target_pairs={{0,3},{1,0},{2,1},{3,2},{4,7},{5,4},{6,5},{7,6},{8,11},{9,8},{10,9... | collective-permute-start | bytes 786440 | tf_op jit(solution)/shard_map/ppermute | solution.py:16
  85.3 5.1 %collective-permute-done.5.refs_2_ = bf16[16,2,8,512]{3,2,1,0:T(8,128)(2,1)S(1)} collective-permute-done((bf16[16,2,8,512]{3,2,1,0:T(8,128)(2,1)S(1)}, bf16[16,2,8,512]{3,2,1,0:T(8,128)(2,1)S(1)}, u32[]{:S(2)}, u32[]{:S(2)}) %collective-permute-start.5) | collective-permute-done | bytes 262176 | tf_op jit(solution)/shard_map/ppermute | solution.py:16
  90.3 3.4 %collective-permute-done.6.refs_3_ = bf16[16,2,8,512]{3,2,1,0:T(8,128)(2,1)S(1)} collective-permute-done((bf16[16,2,8,512]{3,2,1,0:T(8,128)(2,1)S(1)}, bf16[16,2,8,512]{3,2,1,0:T(8,128)(2,1)S(1)}, u32[]{:S(2)}, u32[]{:S(2)}) %collective-permute-start.6) | collective-permute-done | bytes 262176 | tf_op jit(solution)/shard_map/ppermute | solution.py:16
  93.7 2.3 %products.1 = bf16[16,3,2,8,512]{4,3,2,1,0:T(8,128)(2,1)S(1)} custom-call(s32[1]{0:T(128)} %bitcast.1.where, bf16[16,2,8,512]{3,2,1,0:T(8,128)(2,1)S(1)} %all-to-all-done.refs_0_, bf16[16,2,8,512]{3,2,1,0:T(8,128)(2,1)S(1)} %collective-permute-done.4.refs_1_, bf16[16,2,8,512]{3,2,1,0:T(8,128)(2,1)S(1)} %collective-permute-done.5.refs_2_, ...), custom_call_target="tpu_custom_call" | custom-call | flops 1073741824 | bytes 12582912 | tf_op jit(solution)/shard_map/products/pallas_call | solution.py:163
  96.0 48.0 %all_to_all.15.back = bf16[16,3,2,8,512]{4,3,2,1,0:T(8,128)(2,1)S(1)} all-to-all(bf16[16,3,2,8,512]{4,3,2,1,0:T(8,128)(2,1)S(1)} %products.1), channel_id=1, replica_groups=mesh['x'=4,'core'=2,'z'=16,'y'=4] {'z'}, dimensions={0} | all-to-all | bytes 1572864 | tf_op jit(solution)/shard_map/all_to_all | solution.py:205
  144.1 1.7 %settle.1 = (bf16[32,8,512]{2,1,0:T(8,128)(2,1)}, bf16[32,8,512]{2,1,0:T(8,128)(2,1)}, bf16[64,2048]{1,0:T(8,128)(2,1)}) custom-call(s32[32]{0:T(128)S(1)} %bitcast.41, bf16[16,3,2,8,512]{4,3,2,1,0:T(8,128)(2,1)S(1)} %all_to_all.15.back, bf16[32,8,512]{2,1,0:T(8,128)(2,1)S(1)} %bitcast.38, bf16[32,8,512]{2,1,0:T(8,128)(2,1)S(1)} %bitcast.39), custom_call_target="tpu_custom_call" | custom-call | flops 524288 | bytes 2097152 | tf_op jit(solution)/shard_map/settle/pallas_call | solution.py:113
  (20 shorter events, 0.6 us)
Async XLA Ops:
  0.6 19.3 %copy-start = (bf16[1,64,16384]{2,1,0:T(8,128)(2,1)S(1)}, bf16[1,64,16384]{2,1,0:T(8,128)(2,1)}, u32[]{:S(2)}) copy-start(bf16[1,64,16384]{2,1,0:T(8,128)(2,1)} %param.6) | copy-start | bytes 6291460
  0.6 19.3 %collective-permute-start = (bf16[64,16384]{1,0:T(8,128)(2,1)}, bf16[64,16384]{1,0:T(8,128)(2,1)}, u32[]{:S(2)}, u32[]{:S(2)}) collective-permute-start(bf16[64,16384]{1,0:T(8,128)(2,1)} %bitcast.35), channel_id=1, source_target_pairs={{0,64},{64,0},{1,65},{65,1},{2,66},{66,2},{3,67},{67,3},{4,68},{68... | collective-permute-start | bytes 6291464 | tf_op jit(solution)/shard_map/ppermute | solution.py:52
  4.6 45.1 %all-to-all-start.1 = ((bf16[16,2,2,8,512]{4,3,2,1,0:T(8,128)(2,1)}), bf16[16,2,2,8,512]{4,3,2,1,0:T(8,128)(2,1)S(1)}, u32[]{:S(2)}, u32[]{:S(2)}) async-start(bf16[16,2,2,8,512]{4,3,2,1,0:T(8,128)(2,1)} %pad_maximum_fusion), calls=%async_computation.1 | async-start | bytes 1048576 | tf_op jit(solution)/shard_map/all_to_all | solution.py:192
  20.0 20.3 %copy-start.3 = (s32[1,32]{1,0:T(1,128)S(1)}, s32[1,32]{1,0:T(1,128)}, u32[]{:S(2)}) copy-start(s32[1,32]{1,0:T(1,128)} %param.7) | copy-start | bytes 388
  23.0 11.7 %collective-permute-start.1 = (bf16[64,2048]{1,0:T(8,128)(2,1)S(1)}, bf16[64,2048]{1,0:T(8,128)(2,1)S(1)}, u32[]{:S(2)}, u32[]{:S(2)}) collective-permute-start(bf16[64,2048]{1,0:T(8,128)(2,1)S(1)} %get-tuple-element.11), channel_id=1, source_target_pairs={{0,256},{128,384},{256,0},{384,128},{1,257},{129,385},{257,1},{385... | collective-permute-start | bytes 786440 | tf_op jit(solution)/shard_map/ppermute | solution.py:16
  27.0 13.2 %collective-permute-start.2 = (bf16[64,2048]{1,0:T(8,128)(2,1)S(1)}, bf16[64,2048]{1,0:T(8,128)(2,1)S(1)}, u32[]{:S(2)}, u32[]{:S(2)}) collective-permute-start(bf16[64,2048]{1,0:T(8,128)(2,1)S(1)} %get-tuple-element.12), channel_id=1, source_target_pairs={{0,128},{128,256},{256,384},{384,0},{1,129},{129,257},{257,385},{3... | collective-permute-start | bytes 786440 | tf_op jit(solution)/shard_map/ppermute | solution.py:16
  28.9 11.3 %collective-permute-start.3 = (bf16[64,2048]{1,0:T(8,128)(2,1)S(1)}, bf16[64,2048]{1,0:T(8,128)(2,1)S(1)}, u32[]{:S(2)}, u32[]{:S(2)}) collective-permute-start(bf16[64,2048]{1,0:T(8,128)(2,1)S(1)} %get-tuple-element.13), channel_id=1, source_target_pairs={{0,384},{128,0},{256,128},{384,256},{1,385},{129,1},{257,129},{385... | collective-permute-start | bytes 786440 | tf_op jit(solution)/shard_map/ppermute | solution.py:16
  49.7 24.5 %all-to-all-start = ((bf16[16,2,8,512]{3,2,1,0:T(8,128)(2,1)}), bf16[16,2,8,512]{3,2,1,0:T(8,128)(2,1)S(1)}, u32[]{:S(2)}, u32[]{:S(2)}) async-start(bf16[16,2,8,512]{3,2,1,0:T(8,128)(2,1)} %bitcast.7), calls=%async_computation | async-start | bytes 524288 | tf_op jit(solution)/shard_map/all_to_all | solution.py:192
  55.9 24.6 %collective-permute-start.8 = (bf16[16,2,8,512]{3,2,1,0:T(8,128)(2,1)S(1)}, bf16[16,2,8,512]{3,2,1,0:T(8,128)(2,1)S(1)}, u32[]{:S(2)}, u32[]{:S(2)}) collective-permute-start(bf16[16,2,8,512]{3,2,1,0:T(8,128)(2,1)S(1)} %slice_bitcast_fusion), channel_id=1, source_target_pairs={{0,2},{1,3},{2,0},{3,1},{4,6},{5,7},{6,4},{7,5},{8,10},{9,11},{10,... | collective-permute-start | bytes 786440 | tf_op jit(solution)/shard_map/ppermute | solution.py:16
  60.1 24.7 %collective-permute-start.9 = (bf16[16,2,8,512]{3,2,1,0:T(8,128)(2,1)S(1)}, bf16[16,2,8,512]{3,2,1,0:T(8,128)(2,1)S(1)}, u32[]{:S(2)}, u32[]{:S(2)}) collective-permute-start(bf16[16,2,8,512]{3,2,1,0:T(8,128)(2,1)S(1)} %slice_bitcast_fusion), channel_id=1, source_target_pairs={{0,3},{1,0},{2,1},{3,2},{4,7},{5,4},{6,5},{7,6},{8,11},{9,8},{10,9... | collective-permute-start | bytes 786440 | tf_op jit(solution)/shard_map/ppermute | solution.py:16
  63.3 21.5 %collective-permute-start.7 = (bf16[16,2,8,512]{3,2,1,0:T(8,128)(2,1)S(1)}, bf16[16,2,8,512]{3,2,1,0:T(8,128)(2,1)S(1)}, u32[]{:S(2)}, u32[]{:S(2)}) collective-permute-start(bf16[16,2,8,512]{3,2,1,0:T(8,128)(2,1)S(1)} %slice_bitcast_fusion), channel_id=1, source_target_pairs={{0,1},{1,2},{2,3},{3,0},{4,5},{5,6},{6,7},{7,4},{8,9},{9,10},{10,1... | collective-permute-start | bytes 786440 | tf_op jit(solution)/shard_map/ppermute | solution.py:16
  74.1 11.1 %collective-permute-start.4 = (bf16[16,2,8,512]{3,2,1,0:T(8,128)(2,1)S(1)}, bf16[16,2,8,512]{3,2,1,0:T(8,128)(2,1)S(1)}, u32[]{:S(2)}, u32[]{:S(2)}) collective-permute-start(bf16[16,2,8,512]{3,2,1,0:T(8,128)(2,1)S(1)} %all-to-all-done.refs_0_), channel_id=1, source_target_pairs={{0,1},{1,2},{2,3},{3,0},{4,5},{5,6},{6,7},{7,4},{8,9},{9,10},{10,1... | collective-permute-start | bytes 786440 | tf_op jit(solution)/shard_map/ppermute | solution.py:16
  77.6 12.7 %collective-permute-start.5 = (bf16[16,2,8,512]{3,2,1,0:T(8,128)(2,1)S(1)}, bf16[16,2,8,512]{3,2,1,0:T(8,128)(2,1)S(1)}, u32[]{:S(2)}, u32[]{:S(2)}) collective-permute-start(bf16[16,2,8,512]{3,2,1,0:T(8,128)(2,1)S(1)} %all-to-all-done.refs_0_), channel_id=1, source_target_pairs={{0,2},{1,3},{2,0},{3,1},{4,6},{5,7},{6,4},{7,5},{8,10},{9,11},{10,... | collective-permute-start | bytes 786440 | tf_op jit(solution)/shard_map/ppermute | solution.py:16
  80.5 13.2 %collective-permute-start.6 = (bf16[16,2,8,512]{3,2,1,0:T(8,128)(2,1)S(1)}, bf16[16,2,8,512]{3,2,1,0:T(8,128)(2,1)S(1)}, u32[]{:S(2)}, u32[]{:S(2)}) collective-permute-start(bf16[16,2,8,512]{3,2,1,0:T(8,128)(2,1)S(1)} %all-to-all-done.refs_0_), channel_id=1, source_target_pairs={{0,3},{1,0},{2,1},{3,2},{4,7},{5,4},{6,5},{7,6},{8,11},{9,8},{10,9... | collective-permute-start | bytes 786440 | tf_op jit(solution)/shard_map/ppermute | solution.py:16
  93.7 50.3 %copy-start.1 = (bf16[1,32,8,512]{3,2,1,0:T(8,128)(2,1)S(1)}, bf16[1,32,8,512]{3,2,1,0:T(8,128)(2,1)}, u32[]{:S(2)}) copy-start(bf16[1,32,8,512]{3,2,1,0:T(8,128)(2,1)} %param.8) | copy-start | bytes 786436
  93.7 50.3 %copy-start.2 = (bf16[1,32,8,512]{3,2,1,0:T(8,128)(2,1)S(1)}, bf16[1,32,8,512]{3,2,1,0:T(8,128)(2,1)}, u32[]{:S(2)}) copy-start(bf16[1,32,8,512]{3,2,1,0:T(8,128)(2,1)} %param.9) | copy-start | bytes 786436

commit v4 on v3

--- a/solution.py
+++ b/solution.py
@@ -96,7 +96,7 @@
     ncb = update.shape[1] // block
     for arr, stat, new in ((0, left, left_new), (1, right, right_new)):
         gram = back[:, arr].astype(f32).reshape(nz * per, piece, block)
-        new[...] = (decay * stat[...].astype(f32) + gram).astype(bf16)
+        new[...] = (stat[...] + gram).astype(bf16)
     for rb in range(0, update.shape[0] // piece, 2):
         for cb in range(ncb):
             pair = []
@@ -202,7 +202,9 @@
     right = jnp.stack([lax.select_n((y - owner) % ny, *right) for owner in range(ny)])
     right = right.transpose(2, 1, 0, 3, 4).reshape(per, block, block)
     back = products(from_y(grads), roots, right, y)
+    back, left_stat, right_stat = lax.optimization_barrier((back, left_stat, right_stat))
     back = lax.all_to_all(back, "z", 0, 0, tiled=True)
+    left_stat, right_stat = (decay * left_stat.astype(f32), decay * right_stat.astype(f32))
     left_new, right_new, update = settle(
         table, back, left_stat[0], right_stat[0], rows_dev, ncb * block
     )

time: 146 us -> 145 us (level)
  blocking collectives: 48 us -> 0 us
  waiting for transfers between devices: 32 us -> 71.5 us
  starting transfers between devices: 54 us -> 60.7 us
    all_to_all x1 -> x0, blocking collectives: 48 us -> none  [local(): back = lax.all_to_all(back, 'z', 0, 0, tiled=True)]
    all_to_all x0 -> x1, waiting for transfers between devices: none -> 39.5 us  [local(): back = lax.all_to_all(back, 'z', 0, 0, tiled=True)]
    all_to_all x0 -> x1, starting transfers between devices: none -> 6.71 us  [local(): back = lax.all_to_all(back, 'z', 0, 0, tiled=True)]
  transfers between devices with their start and end apart: 12 -> 13, of which waited for: 6 -> 7; matrix products, arithmetic and copies ran while one was open for 2% -> 2% of each run, Pallas kernels for 3% -> 3%
where the time goes in v4:
time: 145 us
  waiting for transfers between devices  71.5 us (49%)
  starting transfers between devices  60.7 us (42%)
  Pallas kernels  9 us (6%)
  other arithmetic  2.35 us (2%)
    all_to_all x1, waiting for transfers between devices, local(): back = lax.all_to_all(back, 'z', 0, 0, tiled=True)  39.5 us
    ppermute x9, starting transfers between devices, shift(): return lax.ppermute(value, axis, [(i, (i + by) % n) for i in range(n)])  30.6 us
    all_to_all x2, starting transfers between devices, to_owner(): return lax.all_to_all(value, 'z', 0, 0, tiled=True)  21.4 us
    all_to_all x2, waiting for transfers between devices, to_owner(): return lax.all_to_all(value, 'z', 0, 0, tiled=True)  16.2 us
    ppermute x9, waiting for transfers between devices, shift(): return lax.ppermute(value, axis, [(i, (i + by) % n) for i in range(n)])  15.8 us
    all_to_all x1, starting transfers between devices, local(): back = lax.all_to_all(back, 'z', 0, 0, tiled=True)  6.71 us
    pallas_call x1, Pallas kernels, sum_dp(): pl.pallas_call(add_kernel, grid_spec=pltpu.PrefetchScalarGridSpec(num_sca...  3.01 us
    pallas_call x1, Pallas kernels, products(): pl.pallas_call(products_kernel, grid_spec=pltpu.PrefetchScalarGridSpec(nu...  2.97 us
  transfers between devices with their start and end apart: 13, of which 7 were waited for; matrix products, arithmetic and copies ran while one was open for 2% of the time, Pallas kernels for 3%

profile of v4, /device:TPU:42, one launch (start us, length us, event | category | flops | bytes accessed | tf_op | source)
XLA Modules:
  0.0 144.7 jit_solution(1713900526008004412)
XLA Ops:
  0.6 2.1 %collective-permute-start = (bf16[64,16384]{1,0:T(8,128)(2,1)}, bf16[64,16384]{1,0:T(8,128)(2,1)}, u32[]{:S(2)}, u32[]{:S(2)}) collective-permute-start(bf16[64,16384]{1,0:T(8,128)(2,1)} %bitcast.37), channel_id=1, source_target_pairs={{0,64},{64,0},{1,65},{65,1},{2,66},{66,2},{3,67},{67,3},{4,68},{68... | collective-permute-start | bytes 6291464 | tf_op jit(solution)/shard_map/ppermute | solution.py:52
  2.7 1.9 %pad_maximum_fusion = bf16[16,2,2,8,512]{4,3,2,1,0:T(8,128)(2,1)} fusion(bf16[16,1,2,8,512]{4,3,2,1,0:T(8,128)(2,1)} %bitcast.42, bf16[16,1,2,8,512]{4,3,2,1,0:T(8,128)(2,1)} %bitcast.43), kind=kLoop, calls=%fused_computation.1 | loop fusion | flops 262144 | bytes 1048576 | tf_op jit(solution)/shard_map/stack | solution.py:198
  4.6 15.2 %all-to-all-start.1 = ((bf16[16,2,2,8,512]{4,3,2,1,0:T(8,128)(2,1)}), bf16[16,2,2,8,512]{4,3,2,1,0:T(8,128)(2,1)S(1)}, u32[]{:S(2)}, u32[]{:S(2)}) async-start(bf16[16,2,2,8,512]{4,3,2,1,0:T(8,128)(2,1)} %pad_maximum_fusion), calls=%async_computation.1 | async-start | bytes 1048576 | tf_op jit(solution)/shard_map/all_to_all | solution.py:192
  20.0 3.0 %add_cores.1 = (f32[64,2048]{1,0:T(8,128)S(1)}, bf16[64,2048]{1,0:T(8,128)(2,1)S(1)}, bf16[64,2048]{1,0:T(8,128)(2,1)S(1)}, bf16[64,2048]{1,0:T(8,128)(2,1)S(1)}) custom-call(s32[8]{0:T(128)S(1)} %concatenate.4.where, bf16[64,16384]{1,0:T(8,128)(2,1)S(1)} %bitcast.38, bf16[64,16384]{1,0:T(8,128)(2,1)} %collective-permute-done.got), custom_call_target="tpu_custom_call" | custom-call | flops 524288 | bytes 4194304 | tf_op jit(solution)/shard_map/add_cores/pallas_call | solution.py:58
  23.0 4.0 %collective-permute-start.1 = (bf16[64,2048]{1,0:T(8,128)(2,1)S(1)}, bf16[64,2048]{1,0:T(8,128)(2,1)S(1)}, u32[]{:S(2)}, u32[]{:S(2)}) collective-permute-start(bf16[64,2048]{1,0:T(8,128)(2,1)S(1)} %get-tuple-element.14), channel_id=1, source_target_pairs={{0,256},{128,384},{256,0},{384,128},{1,257},{129,385},{257,1},{385... | collective-permute-start | bytes 786440 | tf_op jit(solution)/shard_map/ppermute | solution.py:16
  27.0 1.9 %collective-permute-start.2 = (bf16[64,2048]{1,0:T(8,128)(2,1)S(1)}, bf16[64,2048]{1,0:T(8,128)(2,1)S(1)}, u32[]{:S(2)}, u32[]{:S(2)}) collective-permute-start(bf16[64,2048]{1,0:T(8,128)(2,1)S(1)} %get-tuple-element.15), channel_id=1, source_target_pairs={{0,128},{128,256},{256,384},{384,0},{1,129},{129,257},{257,385},{3... | collective-permute-start | bytes 786440 | tf_op jit(solution)/shard_map/ppermute | solution.py:16
  28.9 3.9 %collective-permute-start.3 = (bf16[64,2048]{1,0:T(8,128)(2,1)S(1)}, bf16[64,2048]{1,0:T(8,128)(2,1)S(1)}, u32[]{:S(2)}, u32[]{:S(2)}) collective-permute-start(bf16[64,2048]{1,0:T(8,128)(2,1)S(1)} %get-tuple-element.16), channel_id=1, source_target_pairs={{0,384},{128,0},{256,128},{384,256},{1,385},{129,1},{257,129},{385... | collective-permute-start | bytes 786440 | tf_op jit(solution)/shard_map/ppermute | solution.py:16
  32.9 1.8 %collective-permute-done.1.first = bf16[64,2048]{1,0:T(8,128)(2,1)S(1)} collective-permute-done((bf16[64,2048]{1,0:T(8,128)(2,1)S(1)}, bf16[64,2048]{1,0:T(8,128)(2,1)S(1)}, u32[]{:S(2)}, u32[]{:S(2)}) %collective-permute-start.1) | collective-permute-done | bytes 262176 | tf_op jit(solution)/shard_map/ppermute | solution.py:16
  34.6 5.6 %collective-permute-done.2.second = bf16[64,2048]{1,0:T(8,128)(2,1)S(1)} collective-permute-done((bf16[64,2048]{1,0:T(8,128)(2,1)S(1)}, bf16[64,2048]{1,0:T(8,128)(2,1)S(1)}, u32[]{:S(2)}, u32[]{:S(2)}) %collective-permute-start.2) | collective-permute-done | bytes 262176 | tf_op jit(solution)/shard_map/ppermute | solution.py:16
  41.6 8.1 %all-to-all-done.1.refs_4_ = bf16[16,2,2,8,512]{4,3,2,1,0:T(8,128)(2,1)S(1)} async-done(((bf16[16,2,2,8,512]{4,3,2,1,0:T(8,128)(2,1)}), bf16[16,2,2,8,512]{4,3,2,1,0:T(8,128)(2,1)S(1)}, u32[]{:S(2)}, u32[]{:S(2)}) %all-to-all-start.1) | async-done | bytes 524320 | tf_op jit(solution)/shard_map/all_to_all | solution.py:192
  49.6 6.2 %all-to-all-start = ((bf16[16,2,8,512]{3,2,1,0:T(8,128)(2,1)}), bf16[16,2,8,512]{3,2,1,0:T(8,128)(2,1)S(1)}, u32[]{:S(2)}, u32[]{:S(2)}) async-start(bf16[16,2,8,512]{3,2,1,0:T(8,128)(2,1)} %bitcast.7), calls=%async_computation | async-start | bytes 524288 | tf_op jit(solution)/shard_map/all_to_all | solution.py:192
  55.9 4.2 %collective-permute-start.8 = (bf16[16,2,8,512]{3,2,1,0:T(8,128)(2,1)S(1)}, bf16[16,2,8,512]{3,2,1,0:T(8,128)(2,1)S(1)}, u32[]{:S(2)}, u32[]{:S(2)}) collective-permute-start(bf16[16,2,8,512]{3,2,1,0:T(8,128)(2,1)S(1)} %slice_bitcast_fusion), channel_id=1, source_target_pairs={{0,2},{1,3},{2,0},{3,1},{4,6},{5,7},{6,4},{7,5},{8,10},{9,11},{10,... | collective-permute-start | bytes 786440 | tf_op jit(solution)/shard_map/ppermute | solution.py:16
  60.1 3.3 %collective-permute-start.9 = (bf16[16,2,8,512]{3,2,1,0:T(8,128)(2,1)S(1)}, bf16[16,2,8,512]{3,2,1,0:T(8,128)(2,1)S(1)}, u32[]{:S(2)}, u32[]{:S(2)}) collective-permute-start(bf16[16,2,8,512]{3,2,1,0:T(8,128)(2,1)S(1)} %slice_bitcast_fusion), channel_id=1, source_target_pairs={{0,3},{1,0},{2,1},{3,2},{4,7},{5,4},{6,5},{7,6},{8,11},{9,8},{10,9... | collective-permute-start | bytes 786440 | tf_op jit(solution)/shard_map/ppermute | solution.py:16
  63.3 2.6 %collective-permute-start.7 = (bf16[16,2,8,512]{3,2,1,0:T(8,128)(2,1)S(1)}, bf16[16,2,8,512]{3,2,1,0:T(8,128)(2,1)S(1)}, u32[]{:S(2)}, u32[]{:S(2)}) collective-permute-start(bf16[16,2,8,512]{3,2,1,0:T(8,128)(2,1)S(1)} %slice_bitcast_fusion), channel_id=1, source_target_pairs={{0,1},{1,2},{2,3},{3,0},{4,5},{5,6},{6,7},{7,4},{8,9},{9,10},{10,1... | collective-permute-start | bytes 786440 | tf_op jit(solution)/shard_map/ppermute | solution.py:16
  66.0 8.1 %all-to-all-done.refs_0_ = bf16[16,2,8,512]{3,2,1,0:T(8,128)(2,1)S(1)} async-done(((bf16[16,2,8,512]{3,2,1,0:T(8,128)(2,1)}), bf16[16,2,8,512]{3,2,1,0:T(8,128)(2,1)S(1)}, u32[]{:S(2)}, u32[]{:S(2)}) %all-to-all-start) | async-done | bytes 262176 | tf_op jit(solution)/shard_map/all_to_all | solution.py:192
  74.1 3.5 %collective-permute-start.4 = (bf16[16,2,8,512]{3,2,1,0:T(8,128)(2,1)S(1)}, bf16[16,2,8,512]{3,2,1,0:T(8,128)(2,1)S(1)}, u32[]{:S(2)}, u32[]{:S(2)}) collective-permute-start(bf16[16,2,8,512]{3,2,1,0:T(8,128)(2,1)S(1)} %all-to-all-done.refs_0_), channel_id=1, source_target_pairs={{0,1},{1,2},{2,3},{3,0},{4,5},{5,6},{6,7},{7,4},{8,9},{9,10},{10,1... | collective-permute-start | bytes 786440 | tf_op jit(solution)/shard_map/ppermute | solution.py:16
  77.6 2.8 %collective-permute-start.5 = (bf16[16,2,8,512]{3,2,1,0:T(8,128)(2,1)S(1)}, bf16[16,2,8,512]{3,2,1,0:T(8,128)(2,1)S(1)}, u32[]{:S(2)}, u32[]{:S(2)}) collective-permute-start(bf16[16,2,8,512]{3,2,1,0:T(8,128)(2,1)S(1)} %all-to-all-done.refs_0_), channel_id=1, source_target_pairs={{0,2},{1,3},{2,0},{3,1},{4,6},{5,7},{6,4},{7,5},{8,10},{9,11},{10,... | collective-permute-start | bytes 786440 | tf_op jit(solution)/shard_map/ppermute | solution.py:16
  80.5 4.3 %collective-permute-start.6 = (bf16[16,2,8,512]{3,2,1,0:T(8,128)(2,1)S(1)}, bf16[16,2,8,512]{3,2,1,0:T(8,128)(2,1)S(1)}, u32[]{:S(2)}, u32[]{:S(2)}) collective-permute-start(bf16[16,2,8,512]{3,2,1,0:T(8,128)(2,1)S(1)} %all-to-all-done.refs_0_), channel_id=1, source_target_pairs={{0,3},{1,0},{2,1},{3,2},{4,7},{5,4},{6,5},{7,6},{8,11},{9,8},{10,9... | collective-permute-start | bytes 786440 | tf_op jit(solution)/shard_map/ppermute | solution.py:16
  85.2 5.1 %collective-permute-done.5.refs_2_ = bf16[16,2,8,512]{3,2,1,0:T(8,128)(2,1)S(1)} collective-permute-done((bf16[16,2,8,512]{3,2,1,0:T(8,128)(2,1)S(1)}, bf16[16,2,8,512]{3,2,1,0:T(8,128)(2,1)S(1)}, u32[]{:S(2)}, u32[]{:S(2)}) %collective-permute-start.5) | collective-permute-done | bytes 262176 | tf_op jit(solution)/shard_map/ppermute | solution.py:16
  90.3 3.4 %collective-permute-done.6.refs_3_ = bf16[16,2,8,512]{3,2,1,0:T(8,128)(2,1)S(1)} collective-permute-done((bf16[16,2,8,512]{3,2,1,0:T(8,128)(2,1)S(1)}, bf16[16,2,8,512]{3,2,1,0:T(8,128)(2,1)S(1)}, u32[]{:S(2)}, u32[]{:S(2)}) %collective-permute-start.6) | collective-permute-done | bytes 262176 | tf_op jit(solution)/shard_map/ppermute | solution.py:16
  93.7 3.0 %products.1 = bf16[16,3,2,8,512]{4,3,2,1,0:T(8,128)(2,1)} custom-call(s32[1]{0:T(128)} %bitcast.1.where, bf16[16,2,8,512]{3,2,1,0:T(8,128)(2,1)S(1)} %all-to-all-done.refs_0_, bf16[16,2,8,512]{3,2,1,0:T(8,128)(2,1)S(1)} %collective-permute-done.4.refs_1_, bf16[16,2,8,512]{3,2,1,0:T(8,128)(2,1)S(1)} %collective-permute-done.5.refs_2_, ...), custom_call_target="tpu_custom_call" | custom-call | flops 1073741824 | bytes 12582912 | tf_op jit(solution)/shard_map/products/pallas_call | solution.py:163
  96.7 6.7 %all-to-all-start.2 = ((bf16[16,3,2,8,512]{4,3,2,1,0:T(8,128)(2,1)}), bf16[16,3,2,8,512]{4,3,2,1,0:T(8,128)(2,1)S(1)}, u32[]{:S(2)}, u32[]{:S(2)}) async-start(bf16[16,3,2,8,512]{4,3,2,1,0:T(8,128)(2,1)} %products.1), calls=%async_computation.2 | async-start | bytes 1572864 | tf_op jit(solution)/shard_map/all_to_all | solution.py:206
  103.6 39.5 %all-to-all-done.2.back = bf16[16,3,2,8,512]{4,3,2,1,0:T(8,128)(2,1)S(1)} async-done(((bf16[16,3,2,8,512]{4,3,2,1,0:T(8,128)(2,1)}), bf16[16,3,2,8,512]{4,3,2,1,0:T(8,128)(2,1)S(1)}, u32[]{:S(2)}, u32[]{:S(2)}) %all-to-all-start.2) | async-done | bytes 786464 | tf_op jit(solution)/shard_map/all_to_all | solution.py:206
  143.1 1.6 %settle.1 = (bf16[32,8,512]{2,1,0:T(8,128)(2,1)}, bf16[32,8,512]{2,1,0:T(8,128)(2,1)}, bf16[64,2048]{1,0:T(8,128)(2,1)}) custom-call(s32[32]{0:T(128)S(1)} %bitcast.41, bf16[16,3,2,8,512]{4,3,2,1,0:T(8,128)(2,1)S(1)} %all-to-all-done.2.back, f32[32,8,512]{2,1,0:T(8,128)S(1)} %get-tuple-element.28.left, f32[32,8,512]{2,1,0:T(8,128)S(1)} %get-tuple-element.27.right), custom_call_target="tpu_custom_call" | custom-call | flops 524288 | bytes 2097152 | tf_op jit(solution)/shard_map/settle/pallas_call | solution.py:113
  (22 shorter events, 2.1 us)
Async XLA Ops:
  0.6 19.3 %copy-start = (bf16[1,64,16384]{2,1,0:T(8,128)(2,1)S(1)}, bf16[1,64,16384]{2,1,0:T(8,128)(2,1)}, u32[]{:S(2)}) copy-start(bf16[1,64,16384]{2,1,0:T(8,128)(2,1)} %param.6) | copy-start | bytes 6291460
  0.6 19.3 %collective-permute-start = (bf16[64,16384]{1,0:T(8,128)(2,1)}, bf16[64,16384]{1,0:T(8,128)(2,1)}, u32[]{:S(2)}, u32[]{:S(2)}) collective-permute-start(bf16[64,16384]{1,0:T(8,128)(2,1)} %bitcast.37), channel_id=1, source_target_pairs={{0,64},{64,0},{1,65},{65,1},{2,66},{66,2},{3,67},{67,3},{4,68},{68... | collective-permute-start | bytes 6291464 | tf_op jit(solution)/shard_map/ppermute | solution.py:52
  4.6 45.1 %all-to-all-start.1 = ((bf16[16,2,2,8,512]{4,3,2,1,0:T(8,128)(2,1)}), bf16[16,2,2,8,512]{4,3,2,1,0:T(8,128)(2,1)S(1)}, u32[]{:S(2)}, u32[]{:S(2)}) async-start(bf16[16,2,2,8,512]{4,3,2,1,0:T(8,128)(2,1)} %pad_maximum_fusion), calls=%async_computation.1 | async-start | bytes 1048576 | tf_op jit(solution)/shard_map/all_to_all | solution.py:192
  19.9 20.3 %copy-start.1 = (s32[1,32]{1,0:T(1,128)S(1)}, s32[1,32]{1,0:T(1,128)}, u32[]{:S(2)}) copy-start(s32[1,32]{1,0:T(1,128)} %param.7) | copy-start | bytes 388
  23.0 11.7 %collective-permute-start.1 = (bf16[64,2048]{1,0:T(8,128)(2,1)S(1)}, bf16[64,2048]{1,0:T(8,128)(2,1)S(1)}, u32[]{:S(2)}, u32[]{:S(2)}) collective-permute-start(bf16[64,2048]{1,0:T(8,128)(2,1)S(1)} %get-tuple-element.14), channel_id=1, source_target_pairs={{0,256},{128,384},{256,0},{384,128},{1,257},{129,385},{257,1},{385... | collective-permute-start | bytes 786440 | tf_op jit(solution)/shard_map/ppermute | solution.py:16
  27.0 13.2 %collective-permute-start.2 = (bf16[64,2048]{1,0:T(8,128)(2,1)S(1)}, bf16[64,2048]{1,0:T(8,128)(2,1)S(1)}, u32[]{:S(2)}, u32[]{:S(2)}) collective-permute-start(bf16[64,2048]{1,0:T(8,128)(2,1)S(1)} %get-tuple-element.15), channel_id=1, source_target_pairs={{0,128},{128,256},{256,384},{384,0},{1,129},{129,257},{257,385},{3... | collective-permute-start | bytes 786440 | tf_op jit(solution)/shard_map/ppermute | solution.py:16
  28.9 11.3 %collective-permute-start.3 = (bf16[64,2048]{1,0:T(8,128)(2,1)S(1)}, bf16[64,2048]{1,0:T(8,128)(2,1)S(1)}, u32[]{:S(2)}, u32[]{:S(2)}) collective-permute-start(bf16[64,2048]{1,0:T(8,128)(2,1)S(1)} %get-tuple-element.16), channel_id=1, source_target_pairs={{0,384},{128,0},{256,128},{384,256},{1,385},{129,1},{257,129},{385... | collective-permute-start | bytes 786440 | tf_op jit(solution)/shard_map/ppermute | solution.py:16
  49.6 24.5 %all-to-all-start = ((bf16[16,2,8,512]{3,2,1,0:T(8,128)(2,1)}), bf16[16,2,8,512]{3,2,1,0:T(8,128)(2,1)S(1)}, u32[]{:S(2)}, u32[]{:S(2)}) async-start(bf16[16,2,8,512]{3,2,1,0:T(8,128)(2,1)} %bitcast.7), calls=%async_computation | async-start | bytes 524288 | tf_op jit(solution)/shard_map/all_to_all | solution.py:192
  55.9 24.6 %collective-permute-start.8 = (bf16[16,2,8,512]{3,2,1,0:T(8,128)(2,1)S(1)}, bf16[16,2,8,512]{3,2,1,0:T(8,128)(2,1)S(1)}, u32[]{:S(2)}, u32[]{:S(2)}) collective-permute-start(bf16[16,2,8,512]{3,2,1,0:T(8,128)(2,1)S(1)} %slice_bitcast_fusion), channel_id=1, source_target_pairs={{0,2},{1,3},{2,0},{3,1},{4,6},{5,7},{6,4},{7,5},{8,10},{9,11},{10,... | collective-permute-start | bytes 786440 | tf_op jit(solution)/shard_map/ppermute | solution.py:16
  60.1 24.7 %collective-permute-start.9 = (bf16[16,2,8,512]{3,2,1,0:T(8,128)(2,1)S(1)}, bf16[16,2,8,512]{3,2,1,0:T(8,128)(2,1)S(1)}, u32[]{:S(2)}, u32[]{:S(2)}) collective-permute-start(bf16[16,2,8,512]{3,2,1,0:T(8,128)(2,1)S(1)} %slice_bitcast_fusion), channel_id=1, source_target_pairs={{0,3},{1,0},{2,1},{3,2},{4,7},{5,4},{6,5},{7,6},{8,11},{9,8},{10,9... | collective-permute-start | bytes 786440 | tf_op jit(solution)/shard_map/ppermute | solution.py:16
  63.3 21.5 %collective-permute-start.7 = (bf16[16,2,8,512]{3,2,1,0:T(8,128)(2,1)S(1)}, bf16[16,2,8,512]{3,2,1,0:T(8,128)(2,1)S(1)}, u32[]{:S(2)}, u32[]{:S(2)}) collective-permute-start(bf16[16,2,8,512]{3,2,1,0:T(8,128)(2,1)S(1)} %slice_bitcast_fusion), channel_id=1, source_target_pairs={{0,1},{1,2},{2,3},{3,0},{4,5},{5,6},{6,7},{7,4},{8,9},{9,10},{10,1... | collective-permute-start | bytes 786440 | tf_op jit(solution)/shard_map/ppermute | solution.py:16
  74.1 11.1 %collective-permute-start.4 = (bf16[16,2,8,512]{3,2,1,0:T(8,128)(2,1)S(1)}, bf16[16,2,8,512]{3,2,1,0:T(8,128)(2,1)S(1)}, u32[]{:S(2)}, u32[]{:S(2)}) collective-permute-start(bf16[16,2,8,512]{3,2,1,0:T(8,128)(2,1)S(1)} %all-to-all-done.refs_0_), channel_id=1, source_target_pairs={{0,1},{1,2},{2,3},{3,0},{4,5},{5,6},{6,7},{7,4},{8,9},{9,10},{10,1... | collective-permute-start | bytes 786440 | tf_op jit(solution)/shard_map/ppermute | solution.py:16
  77.6 12.7 %collective-permute-start.5 = (bf16[16,2,8,512]{3,2,1,0:T(8,128)(2,1)S(1)}, bf16[16,2,8,512]{3,2,1,0:T(8,128)(2,1)S(1)}, u32[]{:S(2)}, u32[]{:S(2)}) collective-permute-start(bf16[16,2,8,512]{3,2,1,0:T(8,128)(2,1)S(1)} %all-to-all-done.refs_0_), channel_id=1, source_target_pairs={{0,2},{1,3},{2,0},{3,1},{4,6},{5,7},{6,4},{7,5},{8,10},{9,11},{10,... | collective-permute-start | bytes 786440 | tf_op jit(solution)/shard_map/ppermute | solution.py:16
  80.5 13.2 %collective-permute-start.6 = (bf16[16,2,8,512]{3,2,1,0:T(8,128)(2,1)S(1)}, bf16[16,2,8,512]{3,2,1,0:T(8,128)(2,1)S(1)}, u32[]{:S(2)}, u32[]{:S(2)}) collective-permute-start(bf16[16,2,8,512]{3,2,1,0:T(8,128)(2,1)S(1)} %all-to-all-done.refs_0_), channel_id=1, source_target_pairs={{0,3},{1,0},{2,1},{3,2},{4,7},{5,4},{6,5},{7,6},{8,11},{9,8},{10,9... | collective-permute-start | bytes 786440 | tf_op jit(solution)/shard_map/ppermute | solution.py:16
  93.7 9.7 %copy-start.2 = (bf16[1,32,8,512]{3,2,1,0:T(8,128)(2,1)S(1)}, bf16[1,32,8,512]{3,2,1,0:T(8,128)(2,1)}, u32[]{:S(2)}) copy-start(bf16[1,32,8,512]{3,2,1,0:T(8,128)(2,1)} %param.9) | copy-start | bytes 786436
  93.7 9.7 %copy-start.3 = (bf16[1,32,8,512]{3,2,1,0:T(8,128)(2,1)S(1)}, bf16[1,32,8,512]{3,2,1,0:T(8,128)(2,1)}, u32[]{:S(2)}) copy-start(bf16[1,32,8,512]{3,2,1,0:T(8,128)(2,1)} %param.8) | copy-start | bytes 786436
  96.7 46.4 %all-to-all-start.2 = ((bf16[16,3,2,8,512]{4,3,2,1,0:T(8,128)(2,1)}), bf16[16,3,2,8,512]{4,3,2,1,0:T(8,128)(2,1)S(1)}, u32[]{:S(2)}, u32[]{:S(2)}) async-start(bf16[16,3,2,8,512]{4,3,2,1,0:T(8,128)(2,1)} %products.1), calls=%async_computation.2 | async-start | bytes 1572864 | tf_op jit(solution)/shard_map/all_to_all | solution.py:206

commit v5 on v4

--- a/solution.py
+++ b/solution.py
@@ -16,18 +16,33 @@
     return lax.ppermute(value, axis, [(i, (i + by) % n) for i in range(n)])
 
 
-def add_kernel(where, grad, got, own, *outs):
-    step = pl.program_id(0)
-    total = grad[...].astype(f32) + got[...].astype(f32)
-    for i, out in enumerate(outs):
-
-        @pl.when(step == i)
-        def _():
-            out[...] = total.astype(bf16)
-
-    @pl.when(step == len(outs))
-    def _():
-        own[...] = total
+def stack_kernel(left, right, out):
+    out[:, 0] = left[...]
+    out[:, 1] = right[...]
+
+
+def add_kernel(where, grad, got, own, *refs):
+    outs, (mine, theirs, sems) = refs[:-3], refs[-3:]
+    count, _, band = mine.shape
+    copies = []
+    for i in range(count):
+        columns = pl.ds(pl.multiple_of(where[i] * band, band), band)
+        copies.append(
+            (
+                pltpu.make_async_copy(grad.at[:, columns], mine.at[i], sems.at[0, i]),
+                pltpu.make_async_copy(got.at[:, columns], theirs.at[i], sems.at[1, i]),
+            )
+        )
+        for copy in copies[i]:
+            copy.start()
+    for i in range(count):
+        for copy in copies[i]:
+            copy.wait()
+        total = mine[i].astype(f32) + theirs[i].astype(f32)
+        if i < len(outs):
+            outs[i][...] = total.astype(bf16)
+        else:
+            own[...] = total
 
 
 def total_kernel(table, own, first, second, third, out):
@@ -43,6 +58,20 @@
     return pl.BlockSpec(shape, lambda *_: (0,) * len(shape))
 
 
+def stack_roots(left, right):
+    nz, per, piece, block = left.shape
+    return pl.pallas_call(
+        stack_kernel,
+        grid=(2,),
+        in_specs=[pl.BlockSpec((nz // 2, per, piece, block), lambda i: (i, 0, 0, 0))] * 2,
+        out_specs=pl.BlockSpec((nz // 2, 2, per, piece, block), lambda i: (i, 0, 0, 0, 0)),
+        out_shape=jax.ShapeDtypeStruct((nz, 2, per, piece, block), bf16),
+        cost_estimate=pl.CostEstimate(flops=0, bytes_accessed=8 * left.size, transcendentals=0),
+        compiler_params=params,
+        name="stack_roots",
+    )(left, right)
+
+
 def sum_dp(grad, table, nblocks, piece, block):
     nx = lax.axis_size("x")
     core = lax.axis_index("core")
@@ -59,12 +88,10 @@
         add_kernel,
         grid_spec=pltpu.PrefetchScalarGridSpec(
             num_scalar_prefetch=1,
-            grid=(nx,),
-            in_specs=[
-                pl.BlockSpec((rows, band), lambda i, s: (0, s[nx + i])),
-                pl.BlockSpec((rows, band), lambda i, s: (0, s[nx + i])),
-            ],
+            grid=(1,),
+            in_specs=[pl.BlockSpec(memory_space=pltpu.HBM)] * 2,
             out_specs=[piece_spec] * nx,
+            scratch_shapes=[pltpu.VMEM((nx, rows, band), bf16)] * 2 + [pltpu.SemaphoreType.DMA((2, nx))],
         ),
         out_shape=[jax.ShapeDtypeStruct((rows, band), f32)] + [bf_piece] * (nx - 1),
         cost_estimate=pl.CostEstimate(
@@ -72,7 +99,7 @@
         ),
         compiler_params=params,
         name="add_cores",
-    )(jnp.concatenate([owners, 2 * owners + core]).astype(jnp.int32), grad, got)
+    )(2 * owners + core, grad, got)
     pieces = [shift(value, "x", by) for by, value in zip(order, pieces)]
     return pl.pallas_call(
         total_kernel,

time: 145 us -> 145 us (level)
  transfers between devices with their start and end apart: 13 -> 13, of which waited for: 7 -> 7; matrix products, arithmetic and copies ran while one was open for 2% -> 2% of each run, Pallas kernels for 3% -> 2%
where the time goes in v5:
time: 145 us
  waiting for transfers between devices  72.7 us (50%)
  starting transfers between devices  60.7 us (42%)
  Pallas kernels  7.89 us (5%)
  other arithmetic  2.34 us (2%)
    all_to_all x1, waiting for transfers between devices, local(): back = lax.all_to_all(back, 'z', 0, 0, tiled=True)  39.5 us
    ppermute x9, starting transfers between devices, shift(): return lax.ppermute(value, axis, [(i, (i + by) % n) for i in range(n)])  30.6 us
    all_to_all x2, starting transfers between devices, to_owner(): return lax.all_to_all(value, 'z', 0, 0, tiled=True)  21.4 us
    all_to_all x2, waiting for transfers between devices, to_owner(): return lax.all_to_all(value, 'z', 0, 0, tiled=True)  17.4 us
    ppermute x9, waiting for transfers between devices, shift(): return lax.ppermute(value, axis, [(i, (i + by) % n) for i in range(n)])  15.8 us
    all_to_all x1, starting transfers between devices, local(): back = lax.all_to_all(back, 'z', 0, 0, tiled=True)  6.71 us
    pallas_call x1, Pallas kernels, products(): pl.pallas_call(products_kernel, grid_spec=pltpu.PrefetchScalarGridSpec(nu...  2.97 us
  transfers between devices with their start and end apart: 13, of which 7 were waited for; matrix products, arithmetic and copies ran while one was open for 2% of the time, Pallas kernels for 2%

profile of v5, /device:TPU:42, one launch (start us, length us, event | category | flops | bytes accessed | tf_op | source)
XLA Modules:
  0.0 144.7 jit_solution(17817397961139687440)
XLA Ops:
  0.6 2.1 %collective-permute-start = (bf16[64,16384]{1,0:T(8,128)(2,1)}, bf16[64,16384]{1,0:T(8,128)(2,1)}, u32[]{:S(2)}, u32[]{:S(2)}) collective-permute-start(bf16[64,16384]{1,0:T(8,128)(2,1)} %bitcast.37), channel_id=1, source_target_pairs={{0,64},{64,0},{1,65},{65,1},{2,66},{66,2},{3,67},{67,3},{4,68},{68... | collective-permute-start | bytes 6291464 | tf_op jit(solution)/shard_map/ppermute | solution.py:81
  2.7 1.9 %pad_maximum_fusion = bf16[16,2,2,8,512]{4,3,2,1,0:T(8,128)(2,1)} fusion(bf16[16,1,2,8,512]{4,3,2,1,0:T(8,128)(2,1)} %bitcast.42, bf16[16,1,2,8,512]{4,3,2,1,0:T(8,128)(2,1)} %bitcast.43), kind=kLoop, calls=%fused_computation.1 | loop fusion | flops 262144 | bytes 1048576 | tf_op jit(solution)/shard_map/stack | solution.py:225
  4.6 15.2 %all-to-all-start.1 = ((bf16[16,2,2,8,512]{4,3,2,1,0:T(8,128)(2,1)}), bf16[16,2,2,8,512]{4,3,2,1,0:T(8,128)(2,1)S(1)}, u32[]{:S(2)}, u32[]{:S(2)}) async-start(bf16[16,2,2,8,512]{4,3,2,1,0:T(8,128)(2,1)} %pad_maximum_fusion), calls=%async_computation.1 | async-start | bytes 1048576 | tf_op jit(solution)/shard_map/all_to_all | solution.py:219
  19.9 1.9 %add_cores.1 = (f32[64,2048]{1,0:T(8,128)S(1)}, bf16[64,2048]{1,0:T(8,128)(2,1)S(1)}, bf16[64,2048]{1,0:T(8,128)(2,1)S(1)}, bf16[64,2048]{1,0:T(8,128)(2,1)S(1)}) custom-call(s32[4]{0:T(128)S(1)} %fusion.where, bf16[64,16384]{1,0:T(8,128)(2,1)S(1)} %bitcast.38, bf16[64,16384]{1,0:T(8,128)(2,1)} %collective-permute-done.got), custom_call_target="tpu_custom_call" | custom-call | flops 524288 | bytes 4194304 | tf_op jit(solution)/shard_map/add_cores/pallas_call | solution.py:87
  21.8 4.0 %collective-permute-start.1 = (bf16[64,2048]{1,0:T(8,128)(2,1)S(1)}, bf16[64,2048]{1,0:T(8,128)(2,1)S(1)}, u32[]{:S(2)}, u32[]{:S(2)}) collective-permute-start(bf16[64,2048]{1,0:T(8,128)(2,1)S(1)} %get-tuple-element.14), channel_id=1, source_target_pairs={{0,256},{128,384},{256,0},{384,128},{1,257},{129,385},{257,1},{385... | collective-permute-start | bytes 786440 | tf_op jit(solution)/shard_map/ppermute | solution.py:16
  25.8 1.9 %collective-permute-start.2 = (bf16[64,2048]{1,0:T(8,128)(2,1)S(1)}, bf16[64,2048]{1,0:T(8,128)(2,1)S(1)}, u32[]{:S(2)}, u32[]{:S(2)}) collective-permute-start(bf16[64,2048]{1,0:T(8,128)(2,1)S(1)} %get-tuple-element.15), channel_id=1, source_target_pairs={{0,128},{128,256},{256,384},{384,0},{1,129},{129,257},{257,385},{3... | collective-permute-start | bytes 786440 | tf_op jit(solution)/shard_map/ppermute | solution.py:16
  27.7 3.9 %collective-permute-start.3 = (bf16[64,2048]{1,0:T(8,128)(2,1)S(1)}, bf16[64,2048]{1,0:T(8,128)(2,1)S(1)}, u32[]{:S(2)}, u32[]{:S(2)}) collective-permute-start(bf16[64,2048]{1,0:T(8,128)(2,1)S(1)} %get-tuple-element.16), channel_id=1, source_target_pairs={{0,384},{128,0},{256,128},{384,256},{1,385},{129,1},{257,129},{385... | collective-permute-start | bytes 786440 | tf_op jit(solution)/shard_map/ppermute | solution.py:16
  31.7 1.8 %collective-permute-done.1.first = bf16[64,2048]{1,0:T(8,128)(2,1)S(1)} collective-permute-done((bf16[64,2048]{1,0:T(8,128)(2,1)S(1)}, bf16[64,2048]{1,0:T(8,128)(2,1)S(1)}, u32[]{:S(2)}, u32[]{:S(2)}) %collective-permute-start.1) | collective-permute-done | bytes 262176 | tf_op jit(solution)/shard_map/ppermute | solution.py:16
  33.4 5.6 %collective-permute-done.2.second = bf16[64,2048]{1,0:T(8,128)(2,1)S(1)} collective-permute-done((bf16[64,2048]{1,0:T(8,128)(2,1)S(1)}, bf16[64,2048]{1,0:T(8,128)(2,1)S(1)}, u32[]{:S(2)}, u32[]{:S(2)}) %collective-permute-start.2) | collective-permute-done | bytes 262176 | tf_op jit(solution)/shard_map/ppermute | solution.py:16
  40.4 9.3 %all-to-all-done.1.refs_4_ = bf16[16,2,2,8,512]{4,3,2,1,0:T(8,128)(2,1)S(1)} async-done(((bf16[16,2,2,8,512]{4,3,2,1,0:T(8,128)(2,1)}), bf16[16,2,2,8,512]{4,3,2,1,0:T(8,128)(2,1)S(1)}, u32[]{:S(2)}, u32[]{:S(2)}) %all-to-all-start.1) | async-done | bytes 524320 | tf_op jit(solution)/shard_map/all_to_all | solution.py:219
  49.6 6.2 %all-to-all-start = ((bf16[16,2,8,512]{3,2,1,0:T(8,128)(2,1)}), bf16[16,2,8,512]{3,2,1,0:T(8,128)(2,1)S(1)}, u32[]{:S(2)}, u32[]{:S(2)}) async-start(bf16[16,2,8,512]{3,2,1,0:T(8,128)(2,1)} %bitcast.7), calls=%async_computation | async-start | bytes 524288 | tf_op jit(solution)/shard_map/all_to_all | solution.py:219
  55.9 4.2 %collective-permute-start.8 = (bf16[16,2,8,512]{3,2,1,0:T(8,128)(2,1)S(1)}, bf16[16,2,8,512]{3,2,1,0:T(8,128)(2,1)S(1)}, u32[]{:S(2)}, u32[]{:S(2)}) collective-permute-start(bf16[16,2,8,512]{3,2,1,0:T(8,128)(2,1)S(1)} %slice_bitcast_fusion), channel_id=1, source_target_pairs={{0,2},{1,3},{2,0},{3,1},{4,6},{5,7},{6,4},{7,5},{8,10},{9,11},{10,... | collective-permute-start | bytes 786440 | tf_op jit(solution)/shard_map/ppermute | solution.py:16
  60.1 3.3 %collective-permute-start.9 = (bf16[16,2,8,512]{3,2,1,0:T(8,128)(2,1)S(1)}, bf16[16,2,8,512]{3,2,1,0:T(8,128)(2,1)S(1)}, u32[]{:S(2)}, u32[]{:S(2)}) collective-permute-start(bf16[16,2,8,512]{3,2,1,0:T(8,128)(2,1)S(1)} %slice_bitcast_fusion), channel_id=1, source_target_pairs={{0,3},{1,0},{2,1},{3,2},{4,7},{5,4},{6,5},{7,6},{8,11},{9,8},{10,9... | collective-permute-start | bytes 786440 | tf_op jit(solution)/shard_map/ppermute | solution.py:16
  63.3 2.6 %collective-permute-start.7 = (bf16[16,2,8,512]{3,2,1,0:T(8,128)(2,1)S(1)}, bf16[16,2,8,512]{3,2,1,0:T(8,128)(2,1)S(1)}, u32[]{:S(2)}, u32[]{:S(2)}) collective-permute-start(bf16[16,2,8,512]{3,2,1,0:T(8,128)(2,1)S(1)} %slice_bitcast_fusion), channel_id=1, source_target_pairs={{0,1},{1,2},{2,3},{3,0},{4,5},{5,6},{6,7},{7,4},{8,9},{9,10},{10,1... | collective-permute-start | bytes 786440 | tf_op jit(solution)/shard_map/ppermute | solution.py:16
  66.0 8.1 %all-to-all-done.refs_0_ = bf16[16,2,8,512]{3,2,1,0:T(8,128)(2,1)S(1)} async-done(((bf16[16,2,8,512]{3,2,1,0:T(8,128)(2,1)}), bf16[16,2,8,512]{3,2,1,0:T(8,128)(2,1)S(1)}, u32[]{:S(2)}, u32[]{:S(2)}) %all-to-all-start) | async-done | bytes 262176 | tf_op jit(solution)/shard_map/all_to_all | solution.py:219
  74.1 3.5 %collective-permute-start.4 = (bf16[16,2,8,512]{3,2,1,0:T(8,128)(2,1)S(1)}, bf16[16,2,8,512]{3,2,1,0:T(8,128)(2,1)S(1)}, u32[]{:S(2)}, u32[]{:S(2)}) collective-permute-start(bf16[16,2,8,512]{3,2,1,0:T(8,128)(2,1)S(1)} %all-to-all-done.refs_0_), channel_id=1, source_target_pairs={{0,1},{1,2},{2,3},{3,0},{4,5},{5,6},{6,7},{7,4},{8,9},{9,10},{10,1... | collective-permute-start | bytes 786440 | tf_op jit(solution)/shard_map/ppermute | solution.py:16
  77.6 2.8 %collective-permute-start.5 = (bf16[16,2,8,512]{3,2,1,0:T(8,128)(2,1)S(1)}, bf16[16,2,8,512]{3,2,1,0:T(8,128)(2,1)S(1)}, u32[]{:S(2)}, u32[]{:S(2)}) collective-permute-start(bf16[16,2,8,512]{3,2,1,0:T(8,128)(2,1)S(1)} %all-to-all-done.refs_0_), channel_id=1, source_target_pairs={{0,2},{1,3},{2,0},{3,1},{4,6},{5,7},{6,4},{7,5},{8,10},{9,11},{10,... | collective-permute-start | bytes 786440 | tf_op jit(solution)/shard_map/ppermute | solution.py:16
  80.5 4.3 %collective-permute-start.6 = (bf16[16,2,8,512]{3,2,1,0:T(8,128)(2,1)S(1)}, bf16[16,2,8,512]{3,2,1,0:T(8,128)(2,1)S(1)}, u32[]{:S(2)}, u32[]{:S(2)}) collective-permute-start(bf16[16,2,8,512]{3,2,1,0:T(8,128)(2,1)S(1)} %all-to-all-done.refs_0_), channel_id=1, source_target_pairs={{0,3},{1,0},{2,1},{3,2},{4,7},{5,4},{6,5},{7,6},{8,11},{9,8},{10,9... | collective-permute-start | bytes 786440 | tf_op jit(solution)/shard_map/ppermute | solution.py:16
  85.2 5.1 %collective-permute-done.5.refs_2_ = bf16[16,2,8,512]{3,2,1,0:T(8,128)(2,1)S(1)} collective-permute-done((bf16[16,2,8,512]{3,2,1,0:T(8,128)(2,1)S(1)}, bf16[16,2,8,512]{3,2,1,0:T(8,128)(2,1)S(1)}, u32[]{:S(2)}, u32[]{:S(2)}) %collective-permute-start.5) | collective-permute-done | bytes 262176 | tf_op jit(solution)/shard_map/ppermute | solution.py:16
  90.3 3.4 %collective-permute-done.6.refs_3_ = bf16[16,2,8,512]{3,2,1,0:T(8,128)(2,1)S(1)} collective-permute-done((bf16[16,2,8,512]{3,2,1,0:T(8,128)(2,1)S(1)}, bf16[16,2,8,512]{3,2,1,0:T(8,128)(2,1)S(1)}, u32[]{:S(2)}, u32[]{:S(2)}) %collective-permute-start.6) | collective-permute-done | bytes 262176 | tf_op jit(solution)/shard_map/ppermute | solution.py:16
  93.7 3.0 %products.1 = bf16[16,3,2,8,512]{4,3,2,1,0:T(8,128)(2,1)} custom-call(s32[1]{0:T(128)} %bitcast.1.where, bf16[16,2,8,512]{3,2,1,0:T(8,128)(2,1)S(1)} %all-to-all-done.refs_0_, bf16[16,2,8,512]{3,2,1,0:T(8,128)(2,1)S(1)} %collective-permute-done.4.refs_1_, bf16[16,2,8,512]{3,2,1,0:T(8,128)(2,1)S(1)} %collective-permute-done.5.refs_2_, ...), custom_call_target="tpu_custom_call" | custom-call | flops 1073741824 | bytes 12582912 | tf_op jit(solution)/shard_map/products/pallas_call | solution.py:190
  96.7 6.7 %all-to-all-start.2 = ((bf16[16,3,2,8,512]{4,3,2,1,0:T(8,128)(2,1)}), bf16[16,3,2,8,512]{4,3,2,1,0:T(8,128)(2,1)S(1)}, u32[]{:S(2)}, u32[]{:S(2)}) async-start(bf16[16,3,2,8,512]{4,3,2,1,0:T(8,128)(2,1)} %products.1), calls=%async_computation.2 | async-start | bytes 1572864 | tf_op jit(solution)/shard_map/all_to_all | solution.py:233
  103.6 39.5 %all-to-all-done.2.back = bf16[16,3,2,8,512]{4,3,2,1,0:T(8,128)(2,1)S(1)} async-done(((bf16[16,3,2,8,512]{4,3,2,1,0:T(8,128)(2,1)}), bf16[16,3,2,8,512]{4,3,2,1,0:T(8,128)(2,1)S(1)}, u32[]{:S(2)}, u32[]{:S(2)}) %all-to-all-start.2) | async-done | bytes 786464 | tf_op jit(solution)/shard_map/all_to_all | solution.py:233
  143.1 1.6 %settle.1 = (bf16[32,8,512]{2,1,0:T(8,128)(2,1)}, bf16[32,8,512]{2,1,0:T(8,128)(2,1)}, bf16[64,2048]{1,0:T(8,128)(2,1)}) custom-call(s32[32]{0:T(128)S(1)} %bitcast.41, bf16[16,3,2,8,512]{4,3,2,1,0:T(8,128)(2,1)S(1)} %all-to-all-done.2.back, f32[32,8,512]{2,1,0:T(8,128)S(1)} %get-tuple-element.28.left, f32[32,8,512]{2,1,0:T(8,128)S(1)} %get-tuple-element.27.right), custom_call_target="tpu_custom_call" | custom-call | flops 524288 | bytes 2097152 | tf_op jit(solution)/shard_map/settle/pallas_call | solution.py:140
  (21 shorter events, 2.0 us)
Async XLA Ops:
  0.6 19.2 %copy-start = (bf16[1,64,16384]{2,1,0:T(8,128)(2,1)S(1)}, bf16[1,64,16384]{2,1,0:T(8,128)(2,1)}, u32[]{:S(2)}) copy-start(bf16[1,64,16384]{2,1,0:T(8,128)(2,1)} %param.6) | copy-start | bytes 6291460
  0.6 19.2 %collective-permute-start = (bf16[64,16384]{1,0:T(8,128)(2,1)}, bf16[64,16384]{1,0:T(8,128)(2,1)}, u32[]{:S(2)}, u32[]{:S(2)}) collective-permute-start(bf16[64,16384]{1,0:T(8,128)(2,1)} %bitcast.37), channel_id=1, source_target_pairs={{0,64},{64,0},{1,65},{65,1},{2,66},{66,2},{3,67},{67,3},{4,68},{68... | collective-permute-start | bytes 6291464 | tf_op jit(solution)/shard_map/ppermute | solution.py:81
  4.6 45.1 %all-to-all-start.1 = ((bf16[16,2,2,8,512]{4,3,2,1,0:T(8,128)(2,1)}), bf16[16,2,2,8,512]{4,3,2,1,0:T(8,128)(2,1)S(1)}, u32[]{:S(2)}, u32[]{:S(2)}) async-start(bf16[16,2,2,8,512]{4,3,2,1,0:T(8,128)(2,1)} %pad_maximum_fusion), calls=%async_computation.1 | async-start | bytes 1048576 | tf_op jit(solution)/shard_map/all_to_all | solution.py:219
  19.9 19.2 %copy-start.1 = (s32[1,32]{1,0:T(1,128)S(1)}, s32[1,32]{1,0:T(1,128)}, u32[]{:S(2)}) copy-start(s32[1,32]{1,0:T(1,128)} %param.7) | copy-start | bytes 388
  21.8 11.7 %collective-permute-start.1 = (bf16[64,2048]{1,0:T(8,128)(2,1)S(1)}, bf16[64,2048]{1,0:T(8,128)(2,1)S(1)}, u32[]{:S(2)}, u32[]{:S(2)}) collective-permute-start(bf16[64,2048]{1,0:T(8,128)(2,1)S(1)} %get-tuple-element.14), channel_id=1, source_target_pairs={{0,256},{128,384},{256,0},{384,128},{1,257},{129,385},{257,1},{385... | collective-permute-start | bytes 786440 | tf_op jit(solution)/shard_map/ppermute | solution.py:16
  25.8 13.2 %collective-permute-start.2 = (bf16[64,2048]{1,0:T(8,128)(2,1)S(1)}, bf16[64,2048]{1,0:T(8,128)(2,1)S(1)}, u32[]{:S(2)}, u32[]{:S(2)}) collective-permute-start(bf16[64,2048]{1,0:T(8,128)(2,1)S(1)} %get-tuple-element.15), channel_id=1, source_target_pairs={{0,128},{128,256},{256,384},{384,0},{1,129},{129,257},{257,385},{3... | collective-permute-start | bytes 786440 | tf_op jit(solution)/shard_map/ppermute | solution.py:16
  27.7 11.3 %collective-permute-start.3 = (bf16[64,2048]{1,0:T(8,128)(2,1)S(1)}, bf16[64,2048]{1,0:T(8,128)(2,1)S(1)}, u32[]{:S(2)}, u32[]{:S(2)}) collective-permute-start(bf16[64,2048]{1,0:T(8,128)(2,1)S(1)} %get-tuple-element.16), channel_id=1, source_target_pairs={{0,384},{128,0},{256,128},{384,256},{1,385},{129,1},{257,129},{385... | collective-permute-start | bytes 786440 | tf_op jit(solution)/shard_map/ppermute | solution.py:16
  49.6 24.5 %all-to-all-start = ((bf16[16,2,8,512]{3,2,1,0:T(8,128)(2,1)}), bf16[16,2,8,512]{3,2,1,0:T(8,128)(2,1)S(1)}, u32[]{:S(2)}, u32[]{:S(2)}) async-start(bf16[16,2,8,512]{3,2,1,0:T(8,128)(2,1)} %bitcast.7), calls=%async_computation | async-start | bytes 524288 | tf_op jit(solution)/shard_map/all_to_all | solution.py:219
  55.9 24.6 %collective-permute-start.8 = (bf16[16,2,8,512]{3,2,1,0:T(8,128)(2,1)S(1)}, bf16[16,2,8,512]{3,2,1,0:T(8,128)(2,1)S(1)}, u32[]{:S(2)}, u32[]{:S(2)}) collective-permute-start(bf16[16,2,8,512]{3,2,1,0:T(8,128)(2,1)S(1)} %slice_bitcast_fusion), channel_id=1, source_target_pairs={{0,2},{1,3},{2,0},{3,1},{4,6},{5,7},{6,4},{7,5},{8,10},{9,11},{10,... | collective-permute-start | bytes 786440 | tf_op jit(solution)/shard_map/ppermute | solution.py:16
  60.1 24.7 %collective-permute-start.9 = (bf16[16,2,8,512]{3,2,1,0:T(8,128)(2,1)S(1)}, bf16[16,2,8,512]{3,2,1,0:T(8,128)(2,1)S(1)}, u32[]{:S(2)}, u32[]{:S(2)}) collective-permute-start(bf16[16,2,8,512]{3,2,1,0:T(8,128)(2,1)S(1)} %slice_bitcast_fusion), channel_id=1, source_target_pairs={{0,3},{1,0},{2,1},{3,2},{4,7},{5,4},{6,5},{7,6},{8,11},{9,8},{10,9... | collective-permute-start | bytes 786440 | tf_op jit(solution)/shard_map/ppermute | solution.py:16
  63.3 21.5 %collective-permute-start.7 = (bf16[16,2,8,512]{3,2,1,0:T(8,128)(2,1)S(1)}, bf16[16,2,8,512]{3,2,1,0:T(8,128)(2,1)S(1)}, u32[]{:S(2)}, u32[]{:S(2)}) collective-permute-start(bf16[16,2,8,512]{3,2,1,0:T(8,128)(2,1)S(1)} %slice_bitcast_fusion), channel_id=1, source_target_pairs={{0,1},{1,2},{2,3},{3,0},{4,5},{5,6},{6,7},{7,4},{8,9},{9,10},{10,1... | collective-permute-start | bytes 786440 | tf_op jit(solution)/shard_map/ppermute | solution.py:16
  74.1 11.1 %collective-permute-start.4 = (bf16[16,2,8,512]{3,2,1,0:T(8,128)(2,1)S(1)}, bf16[16,2,8,512]{3,2,1,0:T(8,128)(2,1)S(1)}, u32[]{:S(2)}, u32[]{:S(2)}) collective-permute-start(bf16[16,2,8,512]{3,2,1,0:T(8,128)(2,1)S(1)} %all-to-all-done.refs_0_), channel_id=1, source_target_pairs={{0,1},{1,2},{2,3},{3,0},{4,5},{5,6},{6,7},{7,4},{8,9},{9,10},{10,1... | collective-permute-start | bytes 786440 | tf_op jit(solution)/shard_map/ppermute | solution.py:16
  77.6 12.7 %collective-permute-start.5 = (bf16[16,2,8,512]{3,2,1,0:T(8,128)(2,1)S(1)}, bf16[16,2,8,512]{3,2,1,0:T(8,128)(2,1)S(1)}, u32[]{:S(2)}, u32[]{:S(2)}) collective-permute-start(bf16[16,2,8,512]{3,2,1,0:T(8,128)(2,1)S(1)} %all-to-all-done.refs_0_), channel_id=1, source_target_pairs={{0,2},{1,3},{2,0},{3,1},{4,6},{5,7},{6,4},{7,5},{8,10},{9,11},{10,... | collective-permute-start | bytes 786440 | tf_op jit(solution)/shard_map/ppermute | solution.py:16
  80.5 13.2 %collective-permute-start.6 = (bf16[16,2,8,512]{3,2,1,0:T(8,128)(2,1)S(1)}, bf16[16,2,8,512]{3,2,1,0:T(8,128)(2,1)S(1)}, u32[]{:S(2)}, u32[]{:S(2)}) collective-permute-start(bf16[16,2,8,512]{3,2,1,0:T(8,128)(2,1)S(1)} %all-to-all-done.refs_0_), channel_id=1, source_target_pairs={{0,3},{1,0},{2,1},{3,2},{4,7},{5,4},{6,5},{7,6},{8,11},{9,8},{10,9... | collective-permute-start | bytes 786440 | tf_op jit(solution)/shard_map/ppermute | solution.py:16
  93.7 9.7 %copy-start.2 = (bf16[1,32,8,512]{3,2,1,0:T(8,128)(2,1)S(1)}, bf16[1,32,8,512]{3,2,1,0:T(8,128)(2,1)}, u32[]{:S(2)}) copy-start(bf16[1,32,8,512]{3,2,1,0:T(8,128)(2,1)} %param.9) | copy-start | bytes 786436
  93.7 9.7 %copy-start.3 = (bf16[1,32,8,512]{3,2,1,0:T(8,128)(2,1)S(1)}, bf16[1,32,8,512]{3,2,1,0:T(8,128)(2,1)}, u32[]{:S(2)}) copy-start(bf16[1,32,8,512]{3,2,1,0:T(8,128)(2,1)} %param.8) | copy-start | bytes 786436
  96.7 46.4 %all-to-all-start.2 = ((bf16[16,3,2,8,512]{4,3,2,1,0:T(8,128)(2,1)}), bf16[16,3,2,8,512]{4,3,2,1,0:T(8,128)(2,1)S(1)}, u32[]{:S(2)}, u32[]{:S(2)}) async-start(bf16[16,3,2,8,512]{4,3,2,1,0:T(8,128)(2,1)} %products.1), calls=%async_computation.2 | async-start | bytes 1572864 | tf_op jit(solution)/shard_map/all_to_all | solution.py:233

commit v6 on v4

--- a/solution.py
+++ b/solution.py
@@ -115,7 +115,7 @@
         grid_spec=pltpu.PrefetchScalarGridSpec(
             num_scalar_prefetch=1,
             grid=(1,),
-            in_specs=[whole(back.shape), whole(left.shape), whole(right.shape)],
+            in_specs=[pl.BlockSpec(memory_space=pltpu.VMEM)] * 3,
             out_specs=[whole(left.shape), whole(right.shape), whole((rows, cols))],
         ),
         out_shape=[
@@ -136,6 +136,7 @@
     nz, _, _, piece, block = back.shape
     ny = len(g_parts)
     y = where[0]
+    slot = pl.program_id(0)
     scale = (1.0 - decay) / block
 
     def flat(value):
@@ -145,11 +146,11 @@
         return lax.dot_general(a, b, (over, ((), ())), preferred_element_type=f32)
 
     for by, part in enumerate(g_parts):
-        rows[:, lax.rem(y - by + ny, ny)] = part[:, 0].astype(f32)
+        rows[:, lax.rem(y - by + ny, ny)] = part[:, slot].astype(f32)
     g = rows[...].reshape(block, block).astype(bf16)
-    half = dot(flat(left_root[:, 0, 0]), g).astype(bf16)
-    back[:, 2, 0] = dot(half, right_root[0]).reshape(nz, piece, block).astype(bf16)
-    left = dot(flat(g_parts[0][:, 0]), g, ((1,), (1,)))
+    half = dot(flat(left_root[:, 0, slot]), g).astype(bf16)
+    back[:, 2, 0] = dot(half, right_root[slot]).reshape(nz, piece, block).astype(bf16)
+    left = dot(flat(g_parts[0][:, slot]), g, ((1,), (1,)))
     back[:, 0, 0] = (scale * left).reshape(nz, piece, block).astype(bf16)
     gram[...] = dot(g, g, ((0,), (0,))).reshape(gram.shape)
     back[:, 1, 0] = (scale * gram[:, y]).astype(bf16)
@@ -158,14 +159,13 @@
 def products(g_parts, roots, right_root, y):
     ny = len(g_parts)
     nz, per, piece, block = g_parts[0].shape
-    part = pl.BlockSpec((nz, 1, piece, block), lambda s, _: (0, s, 0, 0))
     several = lambda n: pl.BlockSpec((nz, n, 1, piece, block), lambda s, _: (0, 0, s, 0, 0))
     return pl.pallas_call(
         products_kernel,
         grid_spec=pltpu.PrefetchScalarGridSpec(
             num_scalar_prefetch=1,
             grid=(per,),
-            in_specs=[part] * ny + [several(1), pl.BlockSpec((1, block, block), lambda s, _: (s, 0, 0))],
+            in_specs=[pl.BlockSpec(memory_space=pltpu.VMEM)] * (ny + 2),
             out_specs=several(3),
             scratch_shapes=[pltpu.VMEM((nz, ny, piece, block), f32)] * 2,
         ),

time: 145 us -> 145 us (level)
  the two profiles are of different devices: /device:TPU:42 before, /device:TPU:40 now
where the time goes in v6:
time: 145 us
  waiting for transfers between devices  69.5 us (48%)
  starting transfers between devices  62.8 us (43%)
  Pallas kernels  8.91 us (6%)
  other arithmetic  2.35 us (2%)
    all_to_all x1, waiting for transfers between devices, local(): back = lax.all_to_all(back, 'z', 0, 0, tiled=True)  39.6 us
    ppermute x9, starting transfers between devices, shift(): return lax.ppermute(value, axis, [(i, (i + by) % n) for i in range(n)])  32.7 us
    all_to_all x2, starting transfers between devices, to_owner(): return lax.all_to_all(value, 'z', 0, 0, tiled=True)  21.4 us
    all_to_all x2, waiting for transfers between devices, to_owner(): return lax.all_to_all(value, 'z', 0, 0, tiled=True)  16.2 us
    ppermute x9, waiting for transfers between devices, shift(): return lax.ppermute(value, axis, [(i, (i + by) % n) for i in range(n)])  13.7 us
    all_to_all x1, starting transfers between devices, local(): back = lax.all_to_all(back, 'z', 0, 0, tiled=True)  6.71 us
    pallas_call x1, Pallas kernels, sum_dp(): pl.pallas_call(add_kernel, grid_spec=pltpu.PrefetchScalarGridSpec(num_sca...  3.01 us
  transfers between devices with their start and end apart: 13, of which 8 were waited for; matrix products, arithmetic and copies ran while one was open for 2% of the time, Pallas kernels for 3%

profile of v6, /device:TPU:40, one launch (start us, length us, event | category | flops | bytes accessed | tf_op | source)
XLA Modules:
  0.0 144.7 jit_solution(18366733425939484580)
XLA Ops:
  0.6 2.1 %collective-permute-start = (bf16[64,16384]{1,0:T(8,128)(2,1)}, bf16[64,16384]{1,0:T(8,128)(2,1)}, u32[]{:S(2)}, u32[]{:S(2)}) collective-permute-start(bf16[64,16384]{1,0:T(8,128)(2,1)} %bitcast.37), channel_id=1, source_target_pairs={{0,64},{64,0},{1,65},{65,1},{2,66},{66,2},{3,67},{67,3},{4,68},{68... | collective-permute-start | bytes 6291464 | tf_op jit(solution)/shard_map/ppermute | solution.py:52
  2.7 1.9 %pad_maximum_fusion = bf16[16,2,2,8,512]{4,3,2,1,0:T(8,128)(2,1)} fusion(bf16[16,1,2,8,512]{4,3,2,1,0:T(8,128)(2,1)} %bitcast.42, bf16[16,1,2,8,512]{4,3,2,1,0:T(8,128)(2,1)} %bitcast.43), kind=kLoop, calls=%fused_computation.1 | loop fusion | flops 262144 | bytes 1048576 | tf_op jit(solution)/shard_map/stack | solution.py:198
  4.6 15.2 %all-to-all-start.1 = ((bf16[16,2,2,8,512]{4,3,2,1,0:T(8,128)(2,1)}), bf16[16,2,2,8,512]{4,3,2,1,0:T(8,128)(2,1)S(1)}, u32[]{:S(2)}, u32[]{:S(2)}) async-start(bf16[16,2,2,8,512]{4,3,2,1,0:T(8,128)(2,1)} %pad_maximum_fusion), calls=%async_computation.1 | async-start | bytes 1048576 | tf_op jit(solution)/shard_map/all_to_all | solution.py:192
  20.0 3.0 %add_cores.1 = (f32[64,2048]{1,0:T(8,128)S(1)}, bf16[64,2048]{1,0:T(8,128)(2,1)S(1)}, bf16[64,2048]{1,0:T(8,128)(2,1)S(1)}, bf16[64,2048]{1,0:T(8,128)(2,1)S(1)}) custom-call(s32[8]{0:T(128)S(1)} %concatenate.4.where, bf16[64,16384]{1,0:T(8,128)(2,1)S(1)} %bitcast.38, bf16[64,16384]{1,0:T(8,128)(2,1)} %collective-permute-done.got), custom_call_target="tpu_custom_call" | custom-call | flops 524288 | bytes 4194304 | tf_op jit(solution)/shard_map/add_cores/pallas_call | solution.py:58
  23.0 4.9 %collective-permute-start.1 = (bf16[64,2048]{1,0:T(8,128)(2,1)S(1)}, bf16[64,2048]{1,0:T(8,128)(2,1)S(1)}, u32[]{:S(2)}, u32[]{:S(2)}) collective-permute-start(bf16[64,2048]{1,0:T(8,128)(2,1)S(1)} %get-tuple-element.14), channel_id=1, source_target_pairs={{0,256},{128,384},{256,0},{384,128},{1,257},{129,385},{257,1},{385... | collective-permute-start | bytes 786440 | tf_op jit(solution)/shard_map/ppermute | solution.py:16
  27.9 2.5 %collective-permute-start.2 = (bf16[64,2048]{1,0:T(8,128)(2,1)S(1)}, bf16[64,2048]{1,0:T(8,128)(2,1)S(1)}, u32[]{:S(2)}, u32[]{:S(2)}) collective-permute-start(bf16[64,2048]{1,0:T(8,128)(2,1)S(1)} %get-tuple-element.15), channel_id=1, source_target_pairs={{0,128},{128,256},{256,384},{384,0},{1,129},{129,257},{257,385},{3... | collective-permute-start | bytes 786440 | tf_op jit(solution)/shard_map/ppermute | solution.py:16
  30.4 4.6 %collective-permute-start.3 = (bf16[64,2048]{1,0:T(8,128)(2,1)S(1)}, bf16[64,2048]{1,0:T(8,128)(2,1)S(1)}, u32[]{:S(2)}, u32[]{:S(2)}) collective-permute-start(bf16[64,2048]{1,0:T(8,128)(2,1)S(1)} %get-tuple-element.16), channel_id=1, source_target_pairs={{0,384},{128,0},{256,128},{384,256},{1,385},{129,1},{257,129},{385... | collective-permute-start | bytes 786440 | tf_op jit(solution)/shard_map/ppermute | solution.py:16
  35.5 4.6 %collective-permute-done.2.second = bf16[64,2048]{1,0:T(8,128)(2,1)S(1)} collective-permute-done((bf16[64,2048]{1,0:T(8,128)(2,1)S(1)}, bf16[64,2048]{1,0:T(8,128)(2,1)S(1)}, u32[]{:S(2)}, u32[]{:S(2)}) %collective-permute-start.2) | collective-permute-done | bytes 262176 | tf_op jit(solution)/shard_map/ppermute | solution.py:16
  40.2 1.4 total_in_slots.1
  41.6 8.0 %all-to-all-done.1.refs_4_ = bf16[16,2,2,8,512]{4,3,2,1,0:T(8,128)(2,1)S(1)} async-done(((bf16[16,2,2,8,512]{4,3,2,1,0:T(8,128)(2,1)}), bf16[16,2,2,8,512]{4,3,2,1,0:T(8,128)(2,1)S(1)}, u32[]{:S(2)}, u32[]{:S(2)}) %all-to-all-start.1) | async-done | bytes 524320 | tf_op jit(solution)/shard_map/all_to_all | solution.py:192
  49.6 6.2 %all-to-all-start = ((bf16[16,2,8,512]{3,2,1,0:T(8,128)(2,1)}), bf16[16,2,8,512]{3,2,1,0:T(8,128)(2,1)S(1)}, u32[]{:S(2)}, u32[]{:S(2)}) async-start(bf16[16,2,8,512]{3,2,1,0:T(8,128)(2,1)} %bitcast.7), calls=%async_computation | async-start | bytes 524288 | tf_op jit(solution)/shard_map/all_to_all | solution.py:192
  55.9 4.2 %collective-permute-start.8 = (bf16[16,2,8,512]{3,2,1,0:T(8,128)(2,1)S(1)}, bf16[16,2,8,512]{3,2,1,0:T(8,128)(2,1)S(1)}, u32[]{:S(2)}, u32[]{:S(2)}) collective-permute-start(bf16[16,2,8,512]{3,2,1,0:T(8,128)(2,1)S(1)} %slice_bitcast_fusion), channel_id=1, source_target_pairs={{0,2},{1,3},{2,0},{3,1},{4,6},{5,7},{6,4},{7,5},{8,10},{9,11},{10,... | collective-permute-start | bytes 786440 | tf_op jit(solution)/shard_map/ppermute | solution.py:16
  60.1 3.3 %collective-permute-start.9 = (bf16[16,2,8,512]{3,2,1,0:T(8,128)(2,1)S(1)}, bf16[16,2,8,512]{3,2,1,0:T(8,128)(2,1)S(1)}, u32[]{:S(2)}, u32[]{:S(2)}) collective-permute-start(bf16[16,2,8,512]{3,2,1,0:T(8,128)(2,1)S(1)} %slice_bitcast_fusion), channel_id=1, source_target_pairs={{0,3},{1,0},{2,1},{3,2},{4,7},{5,4},{6,5},{7,6},{8,11},{9,8},{10,9... | collective-permute-start | bytes 786440 | tf_op jit(solution)/shard_map/ppermute | solution.py:16
  63.3 2.6 %collective-permute-start.7 = (bf16[16,2,8,512]{3,2,1,0:T(8,128)(2,1)S(1)}, bf16[16,2,8,512]{3,2,1,0:T(8,128)(2,1)S(1)}, u32[]{:S(2)}, u32[]{:S(2)}) collective-permute-start(bf16[16,2,8,512]{3,2,1,0:T(8,128)(2,1)S(1)} %slice_bitcast_fusion), channel_id=1, source_target_pairs={{0,1},{1,2},{2,3},{3,0},{4,5},{5,6},{6,7},{7,4},{8,9},{9,10},{10,1... | collective-permute-start | bytes 786440 | tf_op jit(solution)/shard_map/ppermute | solution.py:16
  66.0 8.1 %all-to-all-done.refs_0_ = bf16[16,2,8,512]{3,2,1,0:T(8,128)(2,1)S(1)} async-done(((bf16[16,2,8,512]{3,2,1,0:T(8,128)(2,1)}), bf16[16,2,8,512]{3,2,1,0:T(8,128)(2,1)S(1)}, u32[]{:S(2)}, u32[]{:S(2)}) %all-to-all-start) | async-done | bytes 262176 | tf_op jit(solution)/shard_map/all_to_all | solution.py:192
  74.1 3.5 %collective-permute-start.4 = (bf16[16,2,8,512]{3,2,1,0:T(8,128)(2,1)S(1)}, bf16[16,2,8,512]{3,2,1,0:T(8,128)(2,1)S(1)}, u32[]{:S(2)}, u32[]{:S(2)}) collective-permute-start(bf16[16,2,8,512]{3,2,1,0:T(8,128)(2,1)S(1)} %all-to-all-done.refs_0_), channel_id=1, source_target_pairs={{0,1},{1,2},{2,3},{3,0},{4,5},{5,6},{6,7},{7,4},{8,9},{9,10},{10,1... | collective-permute-start | bytes 786440 | tf_op jit(solution)/shard_map/ppermute | solution.py:16
  77.6 2.8 %collective-permute-start.5 = (bf16[16,2,8,512]{3,2,1,0:T(8,128)(2,1)S(1)}, bf16[16,2,8,512]{3,2,1,0:T(8,128)(2,1)S(1)}, u32[]{:S(2)}, u32[]{:S(2)}) collective-permute-start(bf16[16,2,8,512]{3,2,1,0:T(8,128)(2,1)S(1)} %all-to-all-done.refs_0_), channel_id=1, source_target_pairs={{0,2},{1,3},{2,0},{3,1},{4,6},{5,7},{6,4},{7,5},{8,10},{9,11},{10,... | collective-permute-start | bytes 786440 | tf_op jit(solution)/shard_map/ppermute | solution.py:16
  80.5 4.3 %collective-permute-start.6 = (bf16[16,2,8,512]{3,2,1,0:T(8,128)(2,1)S(1)}, bf16[16,2,8,512]{3,2,1,0:T(8,128)(2,1)S(1)}, u32[]{:S(2)}, u32[]{:S(2)}) collective-permute-start(bf16[16,2,8,512]{3,2,1,0:T(8,128)(2,1)S(1)} %all-to-all-done.refs_0_), channel_id=1, source_target_pairs={{0,3},{1,0},{2,1},{3,2},{4,7},{5,4},{6,5},{7,6},{8,11},{9,8},{10,9... | collective-permute-start | bytes 786440 | tf_op jit(solution)/shard_map/ppermute | solution.py:16
  85.2 5.1 %collective-permute-done.5.refs_2_ = bf16[16,2,8,512]{3,2,1,0:T(8,128)(2,1)S(1)} collective-permute-done((bf16[16,2,8,512]{3,2,1,0:T(8,128)(2,1)S(1)}, bf16[16,2,8,512]{3,2,1,0:T(8,128)(2,1)S(1)}, u32[]{:S(2)}, u32[]{:S(2)}) %collective-permute-start.5) | collective-permute-done | bytes 262176 | tf_op jit(solution)/shard_map/ppermute | solution.py:16
  90.3 3.4 %collective-permute-done.6.refs_3_ = bf16[16,2,8,512]{3,2,1,0:T(8,128)(2,1)S(1)} collective-permute-done((bf16[16,2,8,512]{3,2,1,0:T(8,128)(2,1)S(1)}, bf16[16,2,8,512]{3,2,1,0:T(8,128)(2,1)S(1)}, u32[]{:S(2)}, u32[]{:S(2)}) %collective-permute-start.6) | collective-permute-done | bytes 262176 | tf_op jit(solution)/shard_map/ppermute | solution.py:16
  93.7 2.9 %products.1 = bf16[16,3,2,8,512]{4,3,2,1,0:T(8,128)(2,1)} custom-call(s32[1]{0:T(128)} %bitcast.1.where, bf16[16,2,8,512]{3,2,1,0:T(8,128)(2,1)S(1)} %all-to-all-done.refs_0_, bf16[16,2,8,512]{3,2,1,0:T(8,128)(2,1)S(1)} %collective-permute-done.4.refs_1_, bf16[16,2,8,512]{3,2,1,0:T(8,128)(2,1)S(1)} %collective-permute-done.5.refs_2_, ...), custom_call_target="tpu_custom_call" | custom-call | flops 1073741824 | bytes 12582912 | tf_op jit(solution)/shard_map/products/pallas_call | solution.py:163
  96.6 6.7 %all-to-all-start.2 = ((bf16[16,3,2,8,512]{4,3,2,1,0:T(8,128)(2,1)}), bf16[16,3,2,8,512]{4,3,2,1,0:T(8,128)(2,1)S(1)}, u32[]{:S(2)}, u32[]{:S(2)}) async-start(bf16[16,3,2,8,512]{4,3,2,1,0:T(8,128)(2,1)} %products.1), calls=%async_computation.2 | async-start | bytes 1572864 | tf_op jit(solution)/shard_map/all_to_all | solution.py:206
  103.5 39.6 %all-to-all-done.2.back = bf16[16,3,2,8,512]{4,3,2,1,0:T(8,128)(2,1)S(1)} async-done(((bf16[16,3,2,8,512]{4,3,2,1,0:T(8,128)(2,1)}), bf16[16,3,2,8,512]{4,3,2,1,0:T(8,128)(2,1)S(1)}, u32[]{:S(2)}, u32[]{:S(2)}) %all-to-all-start.2) | async-done | bytes 786464 | tf_op jit(solution)/shard_map/all_to_all | solution.py:206
  143.1 1.6 %settle.1 = (bf16[32,8,512]{2,1,0:T(8,128)(2,1)}, bf16[32,8,512]{2,1,0:T(8,128)(2,1)}, bf16[64,2048]{1,0:T(8,128)(2,1)}) custom-call(s32[32]{0:T(128)S(1)} %bitcast.41, bf16[16,3,2,8,512]{4,3,2,1,0:T(8,128)(2,1)S(1)} %all-to-all-done.2.back, f32[32,8,512]{2,1,0:T(8,128)S(1)} %get-tuple-element.28.left, f32[32,8,512]{2,1,0:T(8,128)S(1)} %get-tuple-element.27.right), custom_call_target="tpu_custom_call" | custom-call | flops 524288 | bytes 2097152 | tf_op jit(solution)/shard_map/settle/pallas_call | solution.py:113
  (22 shorter events, 1.4 us)
Async XLA Ops:
  0.6 19.3 %copy-start = (bf16[1,64,16384]{2,1,0:T(8,128)(2,1)S(1)}, bf16[1,64,16384]{2,1,0:T(8,128)(2,1)}, u32[]{:S(2)}) copy-start(bf16[1,64,16384]{2,1,0:T(8,128)(2,1)} %param.6) | copy-start | bytes 6291460
  0.6 19.3 %collective-permute-start = (bf16[64,16384]{1,0:T(8,128)(2,1)}, bf16[64,16384]{1,0:T(8,128)(2,1)}, u32[]{:S(2)}, u32[]{:S(2)}) collective-permute-start(bf16[64,16384]{1,0:T(8,128)(2,1)} %bitcast.37), channel_id=1, source_target_pairs={{0,64},{64,0},{1,65},{65,1},{2,66},{66,2},{3,67},{67,3},{4,68},{68... | collective-permute-start | bytes 6291464 | tf_op jit(solution)/shard_map/ppermute | solution.py:52
  4.6 45.1 %all-to-all-start.1 = ((bf16[16,2,2,8,512]{4,3,2,1,0:T(8,128)(2,1)}), bf16[16,2,2,8,512]{4,3,2,1,0:T(8,128)(2,1)S(1)}, u32[]{:S(2)}, u32[]{:S(2)}) async-start(bf16[16,2,2,8,512]{4,3,2,1,0:T(8,128)(2,1)} %pad_maximum_fusion), calls=%async_computation.1 | async-start | bytes 1048576 | tf_op jit(solution)/shard_map/all_to_all | solution.py:192
  19.9 20.3 %copy-start.1 = (s32[1,32]{1,0:T(1,128)S(1)}, s32[1,32]{1,0:T(1,128)}, u32[]{:S(2)}) copy-start(s32[1,32]{1,0:T(1,128)} %param.7) | copy-start | bytes 388
  23.0 12.6 %collective-permute-start.1 = (bf16[64,2048]{1,0:T(8,128)(2,1)S(1)}, bf16[64,2048]{1,0:T(8,128)(2,1)S(1)}, u32[]{:S(2)}, u32[]{:S(2)}) collective-permute-start(bf16[64,2048]{1,0:T(8,128)(2,1)S(1)} %get-tuple-element.14), channel_id=1, source_target_pairs={{0,256},{128,384},{256,0},{384,128},{1,257},{129,385},{257,1},{385... | collective-permute-start | bytes 786440 | tf_op jit(solution)/shard_map/ppermute | solution.py:16
  27.9 12.2 %collective-permute-start.2 = (bf16[64,2048]{1,0:T(8,128)(2,1)S(1)}, bf16[64,2048]{1,0:T(8,128)(2,1)S(1)}, u32[]{:S(2)}, u32[]{:S(2)}) collective-permute-start(bf16[64,2048]{1,0:T(8,128)(2,1)S(1)} %get-tuple-element.15), channel_id=1, source_target_pairs={{0,128},{128,256},{256,384},{384,0},{1,129},{129,257},{257,385},{3... | collective-permute-start | bytes 786440 | tf_op jit(solution)/shard_map/ppermute | solution.py:16
  30.4 9.8 %collective-permute-start.3 = (bf16[64,2048]{1,0:T(8,128)(2,1)S(1)}, bf16[64,2048]{1,0:T(8,128)(2,1)S(1)}, u32[]{:S(2)}, u32[]{:S(2)}) collective-permute-start(bf16[64,2048]{1,0:T(8,128)(2,1)S(1)} %get-tuple-element.16), channel_id=1, source_target_pairs={{0,384},{128,0},{256,128},{384,256},{1,385},{129,1},{257,129},{385... | collective-permute-start | bytes 786440 | tf_op jit(solution)/shard_map/ppermute | solution.py:16
  49.6 24.5 %all-to-all-start = ((bf16[16,2,8,512]{3,2,1,0:T(8,128)(2,1)}), bf16[16,2,8,512]{3,2,1,0:T(8,128)(2,1)S(1)}, u32[]{:S(2)}, u32[]{:S(2)}) async-start(bf16[16,2,8,512]{3,2,1,0:T(8,128)(2,1)} %bitcast.7), calls=%async_computation | async-start | bytes 524288 | tf_op jit(solution)/shard_map/all_to_all | solution.py:192
  55.9 24.6 %collective-permute-start.8 = (bf16[16,2,8,512]{3,2,1,0:T(8,128)(2,1)S(1)}, bf16[16,2,8,512]{3,2,1,0:T(8,128)(2,1)S(1)}, u32[]{:S(2)}, u32[]{:S(2)}) collective-permute-start(bf16[16,2,8,512]{3,2,1,0:T(8,128)(2,1)S(1)} %slice_bitcast_fusion), channel_id=1, source_target_pairs={{0,2},{1,3},{2,0},{3,1},{4,6},{5,7},{6,4},{7,5},{8,10},{9,11},{10,... | collective-permute-start | bytes 786440 | tf_op jit(solution)/shard_map/ppermute | solution.py:16
  60.1 24.7 %collective-permute-start.9 = (bf16[16,2,8,512]{3,2,1,0:T(8,128)(2,1)S(1)}, bf16[16,2,8,512]{3,2,1,0:T(8,128)(2,1)S(1)}, u32[]{:S(2)}, u32[]{:S(2)}) collective-permute-start(bf16[16,2,8,512]{3,2,1,0:T(8,128)(2,1)S(1)} %slice_bitcast_fusion), channel_id=1, source_target_pairs={{0,3},{1,0},{2,1},{3,2},{4,7},{5,4},{6,5},{7,6},{8,11},{9,8},{10,9... | collective-permute-start | bytes 786440 | tf_op jit(solution)/shard_map/ppermute | solution.py:16
  63.3 21.5 %collective-permute-start.7 = (bf16[16,2,8,512]{3,2,1,0:T(8,128)(2,1)S(1)}, bf16[16,2,8,512]{3,2,1,0:T(8,128)(2,1)S(1)}, u32[]{:S(2)}, u32[]{:S(2)}) collective-permute-start(bf16[16,2,8,512]{3,2,1,0:T(8,128)(2,1)S(1)} %slice_bitcast_fusion), channel_id=1, source_target_pairs={{0,1},{1,2},{2,3},{3,0},{4,5},{5,6},{6,7},{7,4},{8,9},{9,10},{10,1... | collective-permute-start | bytes 786440 | tf_op jit(solution)/shard_map/ppermute | solution.py:16
  74.1 11.1 %collective-permute-start.4 = (bf16[16,2,8,512]{3,2,1,0:T(8,128)(2,1)S(1)}, bf16[16,2,8,512]{3,2,1,0:T(8,128)(2,1)S(1)}, u32[]{:S(2)}, u32[]{:S(2)}) collective-permute-start(bf16[16,2,8,512]{3,2,1,0:T(8,128)(2,1)S(1)} %all-to-all-done.refs_0_), channel_id=1, source_target_pairs={{0,1},{1,2},{2,3},{3,0},{4,5},{5,6},{6,7},{7,4},{8,9},{9,10},{10,1... | collective-permute-start | bytes 786440 | tf_op jit(solution)/shard_map/ppermute | solution.py:16
  77.6 12.7 %collective-permute-start.5 = (bf16[16,2,8,512]{3,2,1,0:T(8,128)(2,1)S(1)}, bf16[16,2,8,512]{3,2,1,0:T(8,128)(2,1)S(1)}, u32[]{:S(2)}, u32[]{:S(2)}) collective-permute-start(bf16[16,2,8,512]{3,2,1,0:T(8,128)(2,1)S(1)} %all-to-all-done.refs_0_), channel_id=1, source_target_pairs={{0,2},{1,3},{2,0},{3,1},{4,6},{5,7},{6,4},{7,5},{8,10},{9,11},{10,... | collective-permute-start | bytes 786440 | tf_op jit(solution)/shard_map/ppermute | solution.py:16
  80.5 13.2 %collective-permute-start.6 = (bf16[16,2,8,512]{3,2,1,0:T(8,128)(2,1)S(1)}, bf16[16,2,8,512]{3,2,1,0:T(8,128)(2,1)S(1)}, u32[]{:S(2)}, u32[]{:S(2)}) collective-permute-start(bf16[16,2,8,512]{3,2,1,0:T(8,128)(2,1)S(1)} %all-to-all-done.refs_0_), channel_id=1, source_target_pairs={{0,3},{1,0},{2,1},{3,2},{4,7},{5,4},{6,5},{7,6},{8,11},{9,8},{10,9... | collective-permute-start | bytes 786440 | tf_op jit(solution)/shard_map/ppermute | solution.py:16
  93.7 9.6 %copy-start.2 = (bf16[1,32,8,512]{3,2,1,0:T(8,128)(2,1)S(1)}, bf16[1,32,8,512]{3,2,1,0:T(8,128)(2,1)}, u32[]{:S(2)}) copy-start(bf16[1,32,8,512]{3,2,1,0:T(8,128)(2,1)} %param.9) | copy-start | bytes 786436
  93.7 9.6 %copy-start.3 = (bf16[1,32,8,512]{3,2,1,0:T(8,128)(2,1)S(1)}, bf16[1,32,8,512]{3,2,1,0:T(8,128)(2,1)}, u32[]{:S(2)}) copy-start(bf16[1,32,8,512]{3,2,1,0:T(8,128)(2,1)} %param.8) | copy-start | bytes 786436
  96.6 46.4 %all-to-all-start.2 = ((bf16[16,3,2,8,512]{4,3,2,1,0:T(8,128)(2,1)}), bf16[16,3,2,8,512]{4,3,2,1,0:T(8,128)(2,1)S(1)}, u32[]{:S(2)}, u32[]{:S(2)}) async-start(bf16[16,3,2,8,512]{4,3,2,1,0:T(8,128)(2,1)} %products.1), calls=%async_computation.2 | async-start | bytes 1572864 | tf_op jit(solution)/shard_map/all_to_all | solution.py:206

commit v7 on v5

--- a/solution.py
+++ b/solution.py
@@ -14,11 +14,6 @@
 def shift(value, axis, by):
     n = lax.axis_size(axis)
     return lax.ppermute(value, axis, [(i, (i + by) % n) for i in range(n)])
-
-
-def stack_kernel(left, right, out):
-    out[:, 0] = left[...]
-    out[:, 1] = right[...]
 
 
 def add_kernel(where, grad, got, own, *refs):
@@ -58,20 +53,6 @@
     return pl.BlockSpec(shape, lambda *_: (0,) * len(shape))
 
 
-def stack_roots(left, right):
-    nz, per, piece, block = left.shape
-    return pl.pallas_call(
-        stack_kernel,
-        grid=(2,),
-        in_specs=[pl.BlockSpec((nz // 2, per, piece, block), lambda i: (i, 0, 0, 0))] * 2,
-        out_specs=pl.BlockSpec((nz // 2, 2, per, piece, block), lambda i: (i, 0, 0, 0, 0)),
-        out_shape=jax.ShapeDtypeStruct((nz, 2, per, piece, block), bf16),
-        cost_estimate=pl.CostEstimate(flops=0, bytes_accessed=8 * left.size, transcendentals=0),
-        compiler_params=params,
-        name="stack_roots",
-    )(left, right)
-
-
 def sum_dp(grad, table, nblocks, piece, block):
     nx = lax.axis_size("x")
     core = lax.axis_index("core")
@@ -142,7 +123,7 @@
         grid_spec=pltpu.PrefetchScalarGridSpec(
             num_scalar_prefetch=1,
             grid=(1,),
-            in_specs=[whole(back.shape), whole(left.shape), whole(right.shape)],
+            in_specs=[pl.BlockSpec(memory_space=pltpu.VMEM)] * 3,
             out_specs=[whole(left.shape), whole(right.shape), whole((rows, cols))],
         ),
         out_shape=[
@@ -163,6 +144,7 @@
     nz, _, _, piece, block = back.shape
     ny = len(g_parts)
     y = where[0]
+    slot = pl.program_id(0)
     scale = (1.0 - decay) / block
 
     def flat(value):
@@ -172,11 +154,11 @@
         return lax.dot_general(a, b, (over, ((), ())), preferred_element_type=f32)
 
     for by, part in enumerate(g_parts):
-        rows[:, lax.rem(y - by + ny, ny)] = part[:, 0].astype(f32)
+        rows[:, lax.rem(y - by + ny, ny)] = part[:, slot].astype(f32)
     g = rows[...].reshape(block, block).astype(bf16)
-    half = dot(flat(left_root[:, 0, 0]), g).astype(bf16)
-    back[:, 2, 0] = dot(half, right_root[0]).reshape(nz, piece, block).astype(bf16)
-    left = dot(flat(g_parts[0][:, 0]), g, ((1,), (1,)))
+    half = dot(flat(left_root[:, 0, slot]), g).astype(bf16)
+    back[:, 2, 0] = dot(half, right_root[slot]).reshape(nz, piece, block).astype(bf16)
+    left = dot(flat(g_parts[0][:, slot]), g, ((1,), (1,)))
     back[:, 0, 0] = (scale * left).reshape(nz, piece, block).astype(bf16)
     gram[...] = dot(g, g, ((0,), (0,))).reshape(gram.shape)
     back[:, 1, 0] = (scale * gram[:, y]).astype(bf16)
@@ -185,14 +167,13 @@
 def products(g_parts, roots, right_root, y):
     ny = len(g_parts)
     nz, per, piece, block = g_parts[0].shape
-    part = pl.BlockSpec((nz, 1, piece, block), lambda s, _: (0, s, 0, 0))
     several = lambda n: pl.BlockSpec((nz, n, 1, piece, block), lambda s, _: (0, 0, s, 0, 0))
     return pl.pallas_call(
         products_kernel,
         grid_spec=pltpu.PrefetchScalarGridSpec(
             num_scalar_prefetch=1,
             grid=(per,),
-            in_specs=[part] * ny + [several(1), pl.BlockSpec((1, block, block), lambda s, _: (s, 0, 0))],
+            in_specs=[pl.BlockSpec(memory_space=pltpu.VMEM)] * (ny + 2),
             out_specs=several(3),
             scratch_shapes=[pltpu.VMEM((nz, ny, piece, block), f32)] * 2,
         ),

time: 145 us -> 145 us (level)
  the two profiles are of different devices: /device:TPU:42 before, /device:TPU:40 now
where the time goes in v7:
time: 145 us
  waiting for transfers between devices  70.7 us (49%)
  starting transfers between devices  62.8 us (43%)
  Pallas kernels  7.8 us (5%)
  other arithmetic  2.34 us (2%)
    all_to_all x1, waiting for transfers between devices, local(): back = lax.all_to_all(back, 'z', 0, 0, tiled=True)  39.6 us
    ppermute x9, starting transfers between devices, shift(): return lax.ppermute(value, axis, [(i, (i + by) % n) for i in range(n)])  32.7 us
    all_to_all x2, starting transfers between devices, to_owner(): return lax.all_to_all(value, 'z', 0, 0, tiled=True)  21.4 us
    all_to_all x2, waiting for transfers between devices, to_owner(): return lax.all_to_all(value, 'z', 0, 0, tiled=True)  17.4 us
    ppermute x9, waiting for transfers between devices, shift(): return lax.ppermute(value, axis, [(i, (i + by) % n) for i in range(n)])  13.7 us
    all_to_all x1, starting transfers between devices, local(): back = lax.all_to_all(back, 'z', 0, 0, tiled=True)  6.71 us
  transfers between devices with their start and end apart: 13, of which 8 were waited for; matrix products, arithmetic and copies ran while one was open for 2% of the time, Pallas kernels for 2%

profile of v7, /device:TPU:40, one launch (start us, length us, event | category | flops | bytes accessed | tf_op | source)
XLA Modules:
  0.0 144.7 jit_solution(2428078054753984552)
XLA Ops:
  0.6 2.1 %collective-permute-start = (bf16[64,16384]{1,0:T(8,128)(2,1)}, bf16[64,16384]{1,0:T(8,128)(2,1)}, u32[]{:S(2)}, u32[]{:S(2)}) collective-permute-start(bf16[64,16384]{1,0:T(8,128)(2,1)} %bitcast.37), channel_id=1, source_target_pairs={{0,64},{64,0},{1,65},{65,1},{2,66},{66,2},{3,67},{67,3},{4,68},{68... | collective-permute-start | bytes 6291464 | tf_op jit(solution)/shard_map/ppermute | solution.py:62
  2.7 1.9 %pad_maximum_fusion = bf16[16,2,2,8,512]{4,3,2,1,0:T(8,128)(2,1)} fusion(bf16[16,1,2,8,512]{4,3,2,1,0:T(8,128)(2,1)} %bitcast.42, bf16[16,1,2,8,512]{4,3,2,1,0:T(8,128)(2,1)} %bitcast.43), kind=kLoop, calls=%fused_computation.1 | loop fusion | flops 262144 | bytes 1048576 | tf_op jit(solution)/shard_map/stack | solution.py:206
  4.6 15.2 %all-to-all-start.1 = ((bf16[16,2,2,8,512]{4,3,2,1,0:T(8,128)(2,1)}), bf16[16,2,2,8,512]{4,3,2,1,0:T(8,128)(2,1)S(1)}, u32[]{:S(2)}, u32[]{:S(2)}) async-start(bf16[16,2,2,8,512]{4,3,2,1,0:T(8,128)(2,1)} %pad_maximum_fusion), calls=%async_computation.1 | async-start | bytes 1048576 | tf_op jit(solution)/shard_map/all_to_all | solution.py:200
  19.9 1.9 %add_cores.1 = (f32[64,2048]{1,0:T(8,128)S(1)}, bf16[64,2048]{1,0:T(8,128)(2,1)S(1)}, bf16[64,2048]{1,0:T(8,128)(2,1)S(1)}, bf16[64,2048]{1,0:T(8,128)(2,1)S(1)}) custom-call(s32[4]{0:T(128)S(1)} %fusion.where, bf16[64,16384]{1,0:T(8,128)(2,1)S(1)} %bitcast.38, bf16[64,16384]{1,0:T(8,128)(2,1)} %collective-permute-done.got), custom_call_target="tpu_custom_call" | custom-call | flops 524288 | bytes 4194304 | tf_op jit(solution)/shard_map/add_cores/pallas_call | solution.py:68
  21.8 4.9 %collective-permute-start.1 = (bf16[64,2048]{1,0:T(8,128)(2,1)S(1)}, bf16[64,2048]{1,0:T(8,128)(2,1)S(1)}, u32[]{:S(2)}, u32[]{:S(2)}) collective-permute-start(bf16[64,2048]{1,0:T(8,128)(2,1)S(1)} %get-tuple-element.14), channel_id=1, source_target_pairs={{0,256},{128,384},{256,0},{384,128},{1,257},{129,385},{257,1},{385... | collective-permute-start | bytes 786440 | tf_op jit(solution)/shard_map/ppermute | solution.py:16
  26.7 2.5 %collective-permute-start.2 = (bf16[64,2048]{1,0:T(8,128)(2,1)S(1)}, bf16[64,2048]{1,0:T(8,128)(2,1)S(1)}, u32[]{:S(2)}, u32[]{:S(2)}) collective-permute-start(bf16[64,2048]{1,0:T(8,128)(2,1)S(1)} %get-tuple-element.15), channel_id=1, source_target_pairs={{0,128},{128,256},{256,384},{384,0},{1,129},{129,257},{257,385},{3... | collective-permute-start | bytes 786440 | tf_op jit(solution)/shard_map/ppermute | solution.py:16
  29.2 4.6 %collective-permute-start.3 = (bf16[64,2048]{1,0:T(8,128)(2,1)S(1)}, bf16[64,2048]{1,0:T(8,128)(2,1)S(1)}, u32[]{:S(2)}, u32[]{:S(2)}) collective-permute-start(bf16[64,2048]{1,0:T(8,128)(2,1)S(1)} %get-tuple-element.16), channel_id=1, source_target_pairs={{0,384},{128,0},{256,128},{384,256},{1,385},{129,1},{257,129},{385... | collective-permute-start | bytes 786440 | tf_op jit(solution)/shard_map/ppermute | solution.py:16
  34.4 4.6 %collective-permute-done.2.second = bf16[64,2048]{1,0:T(8,128)(2,1)S(1)} collective-permute-done((bf16[64,2048]{1,0:T(8,128)(2,1)S(1)}, bf16[64,2048]{1,0:T(8,128)(2,1)S(1)}, u32[]{:S(2)}, u32[]{:S(2)}) %collective-permute-start.2) | collective-permute-done | bytes 262176 | tf_op jit(solution)/shard_map/ppermute | solution.py:16
  39.0 1.4 total_in_slots.1
  40.4 9.2 %all-to-all-done.1.refs_4_ = bf16[16,2,2,8,512]{4,3,2,1,0:T(8,128)(2,1)S(1)} async-done(((bf16[16,2,2,8,512]{4,3,2,1,0:T(8,128)(2,1)}), bf16[16,2,2,8,512]{4,3,2,1,0:T(8,128)(2,1)S(1)}, u32[]{:S(2)}, u32[]{:S(2)}) %all-to-all-start.1) | async-done | bytes 524320 | tf_op jit(solution)/shard_map/all_to_all | solution.py:200
  49.6 6.2 %all-to-all-start = ((bf16[16,2,8,512]{3,2,1,0:T(8,128)(2,1)}), bf16[16,2,8,512]{3,2,1,0:T(8,128)(2,1)S(1)}, u32[]{:S(2)}, u32[]{:S(2)}) async-start(bf16[16,2,8,512]{3,2,1,0:T(8,128)(2,1)} %bitcast.7), calls=%async_computation | async-start | bytes 524288 | tf_op jit(solution)/shard_map/all_to_all | solution.py:200
  55.9 4.2 %collective-permute-start.8 = (bf16[16,2,8,512]{3,2,1,0:T(8,128)(2,1)S(1)}, bf16[16,2,8,512]{3,2,1,0:T(8,128)(2,1)S(1)}, u32[]{:S(2)}, u32[]{:S(2)}) collective-permute-start(bf16[16,2,8,512]{3,2,1,0:T(8,128)(2,1)S(1)} %slice_bitcast_fusion), channel_id=1, source_target_pairs={{0,2},{1,3},{2,0},{3,1},{4,6},{5,7},{6,4},{7,5},{8,10},{9,11},{10,... | collective-permute-start | bytes 786440 | tf_op jit(solution)/shard_map/ppermute | solution.py:16
  60.1 3.3 %collective-permute-start.9 = (bf16[16,2,8,512]{3,2,1,0:T(8,128)(2,1)S(1)}, bf16[16,2,8,512]{3,2,1,0:T(8,128)(2,1)S(1)}, u32[]{:S(2)}, u32[]{:S(2)}) collective-permute-start(bf16[16,2,8,512]{3,2,1,0:T(8,128)(2,1)S(1)} %slice_bitcast_fusion), channel_id=1, source_target_pairs={{0,3},{1,0},{2,1},{3,2},{4,7},{5,4},{6,5},{7,6},{8,11},{9,8},{10,9... | collective-permute-start | bytes 786440 | tf_op jit(solution)/shard_map/ppermute | solution.py:16
  63.3 2.6 %collective-permute-start.7 = (bf16[16,2,8,512]{3,2,1,0:T(8,128)(2,1)S(1)}, bf16[16,2,8,512]{3,2,1,0:T(8,128)(2,1)S(1)}, u32[]{:S(2)}, u32[]{:S(2)}) collective-permute-start(bf16[16,2,8,512]{3,2,1,0:T(8,128)(2,1)S(1)} %slice_bitcast_fusion), channel_id=1, source_target_pairs={{0,1},{1,2},{2,3},{3,0},{4,5},{5,6},{6,7},{7,4},{8,9},{9,10},{10,1... | collective-permute-start | bytes 786440 | tf_op jit(solution)/shard_map/ppermute | solution.py:16
  66.0 8.1 %all-to-all-done.refs_0_ = bf16[16,2,8,512]{3,2,1,0:T(8,128)(2,1)S(1)} async-done(((bf16[16,2,8,512]{3,2,1,0:T(8,128)(2,1)}), bf16[16,2,8,512]{3,2,1,0:T(8,128)(2,1)S(1)}, u32[]{:S(2)}, u32[]{:S(2)}) %all-to-all-start) | async-done | bytes 262176 | tf_op jit(solution)/shard_map/all_to_all | solution.py:200
  74.1 3.5 %collective-permute-start.4 = (bf16[16,2,8,512]{3,2,1,0:T(8,128)(2,1)S(1)}, bf16[16,2,8,512]{3,2,1,0:T(8,128)(2,1)S(1)}, u32[]{:S(2)}, u32[]{:S(2)}) collective-permute-start(bf16[16,2,8,512]{3,2,1,0:T(8,128)(2,1)S(1)} %all-to-all-done.refs_0_), channel_id=1, source_target_pairs={{0,1},{1,2},{2,3},{3,0},{4,5},{5,6},{6,7},{7,4},{8,9},{9,10},{10,1... | collective-permute-start | bytes 786440 | tf_op jit(solution)/shard_map/ppermute | solution.py:16
  77.6 2.8 %collective-permute-start.5 = (bf16[16,2,8,512]{3,2,1,0:T(8,128)(2,1)S(1)}, bf16[16,2,8,512]{3,2,1,0:T(8,128)(2,1)S(1)}, u32[]{:S(2)}, u32[]{:S(2)}) collective-permute-start(bf16[16,2,8,512]{3,2,1,0:T(8,128)(2,1)S(1)} %all-to-all-done.refs_0_), channel_id=1, source_target_pairs={{0,2},{1,3},{2,0},{3,1},{4,6},{5,7},{6,4},{7,5},{8,10},{9,11},{10,... | collective-permute-start | bytes 786440 | tf_op jit(solution)/shard_map/ppermute | solution.py:16
  80.5 4.3 %collective-permute-start.6 = (bf16[16,2,8,512]{3,2,1,0:T(8,128)(2,1)S(1)}, bf16[16,2,8,512]{3,2,1,0:T(8,128)(2,1)S(1)}, u32[]{:S(2)}, u32[]{:S(2)}) collective-permute-start(bf16[16,2,8,512]{3,2,1,0:T(8,128)(2,1)S(1)} %all-to-all-done.refs_0_), channel_id=1, source_target_pairs={{0,3},{1,0},{2,1},{3,2},{4,7},{5,4},{6,5},{7,6},{8,11},{9,8},{10,9... | collective-permute-start | bytes 786440 | tf_op jit(solution)/shard_map/ppermute | solution.py:16
  85.2 5.1 %collective-permute-done.5.refs_2_ = bf16[16,2,8,512]{3,2,1,0:T(8,128)(2,1)S(1)} collective-permute-done((bf16[16,2,8,512]{3,2,1,0:T(8,128)(2,1)S(1)}, bf16[16,2,8,512]{3,2,1,0:T(8,128)(2,1)S(1)}, u32[]{:S(2)}, u32[]{:S(2)}) %collective-permute-start.5) | collective-permute-done | bytes 262176 | tf_op jit(solution)/shard_map/ppermute | solution.py:16
  90.3 3.4 %collective-permute-done.6.refs_3_ = bf16[16,2,8,512]{3,2,1,0:T(8,128)(2,1)S(1)} collective-permute-done((bf16[16,2,8,512]{3,2,1,0:T(8,128)(2,1)S(1)}, bf16[16,2,8,512]{3,2,1,0:T(8,128)(2,1)S(1)}, u32[]{:S(2)}, u32[]{:S(2)}) %collective-permute-start.6) | collective-permute-done | bytes 262176 | tf_op jit(solution)/shard_map/ppermute | solution.py:16
  93.7 2.9 %products.1 = bf16[16,3,2,8,512]{4,3,2,1,0:T(8,128)(2,1)} custom-call(s32[1]{0:T(128)} %bitcast.1.where, bf16[16,2,8,512]{3,2,1,0:T(8,128)(2,1)S(1)} %all-to-all-done.refs_0_, bf16[16,2,8,512]{3,2,1,0:T(8,128)(2,1)S(1)} %collective-permute-done.4.refs_1_, bf16[16,2,8,512]{3,2,1,0:T(8,128)(2,1)S(1)} %collective-permute-done.5.refs_2_, ...), custom_call_target="tpu_custom_call" | custom-call | flops 1073741824 | bytes 12582912 | tf_op jit(solution)/shard_map/products/pallas_call | solution.py:171
  96.6 6.7 %all-to-all-start.2 = ((bf16[16,3,2,8,512]{4,3,2,1,0:T(8,128)(2,1)}), bf16[16,3,2,8,512]{4,3,2,1,0:T(8,128)(2,1)S(1)}, u32[]{:S(2)}, u32[]{:S(2)}) async-start(bf16[16,3,2,8,512]{4,3,2,1,0:T(8,128)(2,1)} %products.1), calls=%async_computation.2 | async-start | bytes 1572864 | tf_op jit(solution)/shard_map/all_to_all | solution.py:214
  103.5 39.6 %all-to-all-done.2.back = bf16[16,3,2,8,512]{4,3,2,1,0:T(8,128)(2,1)S(1)} async-done(((bf16[16,3,2,8,512]{4,3,2,1,0:T(8,128)(2,1)}), bf16[16,3,2,8,512]{4,3,2,1,0:T(8,128)(2,1)S(1)}, u32[]{:S(2)}, u32[]{:S(2)}) %all-to-all-start.2) | async-done | bytes 786464 | tf_op jit(solution)/shard_map/all_to_all | solution.py:214
  143.1 1.6 %settle.1 = (bf16[32,8,512]{2,1,0:T(8,128)(2,1)}, bf16[32,8,512]{2,1,0:T(8,128)(2,1)}, bf16[64,2048]{1,0:T(8,128)(2,1)}) custom-call(s32[32]{0:T(128)S(1)} %bitcast.41, bf16[16,3,2,8,512]{4,3,2,1,0:T(8,128)(2,1)S(1)} %all-to-all-done.2.back, f32[32,8,512]{2,1,0:T(8,128)S(1)} %get-tuple-element.28.left, f32[32,8,512]{2,1,0:T(8,128)S(1)} %get-tuple-element.27.right), custom_call_target="tpu_custom_call" | custom-call | flops 524288 | bytes 2097152 | tf_op jit(solution)/shard_map/settle/pallas_call | solution.py:121
  (21 shorter events, 1.3 us)
Async XLA Ops:
  0.6 19.2 %copy-start = (bf16[1,64,16384]{2,1,0:T(8,128)(2,1)S(1)}, bf16[1,64,16384]{2,1,0:T(8,128)(2,1)}, u32[]{:S(2)}) copy-start(bf16[1,64,16384]{2,1,0:T(8,128)(2,1)} %param.6) | copy-start | bytes 6291460
  0.6 19.2 %collective-permute-start = (bf16[64,16384]{1,0:T(8,128)(2,1)}, bf16[64,16384]{1,0:T(8,128)(2,1)}, u32[]{:S(2)}, u32[]{:S(2)}) collective-permute-start(bf16[64,16384]{1,0:T(8,128)(2,1)} %bitcast.37), channel_id=1, source_target_pairs={{0,64},{64,0},{1,65},{65,1},{2,66},{66,2},{3,67},{67,3},{4,68},{68... | collective-permute-start | bytes 6291464 | tf_op jit(solution)/shard_map/ppermute | solution.py:62
  4.6 45.1 %all-to-all-start.1 = ((bf16[16,2,2,8,512]{4,3,2,1,0:T(8,128)(2,1)}), bf16[16,2,2,8,512]{4,3,2,1,0:T(8,128)(2,1)S(1)}, u32[]{:S(2)}, u32[]{:S(2)}) async-start(bf16[16,2,2,8,512]{4,3,2,1,0:T(8,128)(2,1)} %pad_maximum_fusion), calls=%async_computation.1 | async-start | bytes 1048576 | tf_op jit(solution)/shard_map/all_to_all | solution.py:200
  19.9 19.2 %copy-start.1 = (s32[1,32]{1,0:T(1,128)S(1)}, s32[1,32]{1,0:T(1,128)}, u32[]{:S(2)}) copy-start(s32[1,32]{1,0:T(1,128)} %param.7) | copy-start | bytes 388
  21.8 12.6 %collective-permute-start.1 = (bf16[64,2048]{1,0:T(8,128)(2,1)S(1)}, bf16[64,2048]{1,0:T(8,128)(2,1)S(1)}, u32[]{:S(2)}, u32[]{:S(2)}) collective-permute-start(bf16[64,2048]{1,0:T(8,128)(2,1)S(1)} %get-tuple-element.14), channel_id=1, source_target_pairs={{0,256},{128,384},{256,0},{384,128},{1,257},{129,385},{257,1},{385... | collective-permute-start | bytes 786440 | tf_op jit(solution)/shard_map/ppermute | solution.py:16
  26.7 12.2 %collective-permute-start.2 = (bf16[64,2048]{1,0:T(8,128)(2,1)S(1)}, bf16[64,2048]{1,0:T(8,128)(2,1)S(1)}, u32[]{:S(2)}, u32[]{:S(2)}) collective-permute-start(bf16[64,2048]{1,0:T(8,128)(2,1)S(1)} %get-tuple-element.15), channel_id=1, source_target_pairs={{0,128},{128,256},{256,384},{384,0},{1,129},{129,257},{257,385},{3... | collective-permute-start | bytes 786440 | tf_op jit(solution)/shard_map/ppermute | solution.py:16
  29.2 9.8 %collective-permute-start.3 = (bf16[64,2048]{1,0:T(8,128)(2,1)S(1)}, bf16[64,2048]{1,0:T(8,128)(2,1)S(1)}, u32[]{:S(2)}, u32[]{:S(2)}) collective-permute-start(bf16[64,2048]{1,0:T(8,128)(2,1)S(1)} %get-tuple-element.16), channel_id=1, source_target_pairs={{0,384},{128,0},{256,128},{384,256},{1,385},{129,1},{257,129},{385... | collective-permute-start | bytes 786440 | tf_op jit(solution)/shard_map/ppermute | solution.py:16
  49.6 24.5 %all-to-all-start = ((bf16[16,2,8,512]{3,2,1,0:T(8,128)(2,1)}), bf16[16,2,8,512]{3,2,1,0:T(8,128)(2,1)S(1)}, u32[]{:S(2)}, u32[]{:S(2)}) async-start(bf16[16,2,8,512]{3,2,1,0:T(8,128)(2,1)} %bitcast.7), calls=%async_computation | async-start | bytes 524288 | tf_op jit(solution)/shard_map/all_to_all | solution.py:200
  55.9 24.6 %collective-permute-start.8 = (bf16[16,2,8,512]{3,2,1,0:T(8,128)(2,1)S(1)}, bf16[16,2,8,512]{3,2,1,0:T(8,128)(2,1)S(1)}, u32[]{:S(2)}, u32[]{:S(2)}) collective-permute-start(bf16[16,2,8,512]{3,2,1,0:T(8,128)(2,1)S(1)} %slice_bitcast_fusion), channel_id=1, source_target_pairs={{0,2},{1,3},{2,0},{3,1},{4,6},{5,7},{6,4},{7,5},{8,10},{9,11},{10,... | collective-permute-start | bytes 786440 | tf_op jit(solution)/shard_map/ppermute | solution.py:16
  60.1 24.7 %collective-permute-start.9 = (bf16[16,2,8,512]{3,2,1,0:T(8,128)(2,1)S(1)}, bf16[16,2,8,512]{3,2,1,0:T(8,128)(2,1)S(1)}, u32[]{:S(2)}, u32[]{:S(2)}) collective-permute-start(bf16[16,2,8,512]{3,2,1,0:T(8,128)(2,1)S(1)} %slice_bitcast_fusion), channel_id=1, source_target_pairs={{0,3},{1,0},{2,1},{3,2},{4,7},{5,4},{6,5},{7,6},{8,11},{9,8},{10,9... | collective-permute-start | bytes 786440 | tf_op jit(solution)/shard_map/ppermute | solution.py:16
  63.3 21.5 %collective-permute-start.7 = (bf16[16,2,8,512]{3,2,1,0:T(8,128)(2,1)S(1)}, bf16[16,2,8,512]{3,2,1,0:T(8,128)(2,1)S(1)}, u32[]{:S(2)}, u32[]{:S(2)}) collective-permute-start(bf16[16,2,8,512]{3,2,1,0:T(8,128)(2,1)S(1)} %slice_bitcast_fusion), channel_id=1, source_target_pairs={{0,1},{1,2},{2,3},{3,0},{4,5},{5,6},{6,7},{7,4},{8,9},{9,10},{10,1... | collective-permute-start | bytes 786440 | tf_op jit(solution)/shard_map/ppermute | solution.py:16
  74.1 11.1 %collective-permute-start.4 = (bf16[16,2,8,512]{3,2,1,0:T(8,128)(2,1)S(1)}, bf16[16,2,8,512]{3,2,1,0:T(8,128)(2,1)S(1)}, u32[]{:S(2)}, u32[]{:S(2)}) collective-permute-start(bf16[16,2,8,512]{3,2,1,0:T(8,128)(2,1)S(1)} %all-to-all-done.refs_0_), channel_id=1, source_target_pairs={{0,1},{1,2},{2,3},{3,0},{4,5},{5,6},{6,7},{7,4},{8,9},{9,10},{10,1... | collective-permute-start | bytes 786440 | tf_op jit(solution)/shard_map/ppermute | solution.py:16
  77.6 12.7 %collective-permute-start.5 = (bf16[16,2,8,512]{3,2,1,0:T(8,128)(2,1)S(1)}, bf16[16,2,8,512]{3,2,1,0:T(8,128)(2,1)S(1)}, u32[]{:S(2)}, u32[]{:S(2)}) collective-permute-start(bf16[16,2,8,512]{3,2,1,0:T(8,128)(2,1)S(1)} %all-to-all-done.refs_0_), channel_id=1, source_target_pairs={{0,2},{1,3},{2,0},{3,1},{4,6},{5,7},{6,4},{7,5},{8,10},{9,11},{10,... | collective-permute-start | bytes 786440 | tf_op jit(solution)/shard_map/ppermute | solution.py:16
  80.5 13.2 %collective-permute-start.6 = (bf16[16,2,8,512]{3,2,1,0:T(8,128)(2,1)S(1)}, bf16[16,2,8,512]{3,2,1,0:T(8,128)(2,1)S(1)}, u32[]{:S(2)}, u32[]{:S(2)}) collective-permute-start(bf16[16,2,8,512]{3,2,1,0:T(8,128)(2,1)S(1)} %all-to-all-done.refs_0_), channel_id=1, source_target_pairs={{0,3},{1,0},{2,1},{3,2},{4,7},{5,4},{6,5},{7,6},{8,11},{9,8},{10,9... | collective-permute-start | bytes 786440 | tf_op jit(solution)/shard_map/ppermute | solution.py:16
  93.7 9.6 %copy-start.2 = (bf16[1,32,8,512]{3,2,1,0:T(8,128)(2,1)S(1)}, bf16[1,32,8,512]{3,2,1,0:T(8,128)(2,1)}, u32[]{:S(2)}) copy-start(bf16[1,32,8,512]{3,2,1,0:T(8,128)(2,1)} %param.9) | copy-start | bytes 786436
  93.7 9.6 %copy-start.3 = (bf16[1,32,8,512]{3,2,1,0:T(8,128)(2,1)S(1)}, bf16[1,32,8,512]{3,2,1,0:T(8,128)(2,1)}, u32[]{:S(2)}) copy-start(bf16[1,32,8,512]{3,2,1,0:T(8,128)(2,1)} %param.8) | copy-start | bytes 786436
  96.6 46.4 %all-to-all-start.2 = ((bf16[16,3,2,8,512]{4,3,2,1,0:T(8,128)(2,1)}), bf16[16,3,2,8,512]{4,3,2,1,0:T(8,128)(2,1)S(1)}, u32[]{:S(2)}, u32[]{:S(2)}) async-start(bf16[16,3,2,8,512]{4,3,2,1,0:T(8,128)(2,1)} %products.1), calls=%async_computation.2 | async-start | bytes 1572864 | tf_op jit(solution)/shard_map/all_to_all | solution.py:214
